TPU v7x, 32 devices: a whole 2x2x4 slice. The times are simulated.
32 devices in a mesh: groups: 2 (over y), seq: 4 (over z), ep: 2 (over x), tp: 2 (over core).
Axes of the slice: x: 2, y: 2, z: 4, core: 2. Of those that a mesh axis runs over, the one named last changes fastest.
Arguments:
- hidden: bfloat16 [2048, 1440], P(('groups', 'seq', 'ep')), parts along dimension 0, may hold values from -6 to 6
- expert_ids: int32 [2048, 4], P(('groups', 'seq', 'ep')), parts along dimension 0, may hold values from 0 to 7, all different within a row; in each aligned block of 128 rows (0 to 127, 128 to 255, ...) at most 88 rows name the same one
- gate_units: int32 [2048, 4], P(('groups', 'seq', 'ep')), parts along dimension 0, may hold values from 4096 to 32767
- w_gate: bfloat16 [8, 1440, 1440], P(('seq', 'tp'), None, 'ep'), may hold values from -0.15625 to 0.15625
- w_up: bfloat16 [8, 1440, 1440], P(('seq', 'tp'), None, 'ep'), may hold values from -0.15625 to 0.15625
- w_down: bfloat16 [8, 1440, 1440], P(('seq', 'tp'), None, 'ep'), may hold values from -0.15625 to 0.15625
Outputs:
- moe_out: bfloat16 [2048, 1440], P(('groups', 'seq', 'ep'), 'tp'), parts along dimension 0
There are 2 independent parts, one for each index of `groups`. A program takes and returns all parts, laid end to end along the dimension named above; an argument that names none is the same for every part. Nothing has to cross between parts.
Inputs may be any that keep to these rules, and one draw needn't show every extreme that they name: `expert_ids`: each row names 4 different experts; in each aligned block of 128 rows no expert is named by more than 88 rows, and in every draw some expert is named by exactly 88 rows of some block.
All inputs are finite; a program needn't handle non-finite values.
Results may differ from a plain program's by a relative error of at most 0.0064.
Values may be sent and summed in bfloat16 or wider, within the bound.
No kernel may reach another device: no remote copies, remote signals or barrier semaphores. Data moves between devices by JAX's collectives and lax.ppermute only.
A program may use at most 64 MiB of HBM per device.

v0:
```python
import jax
import jax.numpy as jnp
from jax import lax
from jax.sharding import PartitionSpec as P

TOP = 4


def slice_output(rows_in, gate_cols, up_cols, down_cols):
    gate_pre = jnp.dot(rows_in, gate_cols, preferred_element_type=jnp.float32)
    up_pre = jnp.dot(rows_in, up_cols, preferred_element_type=jnp.float32)
    activation = ((up_pre + 1.0) * gate_pre * jax.nn.sigmoid(1.702 * gate_pre)).astype(jnp.bfloat16)
    return lax.dot_general(
        activation, down_cols, (((1,), (1,)), ((), ())), preferred_element_type=jnp.float32
    ).astype(jnp.bfloat16)


def local(hidden, expert_ids, gate_units, w_gate, w_up, w_down):
    token_count, model_width = hidden.shape
    seq_count = lax.axis_size("seq")
    ep_count = lax.axis_size("ep")
    tp_count = lax.axis_size("tp")
    half_width = model_width // tp_count
    my_half = lax.axis_index("tp")
    expert_count = seq_count * tp_count
    capacity = max(2, (token_count * TOP * 11 + expert_count * 8 - 1) // (expert_count * 8))
    flat_ids = expert_ids.reshape(-1)
    onehot_ids = (flat_ids[:, None] == jnp.arange(expert_count, dtype=jnp.int32)[None, :]).astype(
        jnp.int32
    )
    slot_rank = jnp.sum((jnp.cumsum(onehot_ids, axis=0) - 1) * onehot_ids, axis=1)
    owner_seq = flat_ids // tp_count
    owner_half = flat_ids % tp_count
    send_row = jnp.where(owner_half == my_half, owner_seq * capacity + slot_rank, -1)
    selector = jnp.arange(seq_count * capacity, dtype=jnp.int32)[:, None] == send_row[None, :]
    selector = jnp.any(selector.reshape(seq_count * capacity, token_count, TOP), axis=2).astype(
        jnp.bfloat16
    )
    outgoing = jnp.dot(selector, hidden, preferred_element_type=jnp.float32).astype(jnp.bfloat16)
    outgoing = outgoing.reshape(seq_count, capacity, model_width)
    column_of = (owner_half * seq_count + owner_seq) * capacity + slot_rank
    gate_share = gate_units.reshape(-1).astype(jnp.float32) / 65536.0
    column_ids = jnp.arange(tp_count * seq_count * capacity, dtype=jnp.int32)
    combiner = jnp.where(column_ids[None, :] == column_of[:, None], gate_share[:, None], 0.0)
    combiner = jnp.sum(combiner.reshape(token_count, TOP, -1), axis=1)
    copied = jnp.broadcast_to(outgoing[:, None], (seq_count, ep_count, capacity, model_width))
    copied = copied.reshape(seq_count * ep_count, capacity, model_width)
    arrived = lax.all_to_all(copied, ("seq", "ep"), split_axis=0, concat_axis=0, tiled=True)
    slice_rows = slice_output(arrived.reshape(-1, model_width), w_gate[0], w_up[0], w_down[0])
    slice_rows = slice_rows.reshape(seq_count * ep_count, capacity, model_width)
    came_back = lax.all_to_all(
        lax.all_to_all(slice_rows, ("seq", "ep"), split_axis=0, concat_axis=0, tiled=True),
        "tp",
        split_axis=2,
        concat_axis=0,
        tiled=True,
    )
    came_back = came_back.reshape(tp_count, seq_count, ep_count, capacity, half_width)
    returned = jnp.sum(came_back.astype(jnp.float32), axis=2).astype(jnp.bfloat16)
    result_rows = returned.reshape(-1, half_width).astype(jnp.float32)
    moe_out = jnp.dot(
        combiner, result_rows, precision=lax.Precision.HIGHEST, preferred_element_type=jnp.float32
    )
    return moe_out.astype(jnp.bfloat16)


def solution(mesh):
    return jax.shard_map(
        local,
        mesh=mesh,
        in_specs=(
            P(("groups", "seq", "ep"), None),
            P(("groups", "seq", "ep"), None),
            P(("groups", "seq", "ep"), None),
            P(("seq", "tp"), None, "ep"),
            P(("seq", "tp"), None, "ep"),
            P(("seq", "tp"), None, "ep"),
        ),
        out_specs=P(("groups", "seq", "ep"), "tp"),
        check_vma=False,
    )
```

profile of v0, /device:TPU:0, one launch (start us, length us, event | category | flops | bytes accessed | tf_op | source)
XLA Modules:
  0.0 157.4 jit_solution(9115896044357004231)
XLA Ops:
  0.0 0.0 copy-start
  0.0 0.9 copy.72
  0.9 0.1 eq.70
  1.0 0.1 eq.66
  1.2 1.1 reduce-window.6
  2.3 0.2 slice_reduce_fusion
  2.6 0.1 fusion.10
  2.7 0.1 reduce_sum.33
  2.8 0.1 copy.74
  2.8 0.7 add_select_fusion.2
  3.6 0.1 fusion.9
  3.7 1.4 convolution_convert_fusion.1
  5.1 0.2 broadcast_in_dim.30
  5.3 0.0 copy-start.3
  5.3 57.5 %all_to_all.25 = bf16[8,88,1440]{2,1,0:T(8,128)(2,1)S(1)} all-to-all(bf16[8,88,1440]{2,1,0:T(8,128)(2,1)S(1)} %bitcast.36), channel_id=1, replica_groups=mesh['groups'=2,'seq'=4,'ep'=2,'tp'=2] {'seq','ep'}, dimensions={0} | all-to-all | bytes 4055040 | tf_op jit(solution)/shard_map/all_to_all | solution.py:48
  62.7 0.0 copy-start.1
  62.8 1.3 copy-done.1
  64.1 0.0 copy-done.3
  64.1 3.2 %fusion.1 = f32[704,720]{1,0:T(8,128)} fusion(bf16[704,1440]{1,0:T(8,128)(2,1)S(1)} %bitcast.40, bf16[1,1440,720]{2,1,0:T(8,128)(2,1)S(1)} %copy-done.3), kind=kOutput, calls=%fused_computation.3 | convolution fusion | flops 1459814400 | bytes 6128640 | tf_op jit(solution)/shard_map/dot_general | solution.py:10
  67.3 0.0 copy-done
  67.3 8.6 %convolution_convert_fusion = bf16[704,1440]{1,0:T(8,128)(2,1)} fusion(bf16[1,1440,720]{2,1,0:T(8,128)(2,1)S(1)} %copy-done, f32[704,720]{1,0:T(8,128)} %fusion.1, bf16[704,1440]{1,0:T(8,128)(2,1)} %bitcast.41, bf16[1,1440,720]{2,1,0:T(8,128)(2,1)} %param.10), kind=kOutput, calls=%fused_computation | convolution fusion | flops 2924697600 | bytes 10229760 | tf_op jit(solution)/shard_map/dot_general | solution.py:13
  75.8 0.0 copy-start.2
  75.8 4.5 %all-to-all-start.1 = ((bf16[8,88,1440]{2,1,0:T(8,128)(2,1)}), bf16[8,88,1440]{2,1,0:T(8,128)(2,1)}, u32[]{:S(2)}, u32[]{:S(2)}) async-start(bf16[8,88,1440]{2,1,0:T(8,128)(2,1)} %bitcast.39), calls=%async_computation.1 | async-start | bytes 4325376 | tf_op jit(solution)/shard_map/all_to_all | solution.py:52
  80.3 0.0 copy-done.2
  80.4 0.2 select_reduce_fusion
  80.5 48.6 %all-to-all-done.1 = bf16[8,88,1440]{2,1,0:T(8,128)(2,1)} async-done(((bf16[8,88,1440]{2,1,0:T(8,128)(2,1)}), bf16[8,88,1440]{2,1,0:T(8,128)(2,1)}, u32[]{:S(2)}, u32[]{:S(2)}) %all-to-all-start.1) | async-done | bytes 2027552 | tf_op jit(solution)/shard_map/all_to_all | solution.py:52
  129.1 4.7 %copy.76 = bf16[8,88,1440]{1,0,2:T(8,128)(2,1)} copy(bf16[8,88,1440]{2,1,0:T(8,128)(2,1)} %all-to-all-done.1) | data formatting | bytes 4055040 | tf_op jit(solution)/shard_map/all_to_all | solution.py:52
  133.8 10.1 %all_to_all.26 = bf16[8,88,1440]{1,0,2:T(8,128)(2,1)} all-to-all(bf16[8,88,1440]{1,0,2:T(8,128)(2,1)} %copy.76), channel_id=1, replica_groups=mesh['groups'=2,'seq'=4,'ep'=2,'tp'=2] {'tp'}, dimensions={2} | all-to-all | bytes 4055040 | tf_op jit(solution)/shard_map/all_to_all | solution.py:51
  143.9 6.2 %copy.77 = bf16[2,8,88,720]{3,0,2,1:T(2,128)(2,1)} copy(bf16[2,8,88,720]{2,1,3,0:T(8,128)(2,1)} %bitcast.35) | data formatting | bytes 4055040 | tf_op jit(solution)/shard_map/all_to_all | solution.py:51
  150.0 5.2 %bitcast_reduce_fusion = bf16[2,4,88,720]{3,0,2,1:T(2,128)(2,1)S(1)} fusion(bf16[2,8,88,720]{3,0,2,1:T(2,128)(2,1)} %copy.77), kind=kLoop, calls=%fused_computation.7 | loop fusion | flops 506880 | bytes 3041280 | tf_op jit(solution)/shard_map/reduce_sum | solution.py:59
  155.3 0.1 copy.78
  155.4 2.0 %convolution_convert_fusion.2 = bf16[128,720]{0,1:T(8,128)(2,1)} fusion(f32[128,704]{0,1:T(8,128)S(1)} %select_reduce_fusion, bf16[704,720]{1,0:T(8,128)(2,1)S(1)} %bitcast.37), kind=kOutput, calls=%fused_computation.11 | convolution fusion | flops 778659840 | bytes 1558528 | tf_op jit(solution)/shard_map/dot_general | solution.py:61
  (4 shorter events, 0.0 us)
Async XLA Ops:
  0.0 67.3 %copy-start = (bf16[1,1440,720]{2,1,0:T(8,128)(2,1)S(1)}, bf16[1,1440,720]{2,1,0:T(8,128)(2,1)}, u32[]{:S(2)}) copy-start(bf16[1,1440,720]{2,1,0:T(8,128)(2,1)} %param.11) | copy-start | bytes 6220804
  5.3 58.8 %copy-start.3 = (bf16[1,1440,720]{2,1,0:T(8,128)(2,1)S(1)}, bf16[1,1440,720]{2,1,0:T(8,128)(2,1)}, u32[]{:S(2)}) copy-start(bf16[1,1440,720]{2,1,0:T(8,128)(2,1)} %param.9) | copy-start | bytes 6220804
  62.7 1.3 copy-start.1
  75.8 4.5 %copy-start.2 = (s32[128,4]{0,1:T(4,128)S(1)}, s32[128,4]{0,1:T(4,128)}, u32[]{:S(2)}) copy-start(s32[128,4]{0,1:T(4,128)} %param.8) | copy-start | bytes 6148
  75.8 53.3 %all-to-all-start.1 = ((bf16[8,88,1440]{2,1,0:T(8,128)(2,1)}), bf16[8,88,1440]{2,1,0:T(8,128)(2,1)}, u32[]{:S(2)}, u32[]{:S(2)}) async-start(bf16[8,88,1440]{2,1,0:T(8,128)(2,1)} %bitcast.39), calls=%async_computation.1 | async-start | bytes 4325376 | tf_op jit(solution)/shard_map/all_to_all | solution.py:52
where the time goes:
time: 158 us; the launch traced here: 157 us
  blocking collectives  67.5 us (43%)
  waiting for transfers between devices  48.6 us (31%)
  matrix products  15.2 us (10%)
  local copies, waits for them, and re-layouts  14.1 us (9%)
  other arithmetic  7.45 us (5%)
  starting transfers between devices  4.5 us (3%)
    all_to_all x1, blocking collectives, local(): lax.all_to_all(copied, ('seq', 'ep'), split_axis=0, concat_axis=0, tiled=...  57.5 us
    all_to_all x1, waiting for transfers between devices, local(): lax.all_to_all(slice_rows, ('seq', 'ep'), split_axis=0, concat_axis=0, ti...  48.6 us
    all_to_all x1, blocking collectives, local(): lax.all_to_all(lax.all_to_all(slice_rows, ('seq', 'ep'), split_axis=0, co...  10.1 us
    dot_general x1, matrix products, slice_output(): lax.dot_general(activation, down_cols, (((1,), (1,)), ((), ())), preferre...  8.55 us
    all_to_all x1, local copies, waits for them, and re-layouts, local(): lax.all_to_all(lax.all_to_all(slice_rows, ('seq', 'ep'), split_axis=0, co...  6.16 us
    reduce_sum x1, other arithmetic, local(): jnp.sum(came_back.astype(jnp.float32), axis=2).astype(jnp.bfloat16)  5.2 us
    all_to_all x1, local copies, waits for them, and re-layouts, local(): lax.all_to_all(slice_rows, ('seq', 'ep'), split_axis=0, concat_axis=0, ti...  4.73 us
    all_to_all x1, starting transfers between devices, local(): lax.all_to_all(slice_rows, ('seq', 'ep'), split_axis=0, concat_axis=0, ti...  4.5 us
  transfers between devices with their start and end apart: 1, of which 1 were waited for; matrix products, arithmetic and copies ran while one was open for 0% of the time, Pallas kernels for 0%

commit v1 on v0

--- a/solution.py
+++ b/solution.py
@@ -1,6 +1,10 @@
+import functools
+
 import jax
 import jax.numpy as jnp
 from jax import lax
+from jax.experimental import pallas as pl
+from jax.experimental.pallas import tpu as pltpu
 from jax.sharding import PartitionSpec as P
 
 TOP = 4
@@ -15,7 +19,11 @@
     ).astype(jnp.bfloat16)
 
 
-def local(hidden, expert_ids, gate_units, w_gate, w_up, w_down):
+def capacity_of(token_count, expert_count):
+    return max(2, (token_count * TOP * 11 + expert_count * 8 - 1) // (expert_count * 8))
+
+
+def routed(hidden, expert_ids, gate_units, w_gate, w_up, w_down):
     token_count, model_width = hidden.shape
     seq_count = lax.axis_size("seq")
     ep_count = lax.axis_size("ep")
@@ -23,7 +31,7 @@
     half_width = model_width // tp_count
     my_half = lax.axis_index("tp")
     expert_count = seq_count * tp_count
-    capacity = max(2, (token_count * TOP * 11 + expert_count * 8 - 1) // (expert_count * 8))
+    capacity = capacity_of(token_count, expert_count)
     flat_ids = expert_ids.reshape(-1)
     onehot_ids = (flat_ids[:, None] == jnp.arange(expert_count, dtype=jnp.int32)[None, :]).astype(
         jnp.int32
@@ -64,7 +72,130 @@
     return moe_out.astype(jnp.bfloat16)
 
 
+def expert_kernel(
+    expert_count, place_ref, a0, a1, b0, b1, wg, wu, wd, keep_a, keep_b, send, vg, vu, vd, rows, sems
+):
+    model_width, _ = wg.shape
+    half_rows = a0.shape[0]
+    half_width = model_width // 2
+    tp, expert = place_ref[0], place_ref[1]
+    copies = [
+        pltpu.make_async_copy(src, dst, sems.at[i])
+        for i, (src, dst) in enumerate(((wg, vg), (wu, vu), (wd, vd)))
+    ]
+    for copy in copies:
+        copy.start()
+    mine = pl.multiple_of(tp * half_rows, half_rows)
+    other = pl.multiple_of((1 - tp) * half_rows, half_rows)
+    rows[pl.ds(mine, half_rows), :] = a0[...]
+    rows[pl.ds(other, half_rows), :] = a1[...]
+    rows[pl.ds(2 * half_rows + mine, half_rows), :] = b0[...]
+    rows[pl.ds(2 * half_rows + other, half_rows), :] = b1[...]
+    tail = rows[:, model_width:].astype(jnp.float32)
+    lane = lax.broadcasted_iota(jnp.int32, tail.shape, 1)
+    scale = jnp.where(lane == expert, 256.0, jnp.where(lane == expert + expert_count, 1.0, 0.0))
+    weight = jnp.sum(tail * scale, axis=1, keepdims=True) * (1.0 / 65536.0)
+    x = rows[:, :model_width]
+    copies[0].wait()
+    gate_pre = jnp.dot(x, vg[...], preferred_element_type=jnp.float32)
+    copies[1].wait()
+    up_pre = jnp.dot(x, vu[...], preferred_element_type=jnp.float32)
+    act = ((up_pre + 1.0) * gate_pre * jax.nn.sigmoid(1.702 * gate_pre)).astype(jnp.bfloat16)
+    copies[2].wait()
+    contract = (((1,), (1,)), ((), ()))
+    theirs = vd[pl.ds(pl.multiple_of((1 - tp) * half_width, 16), half_width), :]
+    out = lax.dot_general(act, theirs, contract, preferred_element_type=jnp.float32) * weight
+    send[...] = out.astype(jnp.bfloat16)
+    ours = vd[pl.ds(pl.multiple_of(tp * half_width, 16), half_width), :]
+    out = lax.dot_general(act, ours, contract, preferred_element_type=jnp.float32) * weight
+    keep_a[...] = out[: 2 * half_rows]
+    keep_b[...] = out[2 * half_rows :]
+
+
+def experts(expert_count, place, a0, a1, b0, b1, wg, wu, wd):
+    half_rows, width = a0.shape
+    model_width, slice_width = wg.shape
+    half_width = model_width // 2
+    block = 2 * half_rows
+    vmem = pl.BlockSpec(memory_space=pltpu.VMEM)
+    hbm = pl.BlockSpec(memory_space=pl.ANY)
+    return pl.pallas_call(
+        functools.partial(expert_kernel, expert_count),
+        out_shape=(
+            jax.ShapeDtypeStruct((block, half_width), jnp.float32),
+            jax.ShapeDtypeStruct((block, half_width), jnp.float32),
+            jax.ShapeDtypeStruct((2 * block, half_width), jnp.bfloat16),
+        ),
+        in_specs=[pl.BlockSpec(memory_space=pltpu.SMEM)] + [vmem] * 4 + [hbm] * 3,
+        out_specs=(vmem, vmem, vmem),
+        scratch_shapes=[
+            pltpu.VMEM((model_width, slice_width), jnp.bfloat16),
+            pltpu.VMEM((model_width, slice_width), jnp.bfloat16),
+            pltpu.VMEM((model_width, slice_width), jnp.bfloat16),
+            pltpu.VMEM((2 * block, width), jnp.bfloat16),
+            pltpu.SemaphoreType.DMA((3,)),
+        ],
+        compiler_params=pltpu.CompilerParams(vmem_limit_bytes=32 * 1024 * 1024),
+        cost_estimate=pl.CostEstimate(
+            flops=2 * 2 * block * model_width * slice_width * 3,
+            bytes_accessed=3 * model_width * slice_width * 2 + 4 * block * width * 2,
+            transcendentals=2 * block * slice_width,
+        ),
+    )(place, a0, a1, b0, b1, wg, wu, wd)
+
+
+def gathered(hidden, expert_ids, gate_units, w_gate, w_up, w_down):
+    token_count, model_width = hidden.shape
+    half_rows = token_count // 2
+    tp = lax.axis_index("tp")
+    expert_count = lax.axis_size("seq") * lax.axis_size("tp")
+    expert = lax.axis_index("seq") * lax.axis_size("tp") + tp
+    place = jnp.stack([tp, expert]).astype(jnp.int32)
+    named = expert_ids[:, :, None] == jnp.arange(expert_count, dtype=jnp.int32)[None, None, :]
+    units = jnp.sum(jnp.where(named, gate_units[:, :, None], 0), axis=1)
+    payload = jnp.concatenate(
+        [hidden, (units // 256).astype(jnp.bfloat16), (units % 256).astype(jnp.bfloat16)], axis=1
+    )
+    own = lax.dynamic_slice_in_dim(payload, tp * half_rows, half_rows, 0)
+    own_rest = lax.dynamic_slice_in_dim(payload, (1 - tp) * half_rows, half_rows, 0)
+
+    def z(x, k):
+        return lax.ppermute(x, "seq", [(i, i ^ k) for i in range(lax.axis_size("seq"))])
+
+    def swap(x, axis):
+        return lax.ppermute(x, axis, [(0, 1), (1, 0)])
+
+    near = {0: own}
+    near[3] = z(own, 3)
+    near[1] = z(own, 1)
+    near[2] = z(near[3], 1)
+    far = {k: swap(near[k], "ep") for k in (0, 1, 3, 2)}
+    rest = {k: swap(near[k], "tp") for k in (1, 3, 2)}
+    rest[0] = own_rest
+    far_rest = {k: swap(far[k], "tp") for k in (0, 1, 3, 2)}
+    total = None
+    for k in (0, 1, 3, 2):
+        keep_a, keep_b, send = experts(
+            expert_count, place, near[k], rest[k], far[k], far_rest[k], w_gate[0], w_up[0], w_down[0]
+        )
+        came = swap(send, "tp").astype(jnp.float32)
+        cross = swap((keep_b + came[token_count:]).astype(jnp.bfloat16), "ep")
+        here = keep_a + came[:token_count] + cross.astype(jnp.float32)
+        if k:
+            here = z(here.astype(jnp.bfloat16), k).astype(jnp.float32)
+        total = here if total is None else total + here
+    return total.astype(jnp.bfloat16)
+
+
 def solution(mesh):
+    def local(*args):
+        token_count = args[0].shape[0]
+        seq, ep, tp = (mesh.shape[name] for name in ("seq", "ep", "tp"))
+        dense = capacity_of(token_count, seq * tp) * tp >= token_count
+        if dense and (seq, ep, tp) == (4, 2, 2):
+            return gathered(*args)
+        return routed(*args)
+
     return jax.shard_map(
         local,
         mesh=mesh,

time: 158 us -> 80.1 us (0.51)
  blocking collectives: 67.5 us -> 0 us
  starting transfers between devices: 4.5 us -> 29.4 us
  waiting for transfers between devices: 48.6 us -> 24.9 us
  Pallas kernels: 0 us -> 18.3 us
  matrix products: 15.2 us -> 0 us
  local copies, waits for them, and re-layouts: 14.1 us -> 5.46 us
  other arithmetic: 7.45 us -> 1.66 us
    all_to_all x2 -> x0, blocking collectives: 67.5 us -> none  [the longest x1 57.5 us: local(): lax.all_to_all(copied, ('seq', 'ep'), split_axis=0, concat_axis=0, tiled=...]
    all_to_all x1 -> x0, waiting for transfers between devices: 48.6 us -> none  [local(): lax.all_to_all(slice_rows, ('seq', 'ep'), split_axis=0, concat_axis=0, ti...]
    ppermute x0 -> x25, starting transfers between devices: none -> 29.4 us  [the longest x6 16 us: z(): lax.ppermute(x, 'seq', [(i, i ^ k) for i in range(lax.axis_size('seq'))])]
    ppermute x0 -> x25, waiting for transfers between devices: none -> 24.9 us  [the longest x6 16.4 us: z(): lax.ppermute(x, 'seq', [(i, i ^ k) for i in range(lax.axis_size('seq'))])]
    pallas_call x0 -> x4, Pallas kernels: none -> 18.3 us  [experts(): pl.pallas_call(functools.partial(expert_kernel, expert_count), out_shape=...]
    dot_general x4 -> x0, matrix products: 15.2 us -> none  [the longest x1 8.55 us: slice_output(): lax.dot_general(activation, down_cols, (((1,), (1,)), ((), ())), preferre...]
    all_to_all x2 -> x0, local copies, waits for them, and re-layouts: 10.9 us -> none  [the longest x1 6.16 us: local(): lax.all_to_all(lax.all_to_all(slice_rows, ('seq', 'ep'), split_axis=0, co...]
    reduce_sum x3 -> x1, other arithmetic: 5.46 us -> 0.86 us  [gathered(): units = jnp.sum(jnp.where(named, gate_units[:, :, None], 0), axis=1)]
  transfers between devices with their start and end apart: 1 -> 25, of which waited for: 1 -> 7; matrix products, arithmetic and copies ran while one was open for 0% -> 1% of each run, Pallas kernels for 0% -> 23%
where the time goes in v1:
time: 80.1 us; the launch traced here: 79.9 us
  starting transfers between devices  29.4 us (37%)
  waiting for transfers between devices  24.9 us (31%)
  Pallas kernels  18.3 us (23%)
  local copies, waits for them, and re-layouts  5.46 us (7%)
  other arithmetic  1.66 us (2%)
    pallas_call x4, Pallas kernels, experts(): pl.pallas_call(functools.partial(expert_kernel, expert_count), out_shape=...  18.3 us
    ppermute x6, waiting for transfers between devices, z(): lax.ppermute(x, 'seq', [(i, i ^ k) for i in range(lax.axis_size('seq'))])  16.4 us
    ppermute x6, starting transfers between devices, z(): lax.ppermute(x, 'seq', [(i, i ^ k) for i in range(lax.axis_size('seq'))])  16 us
    ppermute x19, starting transfers between devices, swap(): return lax.ppermute(x, axis, [(0, 1), (1, 0)])  13.4 us
    ppermute x19, waiting for transfers between devices, swap(): return lax.ppermute(x, axis, [(0, 1), (1, 0)])  8.53 us
    unnamed x7, local copies, waits for them, and re-layouts  4.4 us
  transfers between devices with their start and end apart: 25, of which 7 were waited for; matrix products, arithmetic and copies ran while one was open for 1% of the time, Pallas kernels for 23%

profile of v1, /device:TPU:0, one launch (start us, length us, event | category | flops | bytes accessed | tf_op | source)
XLA Modules:
  0.0 79.9 jit_solution(15048466933243390703)
XLA Ops:
  0.0 0.9 %select_reduce_fusion = s32[128,8]{0,1:T(8,128)S(1)} fusion(s32[128,4]{0,1:T(4,128)} %param.8, s32[128,4]{0,1:T(4,128)} %param.7), kind=kLoop, calls=%fused_computation.33 | loop fusion | flops 11264 | bytes 8192 | tf_op jit(solution)/shard_map/reduce_sum | solution.py:155
  0.9 0.1 copy.11
  1.0 0.1 fusion.16
  1.0 1.2 %copy.15 = bf16[128,1440]{1,0:T(8,128)(2,1)S(1)} copy(bf16[128,1440]{0,1:T(8,128)(2,1)} %param.6) | data formatting | bytes 737280 | tf_op args[0]
  2.2 0.1 concatenate.3
  2.4 3.1 %collective-permute-start.4 = (bf16[64,1456]{1,0:T(8,128)(2,1)S(1)}, bf16[64,1456]{1,0:T(8,128)(2,1)S(1)}, u32[]{:S(2)}, u32[]{:S(2)}) collective-permute-start(bf16[64,1456]{1,0:T(8,128)(2,1)S(1)} %get-tuple-element.30.a0), channel_id=1, source_target_pairs={{0,4},{4,0},{8,12},{12,8},{1,5},{5,1},{9,13},{13,9},{2,6},{6,2},{1... | collective-permute-start | bytes 559112 | tf_op jit(solution)/shard_map/ppermute | solution.py:163
  5.4 1.5 %collective-permute-start = (bf16[64,1456]{1,0:T(8,128)(2,1)S(1)}, bf16[64,1456]{1,0:T(8,128)(2,1)S(1)}, u32[]{:S(2)}, u32[]{:S(2)}) collective-permute-start(bf16[64,1456]{1,0:T(8,128)(2,1)S(1)} %get-tuple-element.30.a0), channel_id=1, source_target_pairs={{0,2},{2,0},{1,3},{3,1},{4,6},{6,4},{5,7},{7,5},{8,10},{10,8},{9,1... | collective-permute-start | bytes 559112 | tf_op jit(solution)/shard_map/ppermute | solution.py:166
  6.9 2.5 %collective-permute-start.11 = (bf16[64,1456]{1,0:T(8,128)(2,1)S(1)}, bf16[64,1456]{1,0:T(8,128)(2,1)S(1)}, u32[]{:S(2)}, u32[]{:S(2)}) collective-permute-start(bf16[64,1456]{1,0:T(8,128)(2,1)S(1)} %get-tuple-element.30.a0), channel_id=1, source_target_pairs={{0,12},{4,8},{8,4},{12,0},{1,13},{5,9},{9,5},{13,1},{2,14},{6,10},... | collective-permute-start | bytes 559112 | tf_op jit(solution)/shard_map/ppermute | solution.py:163
  9.4 0.9 %collective-permute-done.4.a0 = bf16[64,1456]{1,0:T(8,128)(2,1)S(1)} collective-permute-done((bf16[64,1456]{1,0:T(8,128)(2,1)S(1)}, bf16[64,1456]{1,0:T(8,128)(2,1)S(1)}, u32[]{:S(2)}, u32[]{:S(2)}) %collective-permute-start.4) | collective-permute-done | bytes 186400 | tf_op jit(solution)/shard_map/ppermute | solution.py:163
  10.3 1.9 %collective-permute-start.6 = (bf16[64,1456]{1,0:T(8,128)(2,1)S(1)}, bf16[64,1456]{1,0:T(8,128)(2,1)S(1)}, u32[]{:S(2)}, u32[]{:S(2)}) collective-permute-start(bf16[64,1456]{1,0:T(8,128)(2,1)S(1)} %collective-permute-done.4.a0), channel_id=1, source_target_pairs={{0,2},{2,0},{1,3},{3,1},{4,6},{6,4},{5,7},{7,5},{8,10},{10,8},{9,1... | collective-permute-start | bytes 559112 | tf_op jit(solution)/shard_map/ppermute | solution.py:166
  12.3 0.5 collective-permute-start.5
  12.8 4.1 %collective-permute-done.11.a0 = bf16[64,1456]{1,0:T(8,128)(2,1)S(1)} collective-permute-done((bf16[64,1456]{1,0:T(8,128)(2,1)S(1)}, bf16[64,1456]{1,0:T(8,128)(2,1)S(1)}, u32[]{:S(2)}, u32[]{:S(2)}) %collective-permute-start.11) | collective-permute-done | bytes 186400 | tf_op jit(solution)/shard_map/ppermute | solution.py:163
  16.9 1.5 %collective-permute-start.13 = (bf16[64,1456]{1,0:T(8,128)(2,1)S(1)}, bf16[64,1456]{1,0:T(8,128)(2,1)S(1)}, u32[]{:S(2)}, u32[]{:S(2)}) collective-permute-start(bf16[64,1456]{1,0:T(8,128)(2,1)S(1)} %collective-permute-done.11.a0), channel_id=1, source_target_pairs={{0,2},{2,0},{1,3},{3,1},{4,6},{6,4},{5,7},{7,5},{8,10},{10,8},{9,1... | collective-permute-start | bytes 559112 | tf_op jit(solution)/shard_map/ppermute | solution.py:166
  18.4 0.1 pad_add_fusion.place_ref
  18.4 0.8 %collective-permute-start.18 = (bf16[64,1456]{1,0:T(8,128)(2,1)S(1)}, bf16[64,1456]{1,0:T(8,128)(2,1)S(1)}, u32[]{:S(2)}, u32[]{:S(2)}) collective-permute-start(bf16[64,1456]{1,0:T(8,128)(2,1)S(1)} %collective-permute-done.11.a0), channel_id=1, source_target_pairs={{0,4},{4,0},{8,12},{12,8},{1,5},{5,1},{9,13},{13,9},{2,6},{6,2},{1... | collective-permute-start | bytes 559112 | tf_op jit(solution)/shard_map/ppermute | solution.py:163
  19.3 1.6 %copy-done.1 = bf16[1,1440,720]{2,1,0:T(8,128)(2,1)S(1)} copy-done((bf16[1,1440,720]{2,1,0:T(8,128)(2,1)S(1)}, bf16[1,1440,720]{2,1,0:T(8,128)(2,1)}, u32[]{:S(2)}) %copy-start.1) | copy-done | bytes 2073624
  20.9 1.6 %copy-done.2 = bf16[1,1440,720]{2,1,0:T(8,128)(2,1)S(1)} copy-done((bf16[1,1440,720]{2,1,0:T(8,128)(2,1)S(1)}, bf16[1,1440,720]{2,1,0:T(8,128)(2,1)}, u32[]{:S(2)}) %copy-start.2) | copy-done | bytes 2073624
  22.5 4.9 %shard_map.64 = (f32[128,720]{1,0:T(8,128)S(1)}, f32[128,720]{1,0:T(8,128)S(1)}, bf16[256,720]{1,0:T(8,128)(2,1)S(1)}) custom-call(s32[2]{0:T(128)S(1)} %pad_add_fusion.place_ref, bf16[64,1456]{1,0:T(8,128)(2,1)S(1)} %get-tuple-element.30.a0, bf16[64,1456]{1,0:T(8,128)(2,1)S(1)} %get-tuple-element.29.a1, bf16[64,1456]{1,0:T(8,128)(2,1)S(1)} %collective-permute-done.b0, ...), custom_call_target="tpu_custom_call" | custom-call | flops 1592524800 | bytes 7711744 | tf_op jit(solution)/shard_map/pallas_call | solution.py:122
  27.4 0.6 collective-permute-start.2
  28.0 0.1 collective-permute-start.12
  28.1 0.4 collective-permute-start.14
  28.5 1.5 %collective-permute-start.20 = (bf16[64,1456]{1,0:T(8,128)(2,1)S(1)}, bf16[64,1456]{1,0:T(8,128)(2,1)S(1)}, u32[]{:S(2)}, u32[]{:S(2)}) collective-permute-start(bf16[64,1456]{1,0:T(8,128)(2,1)S(1)} %collective-permute-done.18.a0), channel_id=1, source_target_pairs={{0,2},{2,0},{1,3},{3,1},{4,6},{6,4},{5,7},{7,5},{8,10},{10,8},{9,1... | collective-permute-start | bytes 559112 | tf_op jit(solution)/shard_map/ppermute | solution.py:166
  30.0 4.5 %shard_map.65 = (f32[128,720]{1,0:T(8,128)S(1)}, f32[128,720]{1,0:T(8,128)S(1)}, bf16[256,720]{1,0:T(8,128)(2,1)S(1)}) custom-call(s32[2]{0:T(128)S(1)} %pad_add_fusion.place_ref, bf16[64,1456]{1,0:T(8,128)(2,1)S(1)} %collective-permute-done.4.a0, bf16[64,1456]{1,0:T(8,128)(2,1)S(1)} %collective-permute-done.5.a1, ...), custom_call_target="tpu_custom_call" | custom-call | flops 1592524800 | bytes 7711744 | tf_op jit(solution)/shard_map/pallas_call | solution.py:122
  34.5 0.6 collective-permute-start.8
  35.1 4.5 %shard_map.66 = (f32[128,720]{1,0:T(8,128)S(1)}, f32[128,720]{1,0:T(8,128)S(1)}, bf16[256,720]{1,0:T(8,128)(2,1)S(1)}) custom-call(s32[2]{0:T(128)S(1)} %pad_add_fusion.place_ref, bf16[64,1456]{1,0:T(8,128)(2,1)S(1)} %collective-permute-done.11.a0, bf16[64,1456]{1,0:T(8,128)(2,1)S(1)} %collective-permute-done.12.a1, ...), custom_call_target="tpu_custom_call" | custom-call | flops 1592524800 | bytes 7711744 | tf_op jit(solution)/shard_map/pallas_call | solution.py:122
  39.5 0.1 collective-permute-start.15
  39.6 0.5 collective-permute-start.21
  40.1 0.1 convert_element_type.65
  40.2 0.6 collective-permute-start.3
  40.8 0.8 collective-permute-done.21.b1
  41.6 4.5 %shard_map.67 = (f32[128,720]{1,0:T(8,128)S(1)}, f32[128,720]{1,0:T(8,128)S(1)}, bf16[256,720]{1,0:T(8,128)(2,1)S(1)}) custom-call(s32[2]{0:T(128)S(1)} %pad_add_fusion.place_ref, bf16[64,1456]{1,0:T(8,128)(2,1)S(1)} %collective-permute-done.18.a0, bf16[64,1456]{1,0:T(8,128)(2,1)S(1)} %collective-permute-done.19.a1, ...), custom_call_target="tpu_custom_call" | custom-call | flops 1592524800 | bytes 7711744 | tf_op jit(solution)/shard_map/pallas_call | solution.py:122
  46.1 0.2 collective-permute-start.22
  46.3 0.1 convert_element_type.68
  46.4 0.7 collective-permute-start.9
  47.1 0.1 convert_element_type.73
  47.2 1.5 %collective-permute-start.16 = (bf16[128,720]{1,0:T(8,128)(2,1)S(1)}, bf16[128,720]{1,0:T(8,128)(2,1)S(1)}, u32[]{:S(2)}, u32[]{:S(2)}) collective-permute-start(bf16[128,720]{1,0:T(8,128)(2,1)S(1)} %fusion.3), channel_id=1, source_target_pairs={{0,2},{2,0},{1,3},{3,1},{4,6},{6,4},{5,7},{7,5},{8,10},{10,8},{9,1... | collective-permute-start | bytes 552968 | tf_op jit(solution)/shard_map/ppermute | solution.py:166
  48.7 5.5 %collective-permute-done.9 = bf16[128,720]{1,0:T(8,128)(2,1)S(1)} collective-permute-done((bf16[128,720]{1,0:T(8,128)(2,1)S(1)}, bf16[128,720]{1,0:T(8,128)(2,1)S(1)}, u32[]{:S(2)}, u32[]{:S(2)}) %collective-permute-start.9) | collective-permute-done | bytes 184352 | tf_op jit(solution)/shard_map/ppermute | solution.py:166
  54.2 0.1 fusion.8
  54.3 0.5 collective-permute-start.10
  54.8 0.1 convert_element_type.78
  54.9 1.3 %collective-permute-start.23 = (bf16[128,720]{1,0:T(8,128)(2,1)S(1)}, bf16[128,720]{1,0:T(8,128)(2,1)S(1)}, u32[]{:S(2)}, u32[]{:S(2)}) collective-permute-start(bf16[128,720]{1,0:T(8,128)(2,1)S(1)} %fusion), channel_id=1, source_target_pairs={{0,2},{2,0},{1,3},{3,1},{4,6},{6,4},{5,7},{7,5},{8,10},{10,8},{9,1... | collective-permute-start | bytes 552968 | tf_op jit(solution)/shard_map/ppermute | solution.py:166
  56.2 2.2 %collective-permute-done.16 = bf16[128,720]{1,0:T(8,128)(2,1)S(1)} collective-permute-done((bf16[128,720]{1,0:T(8,128)(2,1)S(1)}, bf16[128,720]{1,0:T(8,128)(2,1)S(1)}, u32[]{:S(2)}, u32[]{:S(2)}) %collective-permute-start.16) | collective-permute-done | bytes 184352 | tf_op jit(solution)/shard_map/ppermute | solution.py:166
  58.5 6.8 %collective-permute-start.17 = (bf16[128,720]{1,0:T(8,128)(2,1)S(1)}, bf16[128,720]{1,0:T(8,128)(2,1)S(1)}, u32[]{:S(2)}, u32[]{:S(2)}) collective-permute-start(bf16[128,720]{1,0:T(8,128)(2,1)S(1)} %fusion.5), channel_id=1, source_target_pairs={{0,12},{4,8},{8,4},{12,0},{1,13},{5,9},{9,5},{13,1},{2,14},{6,10},... | collective-permute-start | bytes 552968 | tf_op jit(solution)/shard_map/ppermute | solution.py:163
  65.3 2.3 %collective-permute-start.24 = (bf16[128,720]{1,0:T(8,128)(2,1)S(1)}, bf16[128,720]{1,0:T(8,128)(2,1)S(1)}, u32[]{:S(2)}, u32[]{:S(2)}) collective-permute-start(bf16[128,720]{1,0:T(8,128)(2,1)S(1)} %fusion.2), channel_id=1, source_target_pairs={{0,8},{4,12},{8,0},{12,4},{1,9},{5,13},{9,1},{13,5},{2,10},{6,14},... | collective-permute-start | bytes 552968 | tf_op jit(solution)/shard_map/ppermute | solution.py:163
  67.6 3.0 %collective-permute-done.17 = bf16[128,720]{1,0:T(8,128)(2,1)S(1)} collective-permute-done((bf16[128,720]{1,0:T(8,128)(2,1)S(1)}, bf16[128,720]{1,0:T(8,128)(2,1)S(1)}, u32[]{:S(2)}, u32[]{:S(2)}) %collective-permute-start.17) | collective-permute-done | bytes 184352 | tf_op jit(solution)/shard_map/ppermute | solution.py:163
  70.6 8.3 %collective-permute-done.24 = bf16[128,720]{1,0:T(8,128)(2,1)S(1)} collective-permute-done((bf16[128,720]{1,0:T(8,128)(2,1)S(1)}, bf16[128,720]{1,0:T(8,128)(2,1)S(1)}, u32[]{:S(2)}, u32[]{:S(2)}) %collective-permute-start.24) | collective-permute-done | bytes 184352 | tf_op jit(solution)/shard_map/ppermute | solution.py:163
  79.0 0.1 fusion.14
  79.1 0.8 %copy.16 = bf16[128,720]{0,1:T(8,128)(2,1)} copy(bf16[128,720]{1,0:T(8,128)(2,1)S(1)} %fusion.14) | data formatting | bytes 368640 | tf_op jit(solution)/shard_map/convert_element_type | solution.py:187
  (32 shorter events, 0.4 us)
Async XLA Ops:
  0.0 19.3 %copy-start = (bf16[1,1440,720]{2,1,0:T(8,128)(2,1)S(1)}, bf16[1,1440,720]{2,1,0:T(8,128)(2,1)}, u32[]{:S(2)}) copy-start(bf16[1,1440,720]{2,1,0:T(8,128)(2,1)} %param.9) | copy-start | bytes 6220804
  2.4 8.0 %collective-permute-start.4 = (bf16[64,1456]{1,0:T(8,128)(2,1)S(1)}, bf16[64,1456]{1,0:T(8,128)(2,1)S(1)}, u32[]{:S(2)}, u32[]{:S(2)}) collective-permute-start(bf16[64,1456]{1,0:T(8,128)(2,1)S(1)} %get-tuple-element.30.a0), channel_id=1, source_target_pairs={{0,4},{4,0},{8,12},{12,8},{1,5},{5,1},{9,13},{13,9},{2,6},{6,2},{1... | collective-permute-start | bytes 559112 | tf_op jit(solution)/shard_map/ppermute | solution.py:163
  5.4 6.8 %collective-permute-start = (bf16[64,1456]{1,0:T(8,128)(2,1)S(1)}, bf16[64,1456]{1,0:T(8,128)(2,1)S(1)}, u32[]{:S(2)}, u32[]{:S(2)}) collective-permute-start(bf16[64,1456]{1,0:T(8,128)(2,1)S(1)} %get-tuple-element.30.a0), channel_id=1, source_target_pairs={{0,2},{2,0},{1,3},{3,1},{4,6},{6,4},{5,7},{7,5},{8,10},{10,8},{9,1... | collective-permute-start | bytes 559112 | tf_op jit(solution)/shard_map/ppermute | solution.py:166
  6.9 9.9 %collective-permute-start.11 = (bf16[64,1456]{1,0:T(8,128)(2,1)S(1)}, bf16[64,1456]{1,0:T(8,128)(2,1)S(1)}, u32[]{:S(2)}, u32[]{:S(2)}) collective-permute-start(bf16[64,1456]{1,0:T(8,128)(2,1)S(1)} %get-tuple-element.30.a0), channel_id=1, source_target_pairs={{0,12},{4,8},{8,4},{12,0},{1,13},{5,9},{9,5},{13,1},{2,14},{6,10},... | collective-permute-start | bytes 559112 | tf_op jit(solution)/shard_map/ppermute | solution.py:163
  10.3 8.9 %collective-permute-start.6 = (bf16[64,1456]{1,0:T(8,128)(2,1)S(1)}, bf16[64,1456]{1,0:T(8,128)(2,1)S(1)}, u32[]{:S(2)}, u32[]{:S(2)}) collective-permute-start(bf16[64,1456]{1,0:T(8,128)(2,1)S(1)} %collective-permute-done.4.a0), channel_id=1, source_target_pairs={{0,2},{2,0},{1,3},{3,1},{4,6},{6,4},{5,7},{7,5},{8,10},{10,8},{9,1... | collective-permute-start | bytes 559112 | tf_op jit(solution)/shard_map/ppermute | solution.py:166
  12.2 7.0 %collective-permute-start.1 = (bf16[64,1456]{1,0:T(8,128)(2,1)S(1)}, bf16[64,1456]{1,0:T(8,128)(2,1)}, u32[]{:S(2)}, u32[]{:S(2)}) collective-permute-start(bf16[64,1456]{1,0:T(8,128)(2,1)S(1)} %collective-permute-done.b0), channel_id=1, source_target_pairs={{0,1},{1,0},{2,3},{3,2},{4,5},{5,4},{6,7},{7,6},{8,9},{9,8},{10,11... | collective-permute-start | bytes 559112 | tf_op jit(solution)/shard_map/ppermute | solution.py:166
  12.3 15.7 %collective-permute-start.5 = (bf16[64,1456]{1,0:T(8,128)(2,1)S(1)}, bf16[64,1456]{1,0:T(8,128)(2,1)S(1)}, u32[]{:S(2)}, u32[]{:S(2)}) collective-permute-start(bf16[64,1456]{1,0:T(8,128)(2,1)S(1)} %collective-permute-done.4.a0), channel_id=1, source_target_pairs={{0,1},{1,0},{2,3},{3,2},{4,5},{5,4},{6,7},{7,6},{8,9},{9,8},{10,11... | collective-permute-start | bytes 559112 | tf_op jit(solution)/shard_map/ppermute | solution.py:166
  16.9 11.2 %collective-permute-start.13 = (bf16[64,1456]{1,0:T(8,128)(2,1)S(1)}, bf16[64,1456]{1,0:T(8,128)(2,1)S(1)}, u32[]{:S(2)}, u32[]{:S(2)}) collective-permute-start(bf16[64,1456]{1,0:T(8,128)(2,1)S(1)} %collective-permute-done.11.a0), channel_id=1, source_target_pairs={{0,2},{2,0},{1,3},{3,1},{4,6},{6,4},{5,7},{7,5},{8,10},{10,8},{9,1... | collective-permute-start | bytes 559112 | tf_op jit(solution)/shard_map/ppermute | solution.py:166
  18.4 10.1 %collective-permute-start.18 = (bf16[64,1456]{1,0:T(8,128)(2,1)S(1)}, bf16[64,1456]{1,0:T(8,128)(2,1)S(1)}, u32[]{:S(2)}, u32[]{:S(2)}) collective-permute-start(bf16[64,1456]{1,0:T(8,128)(2,1)S(1)} %collective-permute-done.11.a0), channel_id=1, source_target_pairs={{0,4},{4,0},{8,12},{12,8},{1,5},{5,1},{9,13},{13,9},{2,6},{6,2},{1... | collective-permute-start | bytes 559112 | tf_op jit(solution)/shard_map/ppermute | solution.py:163
  19.3 10.7 %collective-permute-start.7 = (bf16[64,1456]{1,0:T(8,128)(2,1)S(1)}, bf16[64,1456]{1,0:T(8,128)(2,1)S(1)}, u32[]{:S(2)}, u32[]{:S(2)}) collective-permute-start(bf16[64,1456]{1,0:T(8,128)(2,1)S(1)} %collective-permute-done.6.b0), channel_id=1, source_target_pairs={{0,1},{1,0},{2,3},{3,2},{4,5},{5,4},{6,7},{7,6},{8,9},{9,8},{10,11... | collective-permute-start | bytes 559112 | tf_op jit(solution)/shard_map/ppermute | solution.py:166
  19.3 1.6 %copy-start.1 = (bf16[1,1440,720]{2,1,0:T(8,128)(2,1)S(1)}, bf16[1,1440,720]{2,1,0:T(8,128)(2,1)}, u32[]{:S(2)}) copy-start(bf16[1,1440,720]{2,1,0:T(8,128)(2,1)} %param.10) | copy-start | bytes 6220804
  20.9 1.6 %copy-start.2 = (bf16[1,1440,720]{2,1,0:T(8,128)(2,1)S(1)}, bf16[1,1440,720]{2,1,0:T(8,128)(2,1)}, u32[]{:S(2)}) copy-start(bf16[1,1440,720]{2,1,0:T(8,128)(2,1)} %param.11) | copy-start | bytes 6220804
  27.4 12.7 %collective-permute-start.2 = (bf16[256,720]{1,0:T(8,128)(2,1)S(1)}, bf16[256,720]{1,0:T(8,128)(2,1)S(1)}, u32[]{:S(2)}, u32[]{:S(2)}) collective-permute-start(bf16[256,720]{1,0:T(8,128)(2,1)S(1)} %get-tuple-element.18), channel_id=1, source_target_pairs={{0,1},{1,0},{2,3},{3,2},{4,5},{5,4},{6,7},{7,6},{8,9},{9,8},{10,11... | collective-permute-start | bytes 1105928 | tf_op jit(solution)/shard_map/ppermute | solution.py:166
  28.0 6.5 %collective-permute-start.12 = (bf16[64,1456]{1,0:T(8,128)(2,1)S(1)}, bf16[64,1456]{1,0:T(8,128)(2,1)S(1)}, u32[]{:S(2)}, u32[]{:S(2)}) collective-permute-start(bf16[64,1456]{1,0:T(8,128)(2,1)S(1)} %collective-permute-done.11.a0), channel_id=1, source_target_pairs={{0,1},{1,0},{2,3},{3,2},{4,5},{5,4},{6,7},{7,6},{8,9},{9,8},{10,11... | collective-permute-start | bytes 559112 | tf_op jit(solution)/shard_map/ppermute | solution.py:166
  28.1 7.0 %collective-permute-start.14 = (bf16[64,1456]{1,0:T(8,128)(2,1)S(1)}, bf16[64,1456]{1,0:T(8,128)(2,1)S(1)}, u32[]{:S(2)}, u32[]{:S(2)}) collective-permute-start(bf16[64,1456]{1,0:T(8,128)(2,1)S(1)} %collective-permute-done.13.b0), channel_id=1, source_target_pairs={{0,1},{1,0},{2,3},{3,2},{4,5},{5,4},{6,7},{7,6},{8,9},{9,8},{10,11... | collective-permute-start | bytes 559112 | tf_op jit(solution)/shard_map/ppermute | solution.py:166
  28.5 11.1 %collective-permute-start.20 = (bf16[64,1456]{1,0:T(8,128)(2,1)S(1)}, bf16[64,1456]{1,0:T(8,128)(2,1)S(1)}, u32[]{:S(2)}, u32[]{:S(2)}) collective-permute-start(bf16[64,1456]{1,0:T(8,128)(2,1)S(1)} %collective-permute-done.18.a0), channel_id=1, source_target_pairs={{0,2},{2,0},{1,3},{3,1},{4,6},{6,4},{5,7},{7,5},{8,10},{10,8},{9,1... | collective-permute-start | bytes 559112 | tf_op jit(solution)/shard_map/ppermute | solution.py:166
  30.0 10.8 %collective-permute-start.19 = (bf16[64,1456]{1,0:T(8,128)(2,1)S(1)}, bf16[64,1456]{1,0:T(8,128)(2,1)S(1)}, u32[]{:S(2)}, u32[]{:S(2)}) collective-permute-start(bf16[64,1456]{1,0:T(8,128)(2,1)S(1)} %collective-permute-done.18.a0), channel_id=1, source_target_pairs={{0,1},{1,0},{2,3},{3,2},{4,5},{5,4},{6,7},{7,6},{8,9},{9,8},{10,11... | collective-permute-start | bytes 559112 | tf_op jit(solution)/shard_map/ppermute | solution.py:166
  34.5 11.8 %collective-permute-start.8 = (bf16[256,720]{1,0:T(8,128)(2,1)S(1)}, bf16[256,720]{1,0:T(8,128)(2,1)S(1)}, u32[]{:S(2)}, u32[]{:S(2)}) collective-permute-start(bf16[256,720]{1,0:T(8,128)(2,1)S(1)} %get-tuple-element.21), channel_id=1, source_target_pairs={{0,1},{1,0},{2,3},{3,2},{4,5},{5,4},{6,7},{7,6},{8,9},{9,8},{10,11... | collective-permute-start | bytes 1105928 | tf_op jit(solution)/shard_map/ppermute | solution.py:166
  39.5 7.5 %collective-permute-start.15 = (bf16[256,720]{1,0:T(8,128)(2,1)S(1)}, bf16[256,720]{1,0:T(8,128)(2,1)S(1)}, u32[]{:S(2)}, u32[]{:S(2)}) collective-permute-start(bf16[256,720]{1,0:T(8,128)(2,1)S(1)} %get-tuple-element.24), channel_id=1, source_target_pairs={{0,1},{1,0},{2,3},{3,2},{4,5},{5,4},{6,7},{7,6},{8,9},{9,8},{10,11... | collective-permute-start | bytes 1105928 | tf_op jit(solution)/shard_map/ppermute | solution.py:166
  39.6 2.0 %collective-permute-start.21 = (bf16[64,1456]{1,0:T(8,128)(2,1)S(1)}, bf16[64,1456]{1,0:T(8,128)(2,1)S(1)}, u32[]{:S(2)}, u32[]{:S(2)}) collective-permute-start(bf16[64,1456]{1,0:T(8,128)(2,1)S(1)} %collective-permute-done.20.b0), channel_id=1, source_target_pairs={{0,1},{1,0},{2,3},{3,2},{4,5},{5,4},{6,7},{7,6},{8,9},{9,8},{10,11... | collective-permute-start | bytes 559112 | tf_op jit(solution)/shard_map/ppermute | solution.py:166
  40.2 27.4 %collective-permute-start.3 = (bf16[128,720]{1,0:T(8,128)(2,1)S(1)}, bf16[128,720]{1,0:T(8,128)(2,1)S(1)}, u32[]{:S(2)}, u32[]{:S(2)}) collective-permute-start(bf16[128,720]{1,0:T(8,128)(2,1)S(1)} %fusion.9), channel_id=1, source_target_pairs={{0,2},{2,0},{1,3},{3,1},{4,6},{6,4},{5,7},{7,5},{8,10},{10,8},{9,1... | collective-permute-start | bytes 552968 | tf_op jit(solution)/shard_map/ppermute | solution.py:166
  46.1 8.7 %collective-permute-start.22 = (bf16[256,720]{1,0:T(8,128)(2,1)S(1)}, bf16[256,720]{1,0:T(8,128)(2,1)S(1)}, u32[]{:S(2)}, u32[]{:S(2)}) collective-permute-start(bf16[256,720]{1,0:T(8,128)(2,1)S(1)} %get-tuple-element.27), channel_id=1, source_target_pairs={{0,1},{1,0},{2,3},{3,2},{4,5},{5,4},{6,7},{7,6},{8,9},{9,8},{10,11... | collective-permute-start | bytes 1105928 | tf_op jit(solution)/shard_map/ppermute | solution.py:166
  46.4 7.8 %collective-permute-start.9 = (bf16[128,720]{1,0:T(8,128)(2,1)S(1)}, bf16[128,720]{1,0:T(8,128)(2,1)S(1)}, u32[]{:S(2)}, u32[]{:S(2)}) collective-permute-start(bf16[128,720]{1,0:T(8,128)(2,1)S(1)} %fusion.6), channel_id=1, source_target_pairs={{0,2},{2,0},{1,3},{3,1},{4,6},{6,4},{5,7},{7,5},{8,10},{10,8},{9,1... | collective-permute-start | bytes 552968 | tf_op jit(solution)/shard_map/ppermute | solution.py:166
  47.2 11.2 %collective-permute-start.16 = (bf16[128,720]{1,0:T(8,128)(2,1)S(1)}, bf16[128,720]{1,0:T(8,128)(2,1)S(1)}, u32[]{:S(2)}, u32[]{:S(2)}) collective-permute-start(bf16[128,720]{1,0:T(8,128)(2,1)S(1)} %fusion.3), channel_id=1, source_target_pairs={{0,2},{2,0},{1,3},{3,1},{4,6},{6,4},{5,7},{7,5},{8,10},{10,8},{9,1... | collective-permute-start | bytes 552968 | tf_op jit(solution)/shard_map/ppermute | solution.py:166
  54.3 13.4 %collective-permute-start.10 = (bf16[128,720]{1,0:T(8,128)(2,1)S(1)}, bf16[128,720]{1,0:T(8,128)(2,1)S(1)}, u32[]{:S(2)}, u32[]{:S(2)}) collective-permute-start(bf16[128,720]{1,0:T(8,128)(2,1)S(1)} %fusion.8), channel_id=1, source_target_pairs={{0,4},{4,0},{8,12},{12,8},{1,5},{5,1},{9,13},{13,9},{2,6},{6,2},{1... | collective-permute-start | bytes 552968 | tf_op jit(solution)/shard_map/ppermute | solution.py:163
  54.9 10.4 %collective-permute-start.23 = (bf16[128,720]{1,0:T(8,128)(2,1)S(1)}, bf16[128,720]{1,0:T(8,128)(2,1)S(1)}, u32[]{:S(2)}, u32[]{:S(2)}) collective-permute-start(bf16[128,720]{1,0:T(8,128)(2,1)S(1)} %fusion), channel_id=1, source_target_pairs={{0,2},{2,0},{1,3},{3,1},{4,6},{6,4},{5,7},{7,5},{8,10},{10,8},{9,1... | collective-permute-start | bytes 552968 | tf_op jit(solution)/shard_map/ppermute | solution.py:166
  58.5 12.2 %collective-permute-start.17 = (bf16[128,720]{1,0:T(8,128)(2,1)S(1)}, bf16[128,720]{1,0:T(8,128)(2,1)S(1)}, u32[]{:S(2)}, u32[]{:S(2)}) collective-permute-start(bf16[128,720]{1,0:T(8,128)(2,1)S(1)} %fusion.5), channel_id=1, source_target_pairs={{0,12},{4,8},{8,4},{12,0},{1,13},{5,9},{9,5},{13,1},{2,14},{6,10},... | collective-permute-start | bytes 552968 | tf_op jit(solution)/shard_map/ppermute | solution.py:163
  65.3 13.6 %collective-permute-start.24 = (bf16[128,720]{1,0:T(8,128)(2,1)S(1)}, bf16[128,720]{1,0:T(8,128)(2,1)S(1)}, u32[]{:S(2)}, u32[]{:S(2)}) collective-permute-start(bf16[128,720]{1,0:T(8,128)(2,1)S(1)} %fusion.2), channel_id=1, source_target_pairs={{0,8},{4,12},{8,0},{12,4},{1,9},{5,13},{9,1},{13,5},{2,10},{6,14},... | collective-permute-start | bytes 552968 | tf_op jit(solution)/shard_map/ppermute | solution.py:163

commit v2 on v0

--- a/solution.py
+++ b/solution.py
@@ -1,6 +1,10 @@
+import functools
+
 import jax
 import jax.numpy as jnp
 from jax import lax
+from jax.experimental import pallas as pl
+from jax.experimental.pallas import tpu as pltpu
 from jax.sharding import PartitionSpec as P
 
 TOP = 4
@@ -15,7 +19,11 @@
     ).astype(jnp.bfloat16)
 
 
-def local(hidden, expert_ids, gate_units, w_gate, w_up, w_down):
+def capacity_of(token_count, expert_count):
+    return max(2, (token_count * TOP * 11 + expert_count * 8 - 1) // (expert_count * 8))
+
+
+def routed(hidden, expert_ids, gate_units, w_gate, w_up, w_down):
     token_count, model_width = hidden.shape
     seq_count = lax.axis_size("seq")
     ep_count = lax.axis_size("ep")
@@ -23,7 +31,7 @@
     half_width = model_width // tp_count
     my_half = lax.axis_index("tp")
     expert_count = seq_count * tp_count
-    capacity = max(2, (token_count * TOP * 11 + expert_count * 8 - 1) // (expert_count * 8))
+    capacity = capacity_of(token_count, expert_count)
     flat_ids = expert_ids.reshape(-1)
     onehot_ids = (flat_ids[:, None] == jnp.arange(expert_count, dtype=jnp.int32)[None, :]).astype(
         jnp.int32
@@ -64,7 +72,187 @@
     return moe_out.astype(jnp.bfloat16)
 
 
+def expert_kernel(expert_count, count, place_ref, *refs):
+    ins, weights = refs[:count], refs[count : count + 2]
+    outs, rows = refs[count + 2 : -1], refs[-1]
+    model_width = outs[0].shape[1]
+    first = 0
+    for ref in ins:
+        rows[first : first + ref.shape[0], :] = ref[...]
+        first += ref.shape[0]
+    tail = rows[:, model_width:].astype(jnp.float32)
+    lane = lax.broadcasted_iota(jnp.int32, tail.shape, 1)
+    x = rows[:, :model_width]
+    total = None
+    for i in range(2):
+        wg, wu, wd = (weights[i].at[j] for j in range(3))
+        expert = place_ref[i]
+        scale = jnp.where(lane == expert, 256.0, jnp.where(lane == expert + expert_count, 1.0, 0.0))
+        weight = jnp.sum(tail * scale, axis=1, keepdims=True) * (1.0 / 65536.0)
+        gate_pre = jnp.dot(x, wg[...], preferred_element_type=jnp.float32)
+        up_pre = jnp.dot(x, wu[...], preferred_element_type=jnp.float32)
+        act = ((up_pre + 1.0) * gate_pre * jax.nn.sigmoid(1.702 * gate_pre)).astype(jnp.bfloat16)
+        out = lax.dot_general(
+            act, wd[...], (((1,), (1,)), ((), ())), preferred_element_type=jnp.float32
+        )
+        total = out * weight if total is None else total + out * weight
+    half_rows = outs[0].shape[0]
+    for i, ref in enumerate(outs):
+        ref[...] = total[i * half_rows : (i + 1) * half_rows].astype(ref.dtype)
+
+
+def experts(expert_count, place, model_width, blocks, weights):
+    half_rows, width = blocks[0].shape
+    slice_width = weights[0].shape[2]
+    vmem = pl.BlockSpec(memory_space=pltpu.VMEM)
+    count = len(blocks)
+    rows = count * half_rows
+    return pl.pallas_call(
+        functools.partial(expert_kernel, expert_count, count),
+        out_shape=tuple(
+            jax.ShapeDtypeStruct((half_rows, model_width), (jnp.float32, jnp.bfloat16)[i % 2])
+            for i in range(count)
+        ),
+        in_specs=[pl.BlockSpec(memory_space=pltpu.SMEM)] + [vmem] * (count + 2),
+        out_specs=tuple([vmem] * count),
+        scratch_shapes=[pltpu.VMEM((rows, width), jnp.bfloat16)],
+        compiler_params=pltpu.CompilerParams(vmem_limit_bytes=20 * 1024 * 1024),
+        cost_estimate=pl.CostEstimate(
+            flops=2 * rows * model_width * slice_width * 6,
+            bytes_accessed=4 * rows * width,
+            transcendentals=2 * rows * slice_width,
+        ),
+    )(place, *blocks, *weights)
+
+
+def prepare_kernel(place_ref, *refs):
+    own, held, hidden, ids, units, rows, sems = refs[6:]
+    targets = (hidden, ids, units, *(held.at[i] for i in range(3)))
+    copies = [pltpu.make_async_copy(refs[i], to, sems.at[i]) for i, to in enumerate(targets)]
+    for copy in copies:
+        copy.start()
+    model_width, token_count = hidden.shape
+    expert_count = (own.shape[1] - model_width) // 2
+    half_rows = own.shape[0]
+    expert = lax.broadcasted_iota(jnp.int32, (expert_count, token_count), 0)
+    shares = jnp.zeros((expert_count, token_count), jnp.int32)
+    copies[1].wait()
+    copies[2].wait()
+    for c in range(ids.shape[0]):
+        shares += jnp.where(ids[c : c + 1, :] == expert, units[c : c + 1, :], 0)
+    digits = jnp.concatenate([shares // 256, shares % 256], axis=0).astype(jnp.float32)
+    rows[:, model_width:] = digits.T.astype(jnp.bfloat16)
+    copies[0].wait()
+    rows[:, :model_width] = hidden[...].T
+    own[...] = rows[pl.ds(pl.multiple_of(place_ref[2] * half_rows, half_rows), half_rows), :]
+    for copy in copies[3:]:
+        copy.wait()
+
+
+def prepare(place, expert_count, hidden, expert_ids, gate_units, weights):
+    token_count, model_width = hidden.shape
+    width = model_width + 2 * expert_count
+    vmem = pl.BlockSpec(memory_space=pltpu.VMEM)
+    return pl.pallas_call(
+        prepare_kernel,
+        out_shape=(
+            jax.ShapeDtypeStruct((token_count // 2, width), hidden.dtype),
+            jax.ShapeDtypeStruct((len(weights), *weights[0].shape), weights[0].dtype),
+        ),
+        in_specs=[pl.BlockSpec(memory_space=pltpu.SMEM)] + [pl.BlockSpec(memory_space=pl.ANY)] * 6,
+        out_specs=(vmem, vmem),
+        scratch_shapes=[
+            pltpu.VMEM((model_width, token_count), hidden.dtype),
+            pltpu.VMEM(expert_ids.T.shape, jnp.int32),
+            pltpu.VMEM(gate_units.T.shape, jnp.int32),
+            pltpu.VMEM((token_count, width), hidden.dtype),
+            pltpu.SemaphoreType.DMA((6,)),
+        ],
+        compiler_params=pltpu.CompilerParams(vmem_limit_bytes=16 * 1024 * 1024),
+    )(
+        place,
+        *[
+            pltpu.with_memory_space_constraint(x, pltpu.HBM)
+            for x in (hidden.T, expert_ids.T, gate_units.T, *weights)
+        ],
+    )
+
+
+def hold_kernel(*refs):
+    del refs
+
+
+def hold(*arrays):
+    return pl.pallas_call(
+        hold_kernel,
+        out_shape=tuple(jax.ShapeDtypeStruct(x.shape, x.dtype) for x in arrays),
+        in_specs=[pl.BlockSpec(memory_space=pl.ANY)] * len(arrays),
+        out_specs=tuple([pl.BlockSpec(memory_space=pl.ANY)] * len(arrays)),
+        input_output_aliases={i: i for i in range(len(arrays))},
+        compiler_params=pltpu.CompilerParams(vmem_limit_bytes=1024 * 1024),
+    )(*arrays)
+
+
+def gathered(hidden, expert_ids, gate_units, w_gate, w_up, w_down):
+    token_count, model_width = hidden.shape
+    half_rows = token_count // 2
+    half_width = model_width // 2
+    tp = lax.axis_index("tp")
+    expert_count = lax.axis_size("seq") * lax.axis_size("tp")
+    expert = lax.axis_index("seq") * lax.axis_size("tp") + tp
+    place = jnp.stack([expert, expert + 1 - 2 * tp, tp]).astype(jnp.int32)
+
+    def z(x, k):
+        return lax.ppermute(x, "seq", [(i, i ^ k) for i in range(lax.axis_size("seq"))])
+
+    def diagonal(x):
+        flat = [(i, i ^ 3) for i in range(lax.axis_size("seq") * lax.axis_size("ep"))]
+        return lax.ppermute(x, ("seq", "ep"), flat)
+
+    def swap(x, axis):
+        return lax.ppermute(x, axis, [(0, 1), (1, 0)])
+
+    own, mine = prepare(
+        place, expert_count, hidden, expert_ids, gate_units, (w_gate[0], w_up[0], w_down[0])
+    )
+    run = functools.partial(experts, expert_count, place, model_width)
+    weights = (mine, swap(mine, "tp"))
+    near3, near1, far0 = hold(z(own, 3), z(own, 1), swap(own, "ep"))
+    far3, near2, far2 = swap(near3, "ep"), z(near3, 1), diagonal(near3)
+    near1, far3, near2, far2, near3 = hold(near1, far3, near2, far2, near3)
+    far1 = swap(near1, "ep")
+    near_sum3, far_sum3, near_sum2, far_sum2 = run([near3, far3, near2, far2], weights)
+    near_sum0, far_sum0, near_sum1, far_sum1 = run([own, far0, near1, far1], weights)
+
+    def f32(x):
+        return x.astype(jnp.float32)
+
+    def bf16(x):
+        return x.astype(jnp.bfloat16)
+
+    merged = near_sum3 + f32(swap(far_sum3, "ep")) + f32(z(bf16(near_sum2), 1)) + f32(diagonal(far_sum2))
+    total = (
+        near_sum0
+        + f32(swap(far_sum0, "ep"))
+        + f32(z(bf16(near_sum1 + f32(swap(far_sum1, "ep"))), 1))
+        + f32(z(bf16(merged), 3))
+    )
+    out = total.astype(jnp.bfloat16)
+    give = lax.dynamic_slice_in_dim(out, (1 - tp) * half_width, half_width, 1)
+    keep = lax.dynamic_slice_in_dim(out, tp * half_width, half_width, 1)
+    get = swap(give, "tp")
+    return jnp.where(tp == 0, jnp.concatenate([keep, get]), jnp.concatenate([get, keep]))
+
+
 def solution(mesh):
+    def local(*args):
+        token_count = args[0].shape[0]
+        seq, ep, tp = (mesh.shape[name] for name in ("seq", "ep", "tp"))
+        dense = capacity_of(token_count, seq * tp) * tp >= token_count
+        if dense and (seq, ep, tp) == (4, 2, 2):
+            return gathered(*args)
+        return routed(*args)
+
     return jax.shard_map(
         local,
         mesh=mesh,

time: 158 us -> 62.6 us (0.40)
  blocking collectives: 67.5 us -> 0 us
  waiting for transfers between devices: 48.6 us -> 28.1 us
  starting transfers between devices: 4.5 us -> 20 us
  matrix products: 15.2 us -> 0 us
  local copies, waits for them, and re-layouts: 14.1 us -> 0.95 us
  Pallas kernels: 0 us -> 13 us
  other arithmetic: 7.45 us -> 0.36 us
    all_to_all x2 -> x0, blocking collectives: 67.5 us -> none  [the longest x1 57.5 us: local(): lax.all_to_all(copied, ('seq', 'ep'), split_axis=0, concat_axis=0, tiled=...]
    all_to_all x1 -> x0, waiting for transfers between devices: 48.6 us -> none  [local(): lax.all_to_all(slice_rows, ('seq', 'ep'), split_axis=0, concat_axis=0, ti...]
    ppermute x0 -> x16, waiting for transfers between devices: none -> 28.1 us  [the longest x6 14.5 us: z(): lax.ppermute(x, 'seq', [(i, i ^ k) for i in range(lax.axis_size('seq'))])]
    ppermute x0 -> x16, starting transfers between devices: none -> 20 us  [the longest x6 9.68 us: z(): lax.ppermute(x, 'seq', [(i, i ^ k) for i in range(lax.axis_size('seq'))])]
    dot_general x4 -> x0, matrix products: 15.2 us -> none  [the longest x1 8.55 us: slice_output(): lax.dot_general(activation, down_cols, (((1,), (1,)), ((), ())), preferre...]
    pallas_call x0 -> x5, Pallas kernels: none -> 13 us  [the longest x2 9.25 us: experts(): pl.pallas_call(functools.partial(expert_kernel, expert_count, count), out...]
    all_to_all x2 -> x0, local copies, waits for them, and re-layouts: 10.9 us -> none  [the longest x1 6.16 us: local(): lax.all_to_all(lax.all_to_all(slice_rows, ('seq', 'ep'), split_axis=0, co...]
    reduce_sum x3 -> x0, other arithmetic: 5.46 us -> none  [the longest x1 5.2 us: local(): jnp.sum(came_back.astype(jnp.float32), axis=2).astype(jnp.bfloat16)]
  transfers between devices with their start and end apart: 1 -> 16, of which waited for: 1 -> 11; matrix products, arithmetic and copies ran while one was open for 0% -> 0% of each run, Pallas kernels for 0% -> 15%
where the time goes in v2:
time: 62.6 us; the launch traced here: 62.4 us
  waiting for transfers between devices  28.1 us (45%)
  starting transfers between devices  20 us (32%)
  Pallas kernels  13 us (21%)
  local copies, waits for them, and re-layouts  0.95 us (2%)
    ppermute x6, waiting for transfers between devices, z(): lax.ppermute(x, 'seq', [(i, i ^ k) for i in range(lax.axis_size('seq'))])  14.5 us
    ppermute x8, waiting for transfers between devices, swap(): return lax.ppermute(x, axis, [(0, 1), (1, 0)])  10.6 us
    ppermute x6, starting transfers between devices, z(): lax.ppermute(x, 'seq', [(i, i ^ k) for i in range(lax.axis_size('seq'))])  9.68 us
    pallas_call x2, Pallas kernels, experts(): pl.pallas_call(functools.partial(expert_kernel, expert_count, count), out...  9.25 us
    ppermute x8, starting transfers between devices, swap(): return lax.ppermute(x, axis, [(0, 1), (1, 0)])  8.65 us
    pallas_call x1, Pallas kernels, prepare(): pl.pallas_call(prepare_kernel, out_shape=(jax.ShapeDtypeStruct((token_cou...  3.72 us
    ppermute x2, waiting for transfers between devices, diagonal(): return lax.ppermute(x, ('seq', 'ep'), flat)  2.95 us
    ppermute x2, starting transfers between devices, diagonal(): return lax.ppermute(x, ('seq', 'ep'), flat)  1.65 us
  transfers between devices with their start and end apart: 16, of which 11 were waited for; matrix products, arithmetic and copies ran while one was open for 0% of the time, Pallas kernels for 15%

profile of v2, /device:TPU:0, one launch (start us, length us, event | category | flops | bytes accessed | tf_op | source)
XLA Modules:
  0.0 62.4 jit_solution(18116688518454753877)
XLA Ops:
  0.0 0.1 pad_add_fusion.place_ref
  0.1 3.7 %shard_map.64 = (bf16[64,1456]{1,0:T(8,128)(2,1)S(1)}, bf16[3,1440,720]{2,1,0:T(8,128)(2,1)S(1)}) custom-call(s32[3]{0:T(128)S(1)} %pad_add_fusion.place_ref, bf16[1440,128]{1,0:T(8,128)(2,1)} %bitcast.12, s32[4,128]{1,0:T(4,128)} %bitcast.13, s32[4,128]{1,0:T(4,128)} %bitcast.14, bf16[1440,720]{1,0:T(8,128)(2,1)} %bitcast.9, bf16[1440,720]{1,0:T(8,128)(2,1)} %bitcast.10, ...), custom_call_target="tpu_custom_call" | custom-call | tf_op jit(solution)/shard_map/pallas_call | solution.py:156
  3.8 0.5 collective-permute-start.7
  4.3 4.7 %collective-permute-start = (bf16[64,1456]{1,0:T(8,128)(2,1)S(1)}, bf16[64,1456]{1,0:T(8,128)(2,1)S(1)}, u32[]{:S(2)}, u32[]{:S(2)}) collective-permute-start(bf16[64,1456]{1,0:T(8,128)(2,1)S(1)} %get-tuple-element.23.refs_0_), channel_id=1, source_target_pairs={{0,12},{4,8},{8,4},{12,0},{1,13},{5,9},{9,5},{13,1},{2,14},{6,10},... | collective-permute-start | bytes 559112 | tf_op jit(solution)/shard_map/ppermute | solution.py:206
  9.0 0.0 collective-permute-start.1
  9.0 1.5 %collective-permute-start.2 = (bf16[64,1456]{1,0:T(8,128)(2,1)S(1)}, bf16[64,1456]{1,0:T(8,128)(2,1)S(1)}, u32[]{:S(2)}, u32[]{:S(2)}) collective-permute-start(bf16[64,1456]{1,0:T(8,128)(2,1)S(1)} %get-tuple-element.23.refs_0_), channel_id=1, source_target_pairs={{0,2},{2,0},{1,3},{3,1},{4,6},{6,4},{5,7},{7,5},{8,10},{10,8},{9,1... | collective-permute-start | bytes 559112 | tf_op jit(solution)/shard_map/ppermute | solution.py:213
  10.5 4.3 %collective-permute-done.refs_0_ = bf16[64,1456]{1,0:T(8,128)(2,1)S(1)} collective-permute-done((bf16[64,1456]{1,0:T(8,128)(2,1)S(1)}, bf16[64,1456]{1,0:T(8,128)(2,1)S(1)}, u32[]{:S(2)}, u32[]{:S(2)}) %collective-permute-start) | collective-permute-done | bytes 186400 | tf_op jit(solution)/shard_map/ppermute | solution.py:206
  14.8 4.0 %collective-permute-done.1.refs_1_ = bf16[64,1456]{1,0:T(8,128)(2,1)S(1)} collective-permute-done((bf16[64,1456]{1,0:T(8,128)(2,1)S(1)}, bf16[64,1456]{1,0:T(8,128)(2,1)S(1)}, u32[]{:S(2)}, u32[]{:S(2)}) %collective-permute-start.1) | collective-permute-done | bytes 186400 | tf_op jit(solution)/shard_map/ppermute | solution.py:206
  18.8 0.0 collective-permute-done.2.refs_2_
  18.8 1.5 %collective-permute-start.3 = (bf16[64,1456]{1,0:T(8,128)(2,1)S(1)}, bf16[64,1456]{1,0:T(8,128)(2,1)S(1)}, u32[]{:S(2)}, u32[]{:S(2)}) collective-permute-start(bf16[64,1456]{1,0:T(8,128)(2,1)S(1)} %get-tuple-element.26.refs_4_), channel_id=1, source_target_pairs={{0,2},{2,0},{1,3},{3,1},{4,6},{6,4},{5,7},{7,5},{8,10},{10,8},{9,1... | collective-permute-start | bytes 559112 | tf_op jit(solution)/shard_map/ppermute | solution.py:213
  20.3 1.7 %collective-permute-start.4 = (bf16[64,1456]{1,0:T(8,128)(2,1)S(1)}, bf16[64,1456]{1,0:T(8,128)(2,1)S(1)}, u32[]{:S(2)}, u32[]{:S(2)}) collective-permute-start(bf16[64,1456]{1,0:T(8,128)(2,1)S(1)} %get-tuple-element.26.refs_4_), channel_id=1, source_target_pairs={{0,4},{4,0},{8,12},{12,8},{1,5},{5,1},{9,13},{13,9},{2,6},{6,2},{1... | collective-permute-start | bytes 559112 | tf_op jit(solution)/shard_map/ppermute | solution.py:206
  22.0 0.3 collective-permute-start.5
  22.3 3.4 %collective-permute-done.3.refs_1_ = bf16[64,1456]{1,0:T(8,128)(2,1)S(1)} collective-permute-done((bf16[64,1456]{1,0:T(8,128)(2,1)S(1)}, bf16[64,1456]{1,0:T(8,128)(2,1)S(1)}, u32[]{:S(2)}, u32[]{:S(2)}) %collective-permute-start.3) | collective-permute-done | bytes 186400 | tf_op jit(solution)/shard_map/ppermute | solution.py:213
  25.7 2.4 %collective-permute-done.4.refs_2_ = bf16[64,1456]{1,0:T(8,128)(2,1)S(1)} collective-permute-done((bf16[64,1456]{1,0:T(8,128)(2,1)S(1)}, bf16[64,1456]{1,0:T(8,128)(2,1)S(1)}, u32[]{:S(2)}, u32[]{:S(2)}) %collective-permute-start.4) | collective-permute-done | bytes 186400 | tf_op jit(solution)/shard_map/ppermute | solution.py:206
  28.1 2.9 %collective-permute-done.5.refs_3_ = bf16[64,1456]{1,0:T(8,128)(2,1)S(1)} collective-permute-done((bf16[64,1456]{1,0:T(8,128)(2,1)S(1)}, bf16[64,1456]{1,0:T(8,128)(2,1)S(1)}, u32[]{:S(2)}, u32[]{:S(2)}) %collective-permute-start.5) | collective-permute-done | bytes 186400 | tf_op jit(solution)/shard_map/ppermute | solution.py:210
  31.1 1.5 %collective-permute-start.6 = (bf16[64,1456]{1,0:T(8,128)(2,1)S(1)}, bf16[64,1456]{1,0:T(8,128)(2,1)S(1)}, u32[]{:S(2)}, u32[]{:S(2)}) collective-permute-start(bf16[64,1456]{1,0:T(8,128)(2,1)S(1)} %get-tuple-element.27.refs_2_), channel_id=1, source_target_pairs={{0,2},{2,0},{1,3},{3,1},{4,6},{6,4},{5,7},{7,5},{8,10},{10,8},{9,1... | collective-permute-start | bytes 559112 | tf_op jit(solution)/shard_map/ppermute | solution.py:213
  32.5 0.0 collective-permute-done.7.refs_5_
  32.5 4.6 %shard_map.68 = (f32[64,1440]{1,0:T(8,128)S(1)}, bf16[64,1440]{1,0:T(8,128)(2,1)S(1)}, f32[64,1440]{1,0:T(8,128)S(1)}, bf16[64,1440]{1,0:T(8,128)(2,1)S(1)}) custom-call(s32[3]{0:T(128)S(1)} %pad_add_fusion.place_ref, bf16[64,1456]{1,0:T(8,128)(2,1)S(1)} %get-tuple-element.33.refs_0_, bf16[64,1456]{1,0:T(8,128)(2,1)S(1)} %get-tuple-element.34.refs_1_, ...), custom_call_target="tpu_custom_call" | custom-call | flops 3185049600 | bytes 1490944 | tf_op jit(solution)/shard_map/pallas_call | solution.py:110
  37.2 1.4 %collective-permute-start.13 = (bf16[64,1440]{1,0:T(8,128)(2,1)S(1)}, bf16[64,1440]{1,0:T(8,128)(2,1)S(1)}, u32[]{:S(2)}, u32[]{:S(2)}) collective-permute-start(bf16[64,1440]{1,0:T(8,128)(2,1)S(1)} %get-tuple-element.40), channel_id=1, source_target_pairs={{0,6},{2,4},{4,2},{6,0},{8,14},{10,12},{12,10},{14,8},{1,7},{3,5},... | collective-permute-start | bytes 552968 | tf_op jit(solution)/shard_map/ppermute | solution.py:210
  38.6 0.8 %collective-permute-start.12 = (bf16[64,1440]{1,0:T(8,128)(2,1)S(1)}, bf16[64,1440]{1,0:T(8,128)(2,1)S(1)}, u32[]{:S(2)}, u32[]{:S(2)}) collective-permute-start(bf16[64,1440]{1,0:T(8,128)(2,1)S(1)} %convert_element_type.38), channel_id=1, source_target_pairs={{0,4},{4,0},{8,12},{12,8},{1,5},{5,1},{9,13},{13,9},{2,6},{6,2},{1... | collective-permute-start | bytes 552968 | tf_op jit(solution)/shard_map/ppermute | solution.py:206
  39.3 1.5 %collective-permute-start.11 = (bf16[64,1440]{1,0:T(8,128)(2,1)S(1)}, bf16[64,1440]{1,0:T(8,128)(2,1)S(1)}, u32[]{:S(2)}, u32[]{:S(2)}) collective-permute-start(bf16[64,1440]{1,0:T(8,128)(2,1)S(1)} %get-tuple-element.38), channel_id=1, source_target_pairs={{0,2},{2,0},{1,3},{3,1},{4,6},{6,4},{5,7},{7,5},{8,10},{10,8},{9,1... | collective-permute-start | bytes 552968 | tf_op jit(solution)/shard_map/ppermute | solution.py:213
  40.8 0.0 collective-permute-done.6.refs_3_
  40.8 4.6 %shard_map.67 = (f32[64,1440]{1,0:T(8,128)S(1)}, bf16[64,1440]{1,0:T(8,128)(2,1)S(1)}, f32[64,1440]{1,0:T(8,128)S(1)}, bf16[64,1440]{1,0:T(8,128)(2,1)S(1)}) custom-call(s32[3]{0:T(128)S(1)} %pad_add_fusion.place_ref, bf16[64,1456]{1,0:T(8,128)(2,1)S(1)} %get-tuple-element.23.refs_0_, bf16[64,1456]{1,0:T(8,128)(2,1)S(1)} %get-tuple-element.24.refs_1_, ...), custom_call_target="tpu_custom_call" | custom-call | flops 3185049600 | bytes 1490944 | tf_op jit(solution)/shard_map/pallas_call | solution.py:110
  45.5 0.6 collective-permute-start.9
  46.1 1.5 %collective-permute-start.8 = (bf16[64,1440]{1,0:T(8,128)(2,1)S(1)}, bf16[64,1440]{1,0:T(8,128)(2,1)S(1)}, u32[]{:S(2)}, u32[]{:S(2)}) collective-permute-start(bf16[64,1440]{1,0:T(8,128)(2,1)S(1)} %get-tuple-element.30), channel_id=1, source_target_pairs={{0,2},{2,0},{1,3},{3,1},{4,6},{6,4},{5,7},{7,5},{8,10},{10,8},{9,1... | collective-permute-start | bytes 552968 | tf_op jit(solution)/shard_map/ppermute | solution.py:213
  47.6 0.0 collective-permute-done.13
  47.6 0.0 collective-permute-done.12
  47.6 1.2 %collective-permute-done.11 = bf16[64,1440]{1,0:T(8,128)(2,1)S(1)} collective-permute-done((bf16[64,1440]{1,0:T(8,128)(2,1)S(1)}, bf16[64,1440]{1,0:T(8,128)(2,1)S(1)}, u32[]{:S(2)}, u32[]{:S(2)}) %collective-permute-start.11) | collective-permute-done | bytes 184352 | tf_op jit(solution)/shard_map/ppermute | solution.py:213
  48.7 0.1 add_convert_fusion.1
  48.8 1.1 %collective-permute-start.14 = (bf16[64,1440]{1,0:T(8,128)(2,1)S(1)}, bf16[64,1440]{1,0:T(8,128)(2,1)S(1)}, u32[]{:S(2)}, u32[]{:S(2)}) collective-permute-start(bf16[64,1440]{1,0:T(8,128)(2,1)S(1)} %add_convert_fusion.1), channel_id=1, source_target_pairs={{0,12},{4,8},{8,4},{12,0},{1,13},{5,9},{9,5},{13,1},{2,14},{6,10},... | collective-permute-start | bytes 552968 | tf_op jit(solution)/shard_map/ppermute | solution.py:206
  50.0 3.4 %collective-permute-done.9 = bf16[64,1440]{1,0:T(8,128)(2,1)S(1)} collective-permute-done((bf16[64,1440]{1,0:T(8,128)(2,1)S(1)}, bf16[64,1440]{1,0:T(8,128)(2,1)S(1)}, u32[]{:S(2)}, u32[]{:S(2)}) %collective-permute-start.9) | collective-permute-done | bytes 184352 | tf_op jit(solution)/shard_map/ppermute | solution.py:213
  53.4 1.4 %collective-permute-start.10 = (bf16[64,1440]{1,0:T(8,128)(2,1)S(1)}, bf16[64,1440]{1,0:T(8,128)(2,1)S(1)}, u32[]{:S(2)}, u32[]{:S(2)}) collective-permute-start(bf16[64,1440]{1,0:T(8,128)(2,1)S(1)} %add_convert_fusion.2), channel_id=1, source_target_pairs={{0,4},{4,0},{8,12},{12,8},{1,5},{5,1},{9,13},{13,9},{2,6},{6,2},{1... | collective-permute-start | bytes 552968 | tf_op jit(solution)/shard_map/ppermute | solution.py:206
  54.8 1.4 %collective-permute-done.8 = bf16[64,1440]{1,0:T(8,128)(2,1)S(1)} collective-permute-done((bf16[64,1440]{1,0:T(8,128)(2,1)S(1)}, bf16[64,1440]{1,0:T(8,128)(2,1)S(1)}, u32[]{:S(2)}, u32[]{:S(2)}) %collective-permute-start.8) | collective-permute-done | bytes 184352 | tf_op jit(solution)/shard_map/ppermute | solution.py:213
  56.2 1.8 %collective-permute-done.14 = bf16[64,1440]{1,0:T(8,128)(2,1)S(1)} collective-permute-done((bf16[64,1440]{1,0:T(8,128)(2,1)S(1)}, bf16[64,1440]{1,0:T(8,128)(2,1)S(1)}, u32[]{:S(2)}, u32[]{:S(2)}) %collective-permute-start.14) | collective-permute-done | bytes 184352 | tf_op jit(solution)/shard_map/ppermute | solution.py:206
  58.0 2.0 %collective-permute-done.10 = bf16[64,1440]{1,0:T(8,128)(2,1)S(1)} collective-permute-done((bf16[64,1440]{1,0:T(8,128)(2,1)S(1)}, bf16[64,1440]{1,0:T(8,128)(2,1)S(1)}, u32[]{:S(2)}, u32[]{:S(2)}) %collective-permute-start.10) | collective-permute-done | bytes 184352 | tf_op jit(solution)/shard_map/ppermute | solution.py:206
  60.0 0.1 add_convert_fusion
  60.1 0.1 constant_dynamic-slice_fusion.1
  60.2 0.1 collective-permute-start.15
  60.3 1.3 %collective-permute-done.15 = bf16[64,720]{1,0:T(8,128)(2,1)S(1)} collective-permute-done((bf16[64,720]{1,0:T(8,128)(2,1)S(1)}, bf16[64,720]{1,0:T(8,128)(2,1)S(1)}, u32[]{:S(2)}, u32[]{:S(2)}) %collective-permute-start.15) | collective-permute-done | bytes 92192 | tf_op jit(solution)/shard_map/ppermute | solution.py:213
  61.6 0.8 %copy.15 = bf16[128,720]{0,1:T(8,128)(2,1)} copy(bf16[128,720]{1,0:T(8,128)(2,1)S(1)} %maximum_select_fusion) | data formatting | bytes 368640 | tf_op jit(solution)/shard_map/jit(_where)/select_n | solution.py:244
  (5 shorter events, 0.1 us)
Async XLA Ops:
  3.8 28.7 %collective-permute-start.7 = (bf16[3,1440,720]{2,1,0:T(8,128)(2,1)S(1)}, bf16[3,1440,720]{2,1,0:T(8,128)(2,1)S(1)}, u32[]{:S(2)}, u32[]{:S(2)}) collective-permute-start(bf16[3,1440,720]{2,1,0:T(8,128)(2,1)S(1)} %get-tuple-element.28.refs_4_), channel_id=1, source_target_pairs={{0,1},{1,0},{2,3},{3,2},{4,5},{5,4},{6,7},{7,6},{8,9},{9,8},{10,11... | collective-permute-start | bytes 18662408 | tf_op jit(solution)/shard_map/ppermute | solution.py:213
  4.3 10.5 %collective-permute-start = (bf16[64,1456]{1,0:T(8,128)(2,1)S(1)}, bf16[64,1456]{1,0:T(8,128)(2,1)S(1)}, u32[]{:S(2)}, u32[]{:S(2)}) collective-permute-start(bf16[64,1456]{1,0:T(8,128)(2,1)S(1)} %get-tuple-element.23.refs_0_), channel_id=1, source_target_pairs={{0,12},{4,8},{8,4},{12,0},{1,13},{5,9},{9,5},{13,1},{2,14},{6,10},... | collective-permute-start | bytes 559112 | tf_op jit(solution)/shard_map/ppermute | solution.py:206
  9.0 9.8 %collective-permute-start.1 = (bf16[64,1456]{1,0:T(8,128)(2,1)S(1)}, bf16[64,1456]{1,0:T(8,128)(2,1)S(1)}, u32[]{:S(2)}, u32[]{:S(2)}) collective-permute-start(bf16[64,1456]{1,0:T(8,128)(2,1)S(1)} %get-tuple-element.23.refs_0_), channel_id=1, source_target_pairs={{0,4},{4,0},{8,12},{12,8},{1,5},{5,1},{9,13},{13,9},{2,6},{6,2},{1... | collective-permute-start | bytes 559112 | tf_op jit(solution)/shard_map/ppermute | solution.py:206
  9.0 9.8 %collective-permute-start.2 = (bf16[64,1456]{1,0:T(8,128)(2,1)S(1)}, bf16[64,1456]{1,0:T(8,128)(2,1)S(1)}, u32[]{:S(2)}, u32[]{:S(2)}) collective-permute-start(bf16[64,1456]{1,0:T(8,128)(2,1)S(1)} %get-tuple-element.23.refs_0_), channel_id=1, source_target_pairs={{0,2},{2,0},{1,3},{3,1},{4,6},{6,4},{5,7},{7,5},{8,10},{10,8},{9,1... | collective-permute-start | bytes 559112 | tf_op jit(solution)/shard_map/ppermute | solution.py:213
  18.8 6.9 %collective-permute-start.3 = (bf16[64,1456]{1,0:T(8,128)(2,1)S(1)}, bf16[64,1456]{1,0:T(8,128)(2,1)S(1)}, u32[]{:S(2)}, u32[]{:S(2)}) collective-permute-start(bf16[64,1456]{1,0:T(8,128)(2,1)S(1)} %get-tuple-element.26.refs_4_), channel_id=1, source_target_pairs={{0,2},{2,0},{1,3},{3,1},{4,6},{6,4},{5,7},{7,5},{8,10},{10,8},{9,1... | collective-permute-start | bytes 559112 | tf_op jit(solution)/shard_map/ppermute | solution.py:213
  20.3 7.8 %collective-permute-start.4 = (bf16[64,1456]{1,0:T(8,128)(2,1)S(1)}, bf16[64,1456]{1,0:T(8,128)(2,1)S(1)}, u32[]{:S(2)}, u32[]{:S(2)}) collective-permute-start(bf16[64,1456]{1,0:T(8,128)(2,1)S(1)} %get-tuple-element.26.refs_4_), channel_id=1, source_target_pairs={{0,4},{4,0},{8,12},{12,8},{1,5},{5,1},{9,13},{13,9},{2,6},{6,2},{1... | collective-permute-start | bytes 559112 | tf_op jit(solution)/shard_map/ppermute | solution.py:206
  22.0 9.0 %collective-permute-start.5 = (bf16[64,1456]{1,0:T(8,128)(2,1)S(1)}, bf16[64,1456]{1,0:T(8,128)(2,1)S(1)}, u32[]{:S(2)}, u32[]{:S(2)}) collective-permute-start(bf16[64,1456]{1,0:T(8,128)(2,1)S(1)} %get-tuple-element.26.refs_4_), channel_id=1, source_target_pairs={{0,6},{2,4},{4,2},{6,0},{8,14},{10,12},{12,10},{14,8},{1,7},{3,5},... | collective-permute-start | bytes 559112 | tf_op jit(solution)/shard_map/ppermute | solution.py:210
  31.1 9.8 %collective-permute-start.6 = (bf16[64,1456]{1,0:T(8,128)(2,1)S(1)}, bf16[64,1456]{1,0:T(8,128)(2,1)S(1)}, u32[]{:S(2)}, u32[]{:S(2)}) collective-permute-start(bf16[64,1456]{1,0:T(8,128)(2,1)S(1)} %get-tuple-element.27.refs_2_), channel_id=1, source_target_pairs={{0,2},{2,0},{1,3},{3,1},{4,6},{6,4},{5,7},{7,5},{8,10},{10,8},{9,1... | collective-permute-start | bytes 559112 | tf_op jit(solution)/shard_map/ppermute | solution.py:213
  37.2 10.4 %collective-permute-start.13 = (bf16[64,1440]{1,0:T(8,128)(2,1)S(1)}, bf16[64,1440]{1,0:T(8,128)(2,1)S(1)}, u32[]{:S(2)}, u32[]{:S(2)}) collective-permute-start(bf16[64,1440]{1,0:T(8,128)(2,1)S(1)} %get-tuple-element.40), channel_id=1, source_target_pairs={{0,6},{2,4},{4,2},{6,0},{8,14},{10,12},{12,10},{14,8},{1,7},{3,5},... | collective-permute-start | bytes 552968 | tf_op jit(solution)/shard_map/ppermute | solution.py:210
  38.6 9.0 %collective-permute-start.12 = (bf16[64,1440]{1,0:T(8,128)(2,1)S(1)}, bf16[64,1440]{1,0:T(8,128)(2,1)S(1)}, u32[]{:S(2)}, u32[]{:S(2)}) collective-permute-start(bf16[64,1440]{1,0:T(8,128)(2,1)S(1)} %convert_element_type.38), channel_id=1, source_target_pairs={{0,4},{4,0},{8,12},{12,8},{1,5},{5,1},{9,13},{13,9},{2,6},{6,2},{1... | collective-permute-start | bytes 552968 | tf_op jit(solution)/shard_map/ppermute | solution.py:206
  39.3 9.4 %collective-permute-start.11 = (bf16[64,1440]{1,0:T(8,128)(2,1)S(1)}, bf16[64,1440]{1,0:T(8,128)(2,1)S(1)}, u32[]{:S(2)}, u32[]{:S(2)}) collective-permute-start(bf16[64,1440]{1,0:T(8,128)(2,1)S(1)} %get-tuple-element.38), channel_id=1, source_target_pairs={{0,2},{2,0},{1,3},{3,1},{4,6},{6,4},{5,7},{7,5},{8,10},{10,8},{9,1... | collective-permute-start | bytes 552968 | tf_op jit(solution)/shard_map/ppermute | solution.py:213
  45.5 7.9 %collective-permute-start.9 = (bf16[64,1440]{1,0:T(8,128)(2,1)S(1)}, bf16[64,1440]{1,0:T(8,128)(2,1)S(1)}, u32[]{:S(2)}, u32[]{:S(2)}) collective-permute-start(bf16[64,1440]{1,0:T(8,128)(2,1)S(1)} %get-tuple-element.32), channel_id=1, source_target_pairs={{0,2},{2,0},{1,3},{3,1},{4,6},{6,4},{5,7},{7,5},{8,10},{10,8},{9,1... | collective-permute-start | bytes 552968 | tf_op jit(solution)/shard_map/ppermute | solution.py:213
  46.1 10.1 %collective-permute-start.8 = (bf16[64,1440]{1,0:T(8,128)(2,1)S(1)}, bf16[64,1440]{1,0:T(8,128)(2,1)S(1)}, u32[]{:S(2)}, u32[]{:S(2)}) collective-permute-start(bf16[64,1440]{1,0:T(8,128)(2,1)S(1)} %get-tuple-element.30), channel_id=1, source_target_pairs={{0,2},{2,0},{1,3},{3,1},{4,6},{6,4},{5,7},{7,5},{8,10},{10,8},{9,1... | collective-permute-start | bytes 552968 | tf_op jit(solution)/shard_map/ppermute | solution.py:213
  48.8 9.2 %collective-permute-start.14 = (bf16[64,1440]{1,0:T(8,128)(2,1)S(1)}, bf16[64,1440]{1,0:T(8,128)(2,1)S(1)}, u32[]{:S(2)}, u32[]{:S(2)}) collective-permute-start(bf16[64,1440]{1,0:T(8,128)(2,1)S(1)} %add_convert_fusion.1), channel_id=1, source_target_pairs={{0,12},{4,8},{8,4},{12,0},{1,13},{5,9},{9,5},{13,1},{2,14},{6,10},... | collective-permute-start | bytes 552968 | tf_op jit(solution)/shard_map/ppermute | solution.py:206
  53.4 6.6 %collective-permute-start.10 = (bf16[64,1440]{1,0:T(8,128)(2,1)S(1)}, bf16[64,1440]{1,0:T(8,128)(2,1)S(1)}, u32[]{:S(2)}, u32[]{:S(2)}) collective-permute-start(bf16[64,1440]{1,0:T(8,128)(2,1)S(1)} %add_convert_fusion.2), channel_id=1, source_target_pairs={{0,4},{4,0},{8,12},{12,8},{1,5},{5,1},{9,13},{13,9},{2,6},{6,2},{1... | collective-permute-start | bytes 552968 | tf_op jit(solution)/shard_map/ppermute | solution.py:206
  60.2 1.4 %collective-permute-start.15 = (bf16[64,720]{1,0:T(8,128)(2,1)S(1)}, bf16[64,720]{1,0:T(8,128)(2,1)S(1)}, u32[]{:S(2)}, u32[]{:S(2)}) collective-permute-start(bf16[64,720]{1,0:T(8,128)(2,1)S(1)} %get-tuple-element.42), channel_id=1, source_target_pairs={{0,1},{1,0},{2,3},{3,2},{4,5},{5,4},{6,7},{7,6},{8,9},{9,8},{10,11... | collective-permute-start | bytes 276488 | tf_op jit(solution)/shard_map/ppermute | solution.py:213

commit v3 on v2

--- a/solution.py
+++ b/solution.py
@@ -73,8 +73,8 @@
 
 
 def expert_kernel(expert_count, count, place_ref, *refs):
-    ins, weights = refs[:count], refs[count : count + 2]
-    outs, rows = refs[count + 2 : -1], refs[-1]
+    ins, weights = refs[:count], refs[count : count + 6]
+    outs, rows = refs[count + 6 : -1], refs[-1]
     model_width = outs[0].shape[1]
     first = 0
     for ref in ins:
@@ -85,7 +85,7 @@
     x = rows[:, :model_width]
     total = None
     for i in range(2):
-        wg, wu, wd = (weights[i].at[j] for j in range(3))
+        wg, wu, wd = weights[3 * i : 3 * i + 3]
         expert = place_ref[i]
         scale = jnp.where(lane == expert, 256.0, jnp.where(lane == expert + expert_count, 1.0, 0.0))
         weight = jnp.sum(tail * scale, axis=1, keepdims=True) * (1.0 / 65536.0)
@@ -103,7 +103,7 @@
 
 def experts(expert_count, place, model_width, blocks, weights):
     half_rows, width = blocks[0].shape
-    slice_width = weights[0].shape[2]
+    slice_width = weights[0].shape[1]
     vmem = pl.BlockSpec(memory_space=pltpu.VMEM)
     count = len(blocks)
     rows = count * half_rows
@@ -113,7 +113,7 @@
             jax.ShapeDtypeStruct((half_rows, model_width), (jnp.float32, jnp.bfloat16)[i % 2])
             for i in range(count)
         ),
-        in_specs=[pl.BlockSpec(memory_space=pltpu.SMEM)] + [vmem] * (count + 2),
+        in_specs=[pl.BlockSpec(memory_space=pltpu.SMEM)] + [vmem] * (count + 6),
         out_specs=tuple([vmem] * count),
         scratch_shapes=[pltpu.VMEM((rows, width), jnp.bfloat16)],
         compiler_params=pltpu.CompilerParams(vmem_limit_bytes=20 * 1024 * 1024),
@@ -126,9 +126,8 @@
 
 
 def prepare_kernel(place_ref, *refs):
-    own, held, hidden, ids, units, rows, sems = refs[6:]
-    targets = (hidden, ids, units, *(held.at[i] for i in range(3)))
-    copies = [pltpu.make_async_copy(refs[i], to, sems.at[i]) for i, to in enumerate(targets)]
+    own, hidden, ids, units, rows, sems = refs[3:]
+    copies = [pltpu.make_async_copy(refs[i], refs[i + 4], sems.at[i]) for i in range(3)]
     for copy in copies:
         copy.start()
     model_width, token_count = hidden.shape
@@ -145,37 +144,44 @@
     copies[0].wait()
     rows[:, :model_width] = hidden[...].T
     own[...] = rows[pl.ds(pl.multiple_of(place_ref[2] * half_rows, half_rows), half_rows), :]
-    for copy in copies[3:]:
-        copy.wait()
-
-
-def prepare(place, expert_count, hidden, expert_ids, gate_units, weights):
+
+
+def prepare(place, expert_count, hidden, expert_ids, gate_units):
     token_count, model_width = hidden.shape
     width = model_width + 2 * expert_count
-    vmem = pl.BlockSpec(memory_space=pltpu.VMEM)
+    arrays = hidden.T, expert_ids.T, gate_units.T
     return pl.pallas_call(
         prepare_kernel,
-        out_shape=(
-            jax.ShapeDtypeStruct((token_count // 2, width), hidden.dtype),
-            jax.ShapeDtypeStruct((len(weights), *weights[0].shape), weights[0].dtype),
-        ),
-        in_specs=[pl.BlockSpec(memory_space=pltpu.SMEM)] + [pl.BlockSpec(memory_space=pl.ANY)] * 6,
-        out_specs=(vmem, vmem),
-        scratch_shapes=[
-            pltpu.VMEM((model_width, token_count), hidden.dtype),
-            pltpu.VMEM(expert_ids.T.shape, jnp.int32),
-            pltpu.VMEM(gate_units.T.shape, jnp.int32),
-            pltpu.VMEM((token_count, width), hidden.dtype),
-            pltpu.SemaphoreType.DMA((6,)),
-        ],
-        compiler_params=pltpu.CompilerParams(vmem_limit_bytes=16 * 1024 * 1024),
-    )(
-        place,
-        *[
-            pltpu.with_memory_space_constraint(x, pltpu.HBM)
-            for x in (hidden.T, expert_ids.T, gate_units.T, *weights)
-        ],
-    )
+        out_shape=jax.ShapeDtypeStruct((token_count // 2, width), hidden.dtype),
+        in_specs=[pl.BlockSpec(memory_space=pltpu.SMEM)] + [pl.BlockSpec(memory_space=pl.ANY)] * 3,
+        out_specs=pl.BlockSpec(memory_space=pltpu.VMEM),
+        scratch_shapes=[pltpu.VMEM(x.shape, x.dtype) for x in arrays]
+        + [pltpu.VMEM((token_count, width), hidden.dtype), pltpu.SemaphoreType.DMA((3,))],
+        compiler_params=pltpu.CompilerParams(vmem_limit_bytes=8 * 1024 * 1024),
+    )(place, *[pltpu.with_memory_space_constraint(x, pltpu.HBM) for x in arrays])
+
+
+def stage_kernel(count, *refs):
+    ins, outs, sems = refs[:count], refs[-count - 1 : -1], refs[-1]
+    copies = [pltpu.make_async_copy(ins[i], outs[i], sems.at[i]) for i in range(count)]
+    for copy in copies:
+        copy.start()
+    for copy in copies:
+        copy.wait()
+
+
+def stage(after, *arrays):
+    return pl.pallas_call(
+        functools.partial(stage_kernel, len(arrays)),
+        out_shape=tuple(jax.ShapeDtypeStruct(x.shape, x.dtype) for x in arrays),
+        in_specs=[pl.BlockSpec(memory_space=pl.ANY)] * (len(arrays) + 1),
+        out_specs=tuple([pl.BlockSpec(memory_space=pltpu.VMEM)] * len(arrays)),
+        scratch_shapes=[pltpu.SemaphoreType.DMA((len(arrays),))],
+        compiler_params=pltpu.CompilerParams(vmem_limit_bytes=8 * 1024 * 1024),
+        cost_estimate=pl.CostEstimate(
+            flops=0, bytes_accessed=2 * sum(x.size for x in arrays), transcendentals=0
+        ),
+    )(*[pltpu.with_memory_space_constraint(x, pltpu.HBM) for x in arrays], after)
 
 
 def hold_kernel(*refs):
@@ -212,16 +218,25 @@
     def swap(x, axis):
         return lax.ppermute(x, axis, [(0, 1), (1, 0)])
 
-    own, mine = prepare(
-        place, expert_count, hidden, expert_ids, gate_units, (w_gate[0], w_up[0], w_down[0])
-    )
+    own = prepare(place, expert_count, hidden, expert_ids, gate_units)
     run = functools.partial(experts, expert_count, place, model_width)
-    weights = (mine, swap(mine, "tp"))
-    near3, near1, far0 = hold(z(own, 3), z(own, 1), swap(own, "ep"))
-    far3, near2, far2 = swap(near3, "ep"), z(near3, 1), diagonal(near3)
-    near1, far3, near2, far2, near3 = hold(near1, far3, near2, far2, near3)
-    far1 = swap(near1, "ep")
-    near_sum3, far_sum3, near_sum2, far_sum2 = run([near3, far3, near2, far2], weights)
+    gate2, up2 = swap(w_gate[0], "tp"), swap(w_up[0], "tp")
+    near3, near1, far0, down1, gate1, up1 = hold(
+        z(own, 3),
+        z(own, 1),
+        swap(own, "ep"),
+        *stage(own, w_down[0]),
+        *stage(own, w_gate[0], w_up[0]),
+    )
+    held3, gate2, up2 = hold(near3, gate2, up2)
+    far3, near2, far2 = swap(near3, "ep"), z(near3, 1), diagonal(held3)
+    down2 = swap(down1, "tp")
+    weights = gate1, up1, down1, gate2, up2, down2
+    near_sum3, far_sum3 = run([near3, far3], weights)
+    far_sum3, near1 = hold(far_sum3, near1)
+    near2, far2, near_sum3 = hold(near2, far2, near_sum3)
+    near_sum2, far_sum2 = run([near2, far2], weights)
+    back3, far1, own = hold(swap(far_sum3, "ep"), swap(near1, "ep"), own)
     near_sum0, far_sum0, near_sum1, far_sum1 = run([own, far0, near1, far1], weights)
 
     def f32(x):
@@ -230,11 +245,12 @@
     def bf16(x):
         return x.astype(jnp.bfloat16)
 
-    merged = near_sum3 + f32(swap(far_sum3, "ep")) + f32(z(bf16(near_sum2), 1)) + f32(diagonal(far_sum2))
+    merged = near_sum3 + f32(back3) + f32(z(bf16(near_sum2), 1)) + f32(diagonal(far_sum2))
+    back1, far_sum0 = hold(swap(far_sum1, "ep"), far_sum0)
     total = (
         near_sum0
         + f32(swap(far_sum0, "ep"))
-        + f32(z(bf16(near_sum1 + f32(swap(far_sum1, "ep"))), 1))
+        + f32(z(bf16(near_sum1 + f32(back1)), 1))
         + f32(z(bf16(merged), 3))
     )
     out = total.astype(jnp.bfloat16)

time: 62.6 us -> 58.6 us (0.936)
  waiting for transfers between devices: 28.1 us -> 15.9 us
  starting transfers between devices: 20 us -> 24.1 us
  Pallas kernels: 13 us -> 17 us
    ppermute x6, waiting for transfers between devices: 14.5 us -> 6.27 us  [z(): lax.ppermute(x, 'seq', [(i, i ^ k) for i in range(lax.axis_size('seq'))])]
    ppermute x2, waiting for transfers between devices: 2.95 us -> 0.02 us  [diagonal(): return lax.ppermute(x, ('seq', 'ep'), flat)]
    ppermute x6, starting transfers between devices: 9.68 us -> 12.2 us  [z(): lax.ppermute(x, 'seq', [(i, i ^ k) for i in range(lax.axis_size('seq'))])]
    pallas_call x2 -> x3, Pallas kernels: 9.25 us -> 11.3 us  [experts(): pl.pallas_call(functools.partial(expert_kernel, expert_count, count), out...]
    pallas_call x1 -> x3, Pallas kernels: 3.72 us -> 5.71 us  [the longest x2 3.94 us: stage(): pl.pallas_call(functools.partial(stage_kernel, len(arrays)), out_shape=tu...]
    ppermute x8 -> x10, starting transfers between devices: 8.65 us -> 10.3 us  [swap(): return lax.ppermute(x, axis, [(0, 1), (1, 0)])]
    ppermute x8 -> x10, waiting for transfers between devices: 10.6 us -> 9.57 us  [swap(): return lax.ppermute(x, axis, [(0, 1), (1, 0)])]
  transfers between devices with their start and end apart: 16 -> 18, of which waited for: 11 -> 8; matrix products, arithmetic and copies ran while one was open for 0% -> 0% of each run, Pallas kernels for 15% -> 26%
where the time goes in v3:
time: 58.6 us; the launch traced here: 58.4 us
  starting transfers between devices  24.1 us (41%)
  Pallas kernels  17 us (29%)
  waiting for transfers between devices  15.9 us (27%)
  local copies, waits for them, and re-layouts  0.96 us (2%)
    ppermute x6, starting transfers between devices, z(): lax.ppermute(x, 'seq', [(i, i ^ k) for i in range(lax.axis_size('seq'))])  12.2 us
    pallas_call x3, Pallas kernels, experts(): pl.pallas_call(functools.partial(expert_kernel, expert_count, count), out...  11.3 us
    ppermute x10, starting transfers between devices, swap(): return lax.ppermute(x, axis, [(0, 1), (1, 0)])  10.3 us
    ppermute x10, waiting for transfers between devices, swap(): return lax.ppermute(x, axis, [(0, 1), (1, 0)])  9.57 us
    ppermute x6, waiting for transfers between devices, z(): lax.ppermute(x, 'seq', [(i, i ^ k) for i in range(lax.axis_size('seq'))])  6.27 us
    pallas_call x2, Pallas kernels, stage(): pl.pallas_call(functools.partial(stage_kernel, len(arrays)), out_shape=tu...  3.94 us
    pallas_call x1, Pallas kernels, prepare(): pl.pallas_call(prepare_kernel, out_shape=jax.ShapeDtypeStruct((token_coun...  1.77 us
    ppermute x2, starting transfers between devices, diagonal(): return lax.ppermute(x, ('seq', 'ep'), flat)  1.58 us
  transfers between devices with their start and end apart: 18, of which 8 were waited for; matrix products, arithmetic and copies ran while one was open for 0% of the time, Pallas kernels for 26%

profile of v3, /device:TPU:0, one launch (start us, length us, event | category | flops | bytes accessed | tf_op | source)
XLA Modules:
  0.0 58.4 jit_solution(12281744799609216722)
XLA Ops:
  0.0 0.1 pad_add_fusion.place_ref
  0.1 1.8 %shard_map.64.refs_1_.refs_2_ = bf16[64,1456]{1,0:T(8,128)(2,1)S(1)} custom-call(s32[3]{0:T(128)S(1)} %pad_add_fusion.place_ref, bf16[1440,128]{1,0:T(8,128)(2,1)} %bitcast.14, s32[4,128]{1,0:T(4,128)} %bitcast.15, s32[4,128]{1,0:T(4,128)} %bitcast.16), custom_call_target="tpu_custom_call" | custom-call | tf_op jit(solution)/shard_map/pallas_call | solution.py:153
  1.9 5.1 %collective-permute-start = (bf16[64,1456]{1,0:T(8,128)(2,1)S(1)}, bf16[64,1456]{1,0:T(8,128)(2,1)S(1)}, u32[]{:S(2)}, u32[]{:S(2)}) collective-permute-start(bf16[64,1456]{1,0:T(8,128)(2,1)S(1)} %shard_map.64.refs_1_.refs_2_), channel_id=1, source_target_pairs={{0,12},{4,8},{8,4},{12,0},{1,13},{5,9},{9,5},{13,1},{2,14},{6,10},... | collective-permute-start | bytes 559112 | tf_op jit(solution)/shard_map/ppermute | solution.py:212
  7.0 0.0 collective-permute-start.1
  7.0 1.5 %collective-permute-start.2 = (bf16[64,1456]{1,0:T(8,128)(2,1)S(1)}, bf16[64,1456]{1,0:T(8,128)(2,1)S(1)}, u32[]{:S(2)}, u32[]{:S(2)}) collective-permute-start(bf16[64,1456]{1,0:T(8,128)(2,1)S(1)} %shard_map.64.refs_1_.refs_2_), channel_id=1, source_target_pairs={{0,2},{2,0},{1,3},{3,1},{4,6},{6,4},{5,7},{7,5},{8,10},{10,8},{9,1... | collective-permute-start | bytes 559112 | tf_op jit(solution)/shard_map/ppermute | solution.py:219
  8.5 0.0 collective-permute-start.4
  8.5 0.5 collective-permute-start.5
  9.0 2.3 %shard_map.66 = (bf16[1440,720]{1,0:T(8,128)(2,1)S(1)}, bf16[1440,720]{1,0:T(8,128)(2,1)S(1)}) custom-call(bf16[1440,720]{1,0:T(8,128)(2,1)} %bitcast.11, bf16[1440,720]{1,0:T(8,128)(2,1)} %bitcast.13, bf16[64,1456]{1,0:T(8,128)(2,1)S(1)} %shard_map.64.refs_1_.refs_2_), custom_call_target="tpu_custom_call" | custom-call | bytes 4147200 | tf_op jit(solution)/shard_map/pallas_call | solution.py:174
  11.3 1.6 %shard_map.65.refs_3_ = bf16[1440,720]{1,0:T(8,128)(2,1)S(1)} custom-call(bf16[1440,720]{1,0:T(8,128)(2,1)} %bitcast.9, bf16[64,1456]{1,0:T(8,128)(2,1)S(1)} %shard_map.64.refs_1_.refs_2_), custom_call_target="tpu_custom_call" | custom-call | bytes 2073600 | tf_op jit(solution)/shard_map/pallas_call | solution.py:174
  12.9 0.0 collective-permute-done.refs_0_
  12.9 3.2 %collective-permute-done.1.refs_1_ = bf16[64,1456]{1,0:T(8,128)(2,1)S(1)} collective-permute-done((bf16[64,1456]{1,0:T(8,128)(2,1)S(1)}, bf16[64,1456]{1,0:T(8,128)(2,1)S(1)}, u32[]{:S(2)}, u32[]{:S(2)}) %collective-permute-start.1) | collective-permute-done | bytes 186400 | tf_op jit(solution)/shard_map/ppermute | solution.py:212
  16.2 0.0 collective-permute-done.2.refs_2_
  16.2 0.0 collective-permute-start.6
  16.2 1.5 %collective-permute-start.3 = (bf16[64,1456]{1,0:T(8,128)(2,1)S(1)}, bf16[64,1456]{1,0:T(8,128)(2,1)S(1)}, u32[]{:S(2)}, u32[]{:S(2)}) collective-permute-start(bf16[64,1456]{1,0:T(8,128)(2,1)S(1)} %get-tuple-element.36.refs_0_), channel_id=1, source_target_pairs={{0,2},{2,0},{1,3},{3,1},{4,6},{6,4},{5,7},{7,5},{8,10},{10,8},{9,1... | collective-permute-start | bytes 559112 | tf_op jit(solution)/shard_map/ppermute | solution.py:219
  17.8 1.8 %collective-permute-start.12 = (bf16[64,1456]{1,0:T(8,128)(2,1)S(1)}, bf16[64,1456]{1,0:T(8,128)(2,1)S(1)}, u32[]{:S(2)}, u32[]{:S(2)}) collective-permute-start(bf16[64,1456]{1,0:T(8,128)(2,1)S(1)} %get-tuple-element.36.refs_0_), channel_id=1, source_target_pairs={{0,4},{4,0},{8,12},{12,8},{1,5},{5,1},{9,13},{13,9},{2,6},{6,2},{1... | collective-permute-start | bytes 559112 | tf_op jit(solution)/shard_map/ppermute | solution.py:212
  19.5 0.0 collective-permute-done.4.refs_1_
  19.5 0.0 collective-permute-done.5.refs_2_
  19.5 0.3 collective-permute-start.13
  19.8 3.7 %collective-permute-done.3.refs_1_ = bf16[64,1456]{1,0:T(8,128)(2,1)S(1)} collective-permute-done((bf16[64,1456]{1,0:T(8,128)(2,1)S(1)}, bf16[64,1456]{1,0:T(8,128)(2,1)S(1)}, u32[]{:S(2)}, u32[]{:S(2)}) %collective-permute-start.3) | collective-permute-done | bytes 186400 | tf_op jit(solution)/shard_map/ppermute | solution.py:219
  23.5 0.0 collective-permute-done.6.refs_7_.refs_9_
  23.5 3.3 %shard_map.69 = (f32[64,1440]{1,0:T(8,128)S(1)}, bf16[64,1440]{1,0:T(8,128)(2,1)S(1)}) custom-call(s32[3]{0:T(128)S(1)} %pad_add_fusion.place_ref, bf16[64,1456]{1,0:T(8,128)(2,1)S(1)} %get-tuple-element.36.refs_0_, bf16[64,1456]{1,0:T(8,128)(2,1)S(1)} %collective-permute-done.3.refs_1_, bf16[1440,720]{1,0:T(8,128)(2,1)S(1)} %get-tuple-element.37.refs_2_.refs_4_, ...), custom_call_target="tpu_custom_call" | custom-call | flops 1592524800 | bytes 745472 | tf_op jit(solution)/shard_map/pallas_call | solution.py:110
  26.9 1.6 %collective-permute-start.8 = (bf16[64,1456]{1,0:T(8,128)(2,1)S(1)}, bf16[64,1456]{1,0:T(8,128)(2,1)S(1)}, u32[]{:S(2)}, u32[]{:S(2)}) collective-permute-start(bf16[64,1456]{1,0:T(8,128)(2,1)S(1)} %get-tuple-element.45.refs_2_), channel_id=1, source_target_pairs={{0,2},{2,0},{1,3},{3,1},{4,6},{6,4},{5,7},{7,5},{8,10},{10,8},{9,1... | collective-permute-start | bytes 559112 | tf_op jit(solution)/shard_map/ppermute | solution.py:219
  28.4 0.5 collective-permute-start.7
  29.0 0.0 collective-permute-done.12.refs_0_
  29.0 0.0 collective-permute-done.13.refs_1_
  29.0 3.4 %shard_map.75 = (f32[64,1440]{1,0:T(8,128)S(1)}, bf16[64,1440]{1,0:T(8,128)(2,1)S(1)}) custom-call(s32[3]{0:T(128)S(1)} %pad_add_fusion.place_ref, bf16[64,1456]{1,0:T(8,128)(2,1)S(1)} %get-tuple-element.59.refs_0_, bf16[64,1456]{1,0:T(8,128)(2,1)S(1)} %get-tuple-element.60.refs_1_, bf16[1440,720]{1,0:T(8,128)(2,1)S(1)} %get-tuple-element.37.refs_2_.refs_4_, ...), custom_call_target="tpu_custom_call" | custom-call | flops 1592524800 | bytes 745472 | tf_op jit(solution)/shard_map/pallas_call | solution.py:110
  32.4 1.8 %collective-permute-start.14 = (bf16[64,1440]{1,0:T(8,128)(2,1)S(1)}, bf16[64,1440]{1,0:T(8,128)(2,1)S(1)}, u32[]{:S(2)}, u32[]{:S(2)}) collective-permute-start(bf16[64,1440]{1,0:T(8,128)(2,1)S(1)} %convert_element_type.38), channel_id=1, source_target_pairs={{0,4},{4,0},{8,12},{12,8},{1,5},{5,1},{9,13},{13,9},{2,6},{6,2},{1... | collective-permute-start | bytes 552968 | tf_op jit(solution)/shard_map/ppermute | solution.py:212
  34.1 1.3 %collective-permute-start.15 = (bf16[64,1440]{1,0:T(8,128)(2,1)S(1)}, bf16[64,1440]{1,0:T(8,128)(2,1)S(1)}, u32[]{:S(2)}, u32[]{:S(2)}) collective-permute-start(bf16[64,1440]{1,0:T(8,128)(2,1)S(1)} %get-tuple-element.62), channel_id=1, source_target_pairs={{0,6},{2,4},{4,2},{6,0},{8,14},{10,12},{12,10},{14,8},{1,7},{3,5},... | collective-permute-start | bytes 552968 | tf_op jit(solution)/shard_map/ppermute | solution.py:216
  35.4 2.2 %collective-permute-done.7.refs_0_ = bf16[64,1440]{1,0:T(8,128)(2,1)S(1)} collective-permute-done((bf16[64,1440]{1,0:T(8,128)(2,1)S(1)}, bf16[64,1440]{1,0:T(8,128)(2,1)S(1)}, u32[]{:S(2)}, u32[]{:S(2)}) %collective-permute-start.7) | collective-permute-done | bytes 184352 | tf_op jit(solution)/shard_map/ppermute | solution.py:219
  37.6 0.0 collective-permute-done.8.refs_1_
  37.6 4.6 %shard_map.72 = (f32[64,1440]{1,0:T(8,128)S(1)}, bf16[64,1440]{1,0:T(8,128)(2,1)S(1)}, f32[64,1440]{1,0:T(8,128)S(1)}, bf16[64,1440]{1,0:T(8,128)(2,1)S(1)}) custom-call(s32[3]{0:T(128)S(1)} %pad_add_fusion.place_ref, bf16[64,1456]{1,0:T(8,128)(2,1)S(1)} %get-tuple-element.46.refs_0_, bf16[64,1456]{1,0:T(8,128)(2,1)S(1)} %get-tuple-element.47.refs_1_, ...), custom_call_target="tpu_custom_call" | custom-call | flops 3185049600 | bytes 1490944 | tf_op jit(solution)/shard_map/pallas_call | solution.py:110
  42.3 2.3 %collective-permute-start.9 = (bf16[64,1440]{1,0:T(8,128)(2,1)S(1)}, bf16[64,1440]{1,0:T(8,128)(2,1)S(1)}, u32[]{:S(2)}, u32[]{:S(2)}) collective-permute-start(bf16[64,1440]{1,0:T(8,128)(2,1)S(1)} %get-tuple-element.50), channel_id=1, source_target_pairs={{0,2},{2,0},{1,3},{3,1},{4,6},{6,4},{5,7},{7,5},{8,10},{10,8},{9,1... | collective-permute-start | bytes 552968 | tf_op jit(solution)/shard_map/ppermute | solution.py:219
  44.6 0.0 collective-permute-done.14
  44.6 0.0 collective-permute-done.15
  44.6 0.1 add_convert_fusion.1
  44.7 1.8 %collective-permute-start.16 = (bf16[64,1440]{1,0:T(8,128)(2,1)S(1)}, bf16[64,1440]{1,0:T(8,128)(2,1)S(1)}, u32[]{:S(2)}, u32[]{:S(2)}) collective-permute-start(bf16[64,1440]{1,0:T(8,128)(2,1)S(1)} %add_convert_fusion.1), channel_id=1, source_target_pairs={{0,12},{4,8},{8,4},{12,0},{1,13},{5,9},{9,5},{13,1},{2,14},{6,10},... | collective-permute-start | bytes 552968 | tf_op jit(solution)/shard_map/ppermute | solution.py:212
  46.5 1.7 %collective-permute-done.9.refs_0_ = bf16[64,1440]{1,0:T(8,128)(2,1)S(1)} collective-permute-done((bf16[64,1440]{1,0:T(8,128)(2,1)S(1)}, bf16[64,1440]{1,0:T(8,128)(2,1)S(1)}, u32[]{:S(2)}, u32[]{:S(2)}) %collective-permute-start.9) | collective-permute-done | bytes 184352 | tf_op jit(solution)/shard_map/ppermute | solution.py:219
  48.3 1.8 %collective-permute-start.11 = (bf16[64,1440]{1,0:T(8,128)(2,1)S(1)}, bf16[64,1440]{1,0:T(8,128)(2,1)S(1)}, u32[]{:S(2)}, u32[]{:S(2)}) collective-permute-start(bf16[64,1440]{1,0:T(8,128)(2,1)S(1)} %add_convert_fusion.2), channel_id=1, source_target_pairs={{0,4},{4,0},{8,12},{12,8},{1,5},{5,1},{9,13},{13,9},{2,6},{6,2},{1... | collective-permute-start | bytes 552968 | tf_op jit(solution)/shard_map/ppermute | solution.py:212
  50.0 2.3 %collective-permute-start.10 = (bf16[64,1440]{1,0:T(8,128)(2,1)S(1)}, bf16[64,1440]{1,0:T(8,128)(2,1)S(1)}, u32[]{:S(2)}, u32[]{:S(2)}) collective-permute-start(bf16[64,1440]{1,0:T(8,128)(2,1)S(1)} %get-tuple-element.52), channel_id=1, source_target_pairs={{0,2},{2,0},{1,3},{3,1},{4,6},{6,4},{5,7},{7,5},{8,10},{10,8},{9,1... | collective-permute-start | bytes 552968 | tf_op jit(solution)/shard_map/ppermute | solution.py:219
  52.3 1.0 %collective-permute-done.16 = bf16[64,1440]{1,0:T(8,128)(2,1)S(1)} collective-permute-done((bf16[64,1440]{1,0:T(8,128)(2,1)S(1)}, bf16[64,1440]{1,0:T(8,128)(2,1)S(1)}, u32[]{:S(2)}, u32[]{:S(2)}) %collective-permute-start.16) | collective-permute-done | bytes 184352 | tf_op jit(solution)/shard_map/ppermute | solution.py:212
  53.4 2.0 %collective-permute-done.11 = bf16[64,1440]{1,0:T(8,128)(2,1)S(1)} collective-permute-done((bf16[64,1440]{1,0:T(8,128)(2,1)S(1)}, bf16[64,1440]{1,0:T(8,128)(2,1)S(1)}, u32[]{:S(2)}, u32[]{:S(2)}) %collective-permute-start.11) | collective-permute-done | bytes 184352 | tf_op jit(solution)/shard_map/ppermute | solution.py:212
  55.4 0.6 %collective-permute-done.10 = bf16[64,1440]{1,0:T(8,128)(2,1)S(1)} collective-permute-done((bf16[64,1440]{1,0:T(8,128)(2,1)S(1)}, bf16[64,1440]{1,0:T(8,128)(2,1)S(1)}, u32[]{:S(2)}, u32[]{:S(2)}) %collective-permute-start.10) | collective-permute-done | bytes 184352 | tf_op jit(solution)/shard_map/ppermute | solution.py:219
  56.0 0.1 add_convert_fusion
  56.1 0.1 constant_dynamic-slice_fusion.1
  56.2 0.1 collective-permute-start.17
  56.3 1.3 %collective-permute-done.17 = bf16[64,720]{1,0:T(8,128)(2,1)S(1)} collective-permute-done((bf16[64,720]{1,0:T(8,128)(2,1)S(1)}, bf16[64,720]{1,0:T(8,128)(2,1)S(1)}, u32[]{:S(2)}, u32[]{:S(2)}) %collective-permute-start.17) | collective-permute-done | bytes 92192 | tf_op jit(solution)/shard_map/ppermute | solution.py:219
  57.6 0.8 %copy.26 = bf16[128,720]{0,1:T(8,128)(2,1)} copy(bf16[128,720]{1,0:T(8,128)(2,1)S(1)} %maximum_select_fusion) | data formatting | bytes 368640 | tf_op jit(solution)/shard_map/jit(_where)/select_n | solution.py:260
  (10 shorter events, 0.1 us)
Async XLA Ops:
  1.9 11.1 %collective-permute-start = (bf16[64,1456]{1,0:T(8,128)(2,1)S(1)}, bf16[64,1456]{1,0:T(8,128)(2,1)S(1)}, u32[]{:S(2)}, u32[]{:S(2)}) collective-permute-start(bf16[64,1456]{1,0:T(8,128)(2,1)S(1)} %shard_map.64.refs_1_.refs_2_), channel_id=1, source_target_pairs={{0,12},{4,8},{8,4},{12,0},{1,13},{5,9},{9,5},{13,1},{2,14},{6,10},... | collective-permute-start | bytes 559112 | tf_op jit(solution)/shard_map/ppermute | solution.py:212
  7.0 9.2 %collective-permute-start.1 = (bf16[64,1456]{1,0:T(8,128)(2,1)S(1)}, bf16[64,1456]{1,0:T(8,128)(2,1)S(1)}, u32[]{:S(2)}, u32[]{:S(2)}) collective-permute-start(bf16[64,1456]{1,0:T(8,128)(2,1)S(1)} %shard_map.64.refs_1_.refs_2_), channel_id=1, source_target_pairs={{0,4},{4,0},{8,12},{12,8},{1,5},{5,1},{9,13},{13,9},{2,6},{6,2},{1... | collective-permute-start | bytes 559112 | tf_op jit(solution)/shard_map/ppermute | solution.py:212
  7.0 9.2 %collective-permute-start.2 = (bf16[64,1456]{1,0:T(8,128)(2,1)S(1)}, bf16[64,1456]{1,0:T(8,128)(2,1)S(1)}, u32[]{:S(2)}, u32[]{:S(2)}) collective-permute-start(bf16[64,1456]{1,0:T(8,128)(2,1)S(1)} %shard_map.64.refs_1_.refs_2_), channel_id=1, source_target_pairs={{0,2},{2,0},{1,3},{3,1},{4,6},{6,4},{5,7},{7,5},{8,10},{10,8},{9,1... | collective-permute-start | bytes 559112 | tf_op jit(solution)/shard_map/ppermute | solution.py:219
  8.5 11.1 %collective-permute-start.4 = (bf16[1440,720]{1,0:T(8,128)(2,1)}, bf16[1440,720]{1,0:T(8,128)(2,1)S(1)}, u32[]{:S(2)}, u32[]{:S(2)}) collective-permute-start(bf16[1440,720]{1,0:T(8,128)(2,1)} %bitcast.10), channel_id=1, source_target_pairs={{0,1},{1,0},{2,3},{3,2},{4,5},{5,4},{6,7},{7,6},{8,9},{9,8},{10,11... | collective-permute-start | bytes 6220808 | tf_op jit(solution)/shard_map/ppermute | solution.py:219
  8.5 11.1 %collective-permute-start.5 = (bf16[1440,720]{1,0:T(8,128)(2,1)}, bf16[1440,720]{1,0:T(8,128)(2,1)S(1)}, u32[]{:S(2)}, u32[]{:S(2)}) collective-permute-start(bf16[1440,720]{1,0:T(8,128)(2,1)} %bitcast.12), channel_id=1, source_target_pairs={{0,1},{1,0},{2,3},{3,2},{4,5},{5,4},{6,7},{7,6},{8,9},{9,8},{10,11... | collective-permute-start | bytes 6220808 | tf_op jit(solution)/shard_map/ppermute | solution.py:219
  16.2 7.3 %collective-permute-start.6 = (bf16[1440,720]{1,0:T(8,128)(2,1)S(1)}, bf16[1440,720]{1,0:T(8,128)(2,1)S(1)}, u32[]{:S(2)}, u32[]{:S(2)}) collective-permute-start(bf16[1440,720]{1,0:T(8,128)(2,1)S(1)} %get-tuple-element.39.refs_4_.refs_6_), channel_id=1, source_target_pairs={{0,1},{1,0},{2,3},{3,2},{4,5},{5,4},{6,7},{7,6},{8,9},{9,8},{10,11... | collective-permute-start | bytes 6220808 | tf_op jit(solution)/shard_map/ppermute | solution.py:219
  16.2 7.3 %collective-permute-start.3 = (bf16[64,1456]{1,0:T(8,128)(2,1)S(1)}, bf16[64,1456]{1,0:T(8,128)(2,1)S(1)}, u32[]{:S(2)}, u32[]{:S(2)}) collective-permute-start(bf16[64,1456]{1,0:T(8,128)(2,1)S(1)} %get-tuple-element.36.refs_0_), channel_id=1, source_target_pairs={{0,2},{2,0},{1,3},{3,1},{4,6},{6,4},{5,7},{7,5},{8,10},{10,8},{9,1... | collective-permute-start | bytes 559112 | tf_op jit(solution)/shard_map/ppermute | solution.py:219
  17.8 11.2 %collective-permute-start.12 = (bf16[64,1456]{1,0:T(8,128)(2,1)S(1)}, bf16[64,1456]{1,0:T(8,128)(2,1)S(1)}, u32[]{:S(2)}, u32[]{:S(2)}) collective-permute-start(bf16[64,1456]{1,0:T(8,128)(2,1)S(1)} %get-tuple-element.36.refs_0_), channel_id=1, source_target_pairs={{0,4},{4,0},{8,12},{12,8},{1,5},{5,1},{9,13},{13,9},{2,6},{6,2},{1... | collective-permute-start | bytes 559112 | tf_op jit(solution)/shard_map/ppermute | solution.py:212
  19.5 9.5 %collective-permute-start.13 = (bf16[64,1456]{1,0:T(8,128)(2,1)S(1)}, bf16[64,1456]{1,0:T(8,128)(2,1)S(1)}, u32[]{:S(2)}, u32[]{:S(2)}) collective-permute-start(bf16[64,1456]{1,0:T(8,128)(2,1)S(1)} %get-tuple-element.55), channel_id=1, source_target_pairs={{0,6},{2,4},{4,2},{6,0},{8,14},{10,12},{12,10},{14,8},{1,7},{3,5},... | collective-permute-start | bytes 559112 | tf_op jit(solution)/shard_map/ppermute | solution.py:216
  26.9 10.8 %collective-permute-start.8 = (bf16[64,1456]{1,0:T(8,128)(2,1)S(1)}, bf16[64,1456]{1,0:T(8,128)(2,1)S(1)}, u32[]{:S(2)}, u32[]{:S(2)}) collective-permute-start(bf16[64,1456]{1,0:T(8,128)(2,1)S(1)} %get-tuple-element.45.refs_2_), channel_id=1, source_target_pairs={{0,2},{2,0},{1,3},{3,1},{4,6},{6,4},{5,7},{7,5},{8,10},{10,8},{9,1... | collective-permute-start | bytes 559112 | tf_op jit(solution)/shard_map/ppermute | solution.py:219
  28.4 9.2 %collective-permute-start.7 = (bf16[64,1440]{1,0:T(8,128)(2,1)S(1)}, bf16[64,1440]{1,0:T(8,128)(2,1)S(1)}, u32[]{:S(2)}, u32[]{:S(2)}) collective-permute-start(bf16[64,1440]{1,0:T(8,128)(2,1)S(1)} %get-tuple-element.44), channel_id=1, source_target_pairs={{0,2},{2,0},{1,3},{3,1},{4,6},{6,4},{5,7},{7,5},{8,10},{10,8},{9,1... | collective-permute-start | bytes 552968 | tf_op jit(solution)/shard_map/ppermute | solution.py:219
  32.4 12.2 %collective-permute-start.14 = (bf16[64,1440]{1,0:T(8,128)(2,1)S(1)}, bf16[64,1440]{1,0:T(8,128)(2,1)S(1)}, u32[]{:S(2)}, u32[]{:S(2)}) collective-permute-start(bf16[64,1440]{1,0:T(8,128)(2,1)S(1)} %convert_element_type.38), channel_id=1, source_target_pairs={{0,4},{4,0},{8,12},{12,8},{1,5},{5,1},{9,13},{13,9},{2,6},{6,2},{1... | collective-permute-start | bytes 552968 | tf_op jit(solution)/shard_map/ppermute | solution.py:212
  34.1 10.4 %collective-permute-start.15 = (bf16[64,1440]{1,0:T(8,128)(2,1)S(1)}, bf16[64,1440]{1,0:T(8,128)(2,1)S(1)}, u32[]{:S(2)}, u32[]{:S(2)}) collective-permute-start(bf16[64,1440]{1,0:T(8,128)(2,1)S(1)} %get-tuple-element.62), channel_id=1, source_target_pairs={{0,6},{2,4},{4,2},{6,0},{8,14},{10,12},{12,10},{14,8},{1,7},{3,5},... | collective-permute-start | bytes 552968 | tf_op jit(solution)/shard_map/ppermute | solution.py:216
  42.3 5.9 %collective-permute-start.9 = (bf16[64,1440]{1,0:T(8,128)(2,1)S(1)}, bf16[64,1440]{1,0:T(8,128)(2,1)S(1)}, u32[]{:S(2)}, u32[]{:S(2)}) collective-permute-start(bf16[64,1440]{1,0:T(8,128)(2,1)S(1)} %get-tuple-element.50), channel_id=1, source_target_pairs={{0,2},{2,0},{1,3},{3,1},{4,6},{6,4},{5,7},{7,5},{8,10},{10,8},{9,1... | collective-permute-start | bytes 552968 | tf_op jit(solution)/shard_map/ppermute | solution.py:219
  44.7 8.7 %collective-permute-start.16 = (bf16[64,1440]{1,0:T(8,128)(2,1)S(1)}, bf16[64,1440]{1,0:T(8,128)(2,1)S(1)}, u32[]{:S(2)}, u32[]{:S(2)}) collective-permute-start(bf16[64,1440]{1,0:T(8,128)(2,1)S(1)} %add_convert_fusion.1), channel_id=1, source_target_pairs={{0,12},{4,8},{8,4},{12,0},{1,13},{5,9},{9,5},{13,1},{2,14},{6,10},... | collective-permute-start | bytes 552968 | tf_op jit(solution)/shard_map/ppermute | solution.py:212
  48.3 7.1 %collective-permute-start.11 = (bf16[64,1440]{1,0:T(8,128)(2,1)S(1)}, bf16[64,1440]{1,0:T(8,128)(2,1)S(1)}, u32[]{:S(2)}, u32[]{:S(2)}) collective-permute-start(bf16[64,1440]{1,0:T(8,128)(2,1)S(1)} %add_convert_fusion.2), channel_id=1, source_target_pairs={{0,4},{4,0},{8,12},{12,8},{1,5},{5,1},{9,13},{13,9},{2,6},{6,2},{1... | collective-permute-start | bytes 552968 | tf_op jit(solution)/shard_map/ppermute | solution.py:212
  50.0 6.0 %collective-permute-start.10 = (bf16[64,1440]{1,0:T(8,128)(2,1)S(1)}, bf16[64,1440]{1,0:T(8,128)(2,1)S(1)}, u32[]{:S(2)}, u32[]{:S(2)}) collective-permute-start(bf16[64,1440]{1,0:T(8,128)(2,1)S(1)} %get-tuple-element.52), channel_id=1, source_target_pairs={{0,2},{2,0},{1,3},{3,1},{4,6},{6,4},{5,7},{7,5},{8,10},{10,8},{9,1... | collective-permute-start | bytes 552968 | tf_op jit(solution)/shard_map/ppermute | solution.py:219
  56.2 1.4 %collective-permute-start.17 = (bf16[64,720]{1,0:T(8,128)(2,1)S(1)}, bf16[64,720]{1,0:T(8,128)(2,1)S(1)}, u32[]{:S(2)}, u32[]{:S(2)}) collective-permute-start(bf16[64,720]{1,0:T(8,128)(2,1)S(1)} %get-tuple-element.64), channel_id=1, source_target_pairs={{0,1},{1,0},{2,3},{3,2},{4,5},{5,4},{6,7},{7,6},{8,9},{9,8},{10,11... | collective-permute-start | bytes 276488 | tf_op jit(solution)/shard_map/ppermute | solution.py:219

commit v4 on v3

--- a/solution.py
+++ b/solution.py
@@ -184,6 +184,32 @@
     )(*[pltpu.with_memory_space_constraint(x, pltpu.HBM) for x in arrays], after)
 
 
+def halves_kernel(place_ref, *refs):
+    ins, (here, there) = refs[:-2], refs[-2:]
+    half_width = here.shape[1]
+    total = ins[0][...]
+    for ref in ins[1:]:
+        total = total + ref[...].astype(jnp.float32)
+    first = place_ref[2] == 0
+    left, right = total[:, :half_width], total[:, half_width:]
+    here[...] = jnp.where(first, left, right).astype(here.dtype)
+    there[...] = jnp.where(first, right, left).astype(there.dtype)
+
+
+def halves(place, kept, *arrays):
+    rows, width = arrays[0].shape
+    vmem = pl.BlockSpec(memory_space=pltpu.VMEM)
+    return pl.pallas_call(
+        halves_kernel,
+        out_shape=tuple(
+            jax.ShapeDtypeStruct((rows, width // 2), dtype) for dtype in (kept, jnp.bfloat16)
+        ),
+        in_specs=[pl.BlockSpec(memory_space=pltpu.SMEM)] + [vmem] * len(arrays),
+        out_specs=(vmem, vmem),
+        compiler_params=pltpu.CompilerParams(vmem_limit_bytes=8 * 1024 * 1024),
+    )(place, *arrays)
+
+
 def hold_kernel(*refs):
     del refs
 
@@ -202,7 +228,6 @@
 def gathered(hidden, expert_ids, gate_units, w_gate, w_up, w_down):
     token_count, model_width = hidden.shape
     half_rows = token_count // 2
-    half_width = model_width // 2
     tp = lax.axis_index("tp")
     expert_count = lax.axis_size("seq") * lax.axis_size("tp")
     expert = lax.axis_index("seq") * lax.axis_size("tp") + tp
@@ -233,10 +258,10 @@
     down2 = swap(down1, "tp")
     weights = gate1, up1, down1, gate2, up2, down2
     near_sum3, far_sum3 = run([near3, far3], weights)
-    far_sum3, near1 = hold(far_sum3, near1)
+    far_sum3, far0 = hold(far_sum3, far0)
     near2, far2, near_sum3 = hold(near2, far2, near_sum3)
     near_sum2, far_sum2 = run([near2, far2], weights)
-    back3, far1, own = hold(swap(far_sum3, "ep"), swap(near1, "ep"), own)
+    back3, far1, own = hold(swap(far_sum3, "ep"), z(far0, 1), own)
     near_sum0, far_sum0, near_sum1, far_sum1 = run([own, far0, near1, far1], weights)
 
     def f32(x):
@@ -247,16 +272,14 @@
 
     merged = near_sum3 + f32(back3) + f32(z(bf16(near_sum2), 1)) + f32(diagonal(far_sum2))
     back1, far_sum0 = hold(swap(far_sum1, "ep"), far_sum0)
-    total = (
-        near_sum0
-        + f32(swap(far_sum0, "ep"))
-        + f32(z(bf16(near_sum1 + f32(back1)), 1))
-        + f32(z(bf16(merged), 3))
-    )
-    out = total.astype(jnp.bfloat16)
-    give = lax.dynamic_slice_in_dim(out, (1 - tp) * half_width, half_width, 1)
-    keep = lax.dynamic_slice_in_dim(out, tp * half_width, half_width, 1)
-    get = swap(give, "tp")
+    here1, there1 = halves(place, jnp.bfloat16, near_sum1, back1)
+    seq = [(i, i ^ 1) for i in range(lax.axis_size("seq"))]
+    across = [(2 * i + c, 2 * j + 1 - c) for i, j in seq for c in range(2)]
+    last_there = lax.ppermute(there1, ("seq", "tp"), across)
+    last_here = z(here1, 1)
+    here0, there0 = halves(place, jnp.float32, near_sum0, swap(far_sum0, "ep"), z(bf16(merged), 3))
+    keep = bf16(here0 + f32(last_here))
+    get = bf16(f32(swap(there0, "tp")) + f32(last_there))
     return jnp.where(tp == 0, jnp.concatenate([keep, get]), jnp.concatenate([get, keep]))
 
 

time: 58.6 us -> 57.9 us (0.988)
  starting transfers between devices: 24.1 us -> 22 us
  Pallas kernels: 17 us -> 18.6 us
    ppermute x6 -> x7, waiting for transfers between devices: 6.27 us -> 3.69 us  [z(): lax.ppermute(x, 'seq', [(i, i ^ k) for i in range(lax.axis_size('seq'))])]
    ppermute x10 -> x9, starting transfers between devices: 10.3 us -> 8.14 us  [swap(): return lax.ppermute(x, axis, [(0, 1), (1, 0)])]
    ppermute x2, waiting for transfers between devices: 0.02 us -> 2.04 us  [diagonal(): return lax.ppermute(x, ('seq', 'ep'), flat)]
    pallas_call x0 -> x2, Pallas kernels: none -> 1.51 us  [halves(): pl.pallas_call(halves_kernel, out_shape=tuple((jax.ShapeDtypeStruct((rows...]
    ppermute x6 -> x7, starting transfers between devices: 12.2 us -> 11.8 us  [z(): lax.ppermute(x, 'seq', [(i, i ^ k) for i in range(lax.axis_size('seq'))])]
    ppermute x10 -> x9, waiting for transfers between devices: 9.57 us -> 9.88 us  [swap(): return lax.ppermute(x, axis, [(0, 1), (1, 0)])]
  transfers between devices with their start and end apart: 18 -> 19, of which waited for: 8 -> 9; matrix products, arithmetic and copies ran while one was open for 0% -> 0% of each run, Pallas kernels for 26% -> 29%
where the time goes in v4:
time: 57.9 us; the launch traced here: 57.8 us
  starting transfers between devices  22 us (38%)
  Pallas kernels  18.6 us (32%)
  waiting for transfers between devices  16 us (28%)
  local copies, waits for them, and re-layouts  0.82 us (1%)
    ppermute x7, starting transfers between devices, z(): lax.ppermute(x, 'seq', [(i, i ^ k) for i in range(lax.axis_size('seq'))])  11.8 us
    pallas_call x3, Pallas kernels, experts(): pl.pallas_call(functools.partial(expert_kernel, expert_count, count), out...  11.3 us
    ppermute x9, waiting for transfers between devices, swap(): return lax.ppermute(x, axis, [(0, 1), (1, 0)])  9.88 us
    ppermute x9, starting transfers between devices, swap(): return lax.ppermute(x, axis, [(0, 1), (1, 0)])  8.14 us
    pallas_call x2, Pallas kernels, stage(): pl.pallas_call(functools.partial(stage_kernel, len(arrays)), out_shape=tu...  3.94 us
    ppermute x7, waiting for transfers between devices, z(): lax.ppermute(x, 'seq', [(i, i ^ k) for i in range(lax.axis_size('seq'))])  3.69 us
    ppermute x2, waiting for transfers between devices, diagonal(): return lax.ppermute(x, ('seq', 'ep'), flat)  2.04 us
    pallas_call x1, Pallas kernels, prepare(): pl.pallas_call(prepare_kernel, out_shape=jax.ShapeDtypeStruct((token_coun...  1.77 us
  transfers between devices with their start and end apart: 19, of which 9 were waited for; matrix products, arithmetic and copies ran while one was open for 0% of the time, Pallas kernels for 29%

profile of v4, /device:TPU:0, one launch (start us, length us, event | category | flops | bytes accessed | tf_op | source)
XLA Modules:
  0.0 57.8 jit_solution(1527930021015179321)
XLA Ops:
  0.0 0.1 pad_add_fusion.place_ref
  0.1 1.8 %shard_map.64.refs_1_.refs_2_ = bf16[64,1456]{1,0:T(8,128)(2,1)S(1)} custom-call(s32[3]{0:T(128)S(1)} %pad_add_fusion.place_ref, bf16[1440,128]{1,0:T(8,128)(2,1)} %bitcast.14, s32[4,128]{1,0:T(4,128)} %bitcast.15, s32[4,128]{1,0:T(4,128)} %bitcast.16), custom_call_target="tpu_custom_call" | custom-call | tf_op jit(solution)/shard_map/pallas_call | solution.py:153
  1.9 5.1 %collective-permute-start = (bf16[64,1456]{1,0:T(8,128)(2,1)S(1)}, bf16[64,1456]{1,0:T(8,128)(2,1)S(1)}, u32[]{:S(2)}, u32[]{:S(2)}) collective-permute-start(bf16[64,1456]{1,0:T(8,128)(2,1)S(1)} %shard_map.64.refs_1_.refs_2_), channel_id=1, source_target_pairs={{0,12},{4,8},{8,4},{12,0},{1,13},{5,9},{9,5},{13,1},{2,14},{6,10},... | collective-permute-start | bytes 559112 | tf_op jit(solution)/shard_map/ppermute | solution.py:237
  7.0 0.0 collective-permute-start.1
  7.0 1.5 %collective-permute-start.2 = (bf16[64,1456]{1,0:T(8,128)(2,1)S(1)}, bf16[64,1456]{1,0:T(8,128)(2,1)S(1)}, u32[]{:S(2)}, u32[]{:S(2)}) collective-permute-start(bf16[64,1456]{1,0:T(8,128)(2,1)S(1)} %shard_map.64.refs_1_.refs_2_), channel_id=1, source_target_pairs={{0,2},{2,0},{1,3},{3,1},{4,6},{6,4},{5,7},{7,5},{8,10},{10,8},{9,1... | collective-permute-start | bytes 559112 | tf_op jit(solution)/shard_map/ppermute | solution.py:244
  8.5 0.0 collective-permute-start.4
  8.5 0.5 collective-permute-start.5
  9.0 2.3 %shard_map.66 = (bf16[1440,720]{1,0:T(8,128)(2,1)S(1)}, bf16[1440,720]{1,0:T(8,128)(2,1)S(1)}) custom-call(bf16[1440,720]{1,0:T(8,128)(2,1)} %bitcast.11, bf16[1440,720]{1,0:T(8,128)(2,1)} %bitcast.13, bf16[64,1456]{1,0:T(8,128)(2,1)S(1)} %shard_map.64.refs_1_.refs_2_), custom_call_target="tpu_custom_call" | custom-call | bytes 4147200 | tf_op jit(solution)/shard_map/pallas_call | solution.py:174
  11.3 1.6 %shard_map.65.refs_3_ = bf16[1440,720]{1,0:T(8,128)(2,1)S(1)} custom-call(bf16[1440,720]{1,0:T(8,128)(2,1)} %bitcast.9, bf16[64,1456]{1,0:T(8,128)(2,1)S(1)} %shard_map.64.refs_1_.refs_2_), custom_call_target="tpu_custom_call" | custom-call | bytes 2073600 | tf_op jit(solution)/shard_map/pallas_call | solution.py:174
  12.9 0.0 collective-permute-done.refs_0_
  12.9 3.2 %collective-permute-done.1.refs_1_ = bf16[64,1456]{1,0:T(8,128)(2,1)S(1)} collective-permute-done((bf16[64,1456]{1,0:T(8,128)(2,1)S(1)}, bf16[64,1456]{1,0:T(8,128)(2,1)S(1)}, u32[]{:S(2)}, u32[]{:S(2)}) %collective-permute-start.1) | collective-permute-done | bytes 186400 | tf_op jit(solution)/shard_map/ppermute | solution.py:237
  16.2 0.0 collective-permute-done.2.refs_2_
  16.2 0.0 collective-permute-start.6
  16.2 1.5 %collective-permute-start.3 = (bf16[64,1456]{1,0:T(8,128)(2,1)S(1)}, bf16[64,1456]{1,0:T(8,128)(2,1)S(1)}, u32[]{:S(2)}, u32[]{:S(2)}) collective-permute-start(bf16[64,1456]{1,0:T(8,128)(2,1)S(1)} %get-tuple-element.40.refs_0_), channel_id=1, source_target_pairs={{0,2},{2,0},{1,3},{3,1},{4,6},{6,4},{5,7},{7,5},{8,10},{10,8},{9,1... | collective-permute-start | bytes 559112 | tf_op jit(solution)/shard_map/ppermute | solution.py:244
  17.8 1.8 %collective-permute-start.11 = (bf16[64,1456]{1,0:T(8,128)(2,1)S(1)}, bf16[64,1456]{1,0:T(8,128)(2,1)S(1)}, u32[]{:S(2)}, u32[]{:S(2)}) collective-permute-start(bf16[64,1456]{1,0:T(8,128)(2,1)S(1)} %get-tuple-element.40.refs_0_), channel_id=1, source_target_pairs={{0,4},{4,0},{8,12},{12,8},{1,5},{5,1},{9,13},{13,9},{2,6},{6,2},{1... | collective-permute-start | bytes 559112 | tf_op jit(solution)/shard_map/ppermute | solution.py:237
  19.5 0.0 collective-permute-done.4.refs_1_
  19.5 0.0 collective-permute-done.5.refs_2_
  19.5 0.3 collective-permute-start.12
  19.8 3.7 %collective-permute-done.3.refs_1_ = bf16[64,1456]{1,0:T(8,128)(2,1)S(1)} collective-permute-done((bf16[64,1456]{1,0:T(8,128)(2,1)S(1)}, bf16[64,1456]{1,0:T(8,128)(2,1)S(1)}, u32[]{:S(2)}, u32[]{:S(2)}) %collective-permute-start.3) | collective-permute-done | bytes 186400 | tf_op jit(solution)/shard_map/ppermute | solution.py:244
  23.5 0.0 collective-permute-done.6.refs_7_.refs_9_
  23.5 3.3 %shard_map.69 = (f32[64,1440]{1,0:T(8,128)S(1)}, bf16[64,1440]{1,0:T(8,128)(2,1)S(1)}) custom-call(s32[3]{0:T(128)S(1)} %pad_add_fusion.place_ref, bf16[64,1456]{1,0:T(8,128)(2,1)S(1)} %get-tuple-element.40.refs_0_, bf16[64,1456]{1,0:T(8,128)(2,1)S(1)} %collective-permute-done.3.refs_1_, bf16[1440,720]{1,0:T(8,128)(2,1)S(1)} %get-tuple-element.41.refs_2_.refs_4_, ...), custom_call_target="tpu_custom_call" | custom-call | flops 1592524800 | bytes 745472 | tf_op jit(solution)/shard_map/pallas_call | solution.py:110
  26.9 1.8 %collective-permute-start.8 = (bf16[64,1456]{1,0:T(8,128)(2,1)S(1)}, bf16[64,1456]{1,0:T(8,128)(2,1)S(1)}, u32[]{:S(2)}, u32[]{:S(2)}) collective-permute-start(bf16[64,1456]{1,0:T(8,128)(2,1)S(1)} %get-tuple-element.49.refs_1_), channel_id=1, source_target_pairs={{0,4},{4,0},{8,12},{12,8},{1,5},{5,1},{9,13},{13,9},{2,6},{6,2},{1... | collective-permute-start | bytes 559112 | tf_op jit(solution)/shard_map/ppermute | solution.py:237
  28.6 1.5 %collective-permute-start.7 = (bf16[64,1440]{1,0:T(8,128)(2,1)S(1)}, bf16[64,1440]{1,0:T(8,128)(2,1)S(1)}, u32[]{:S(2)}, u32[]{:S(2)}) collective-permute-start(bf16[64,1440]{1,0:T(8,128)(2,1)S(1)} %get-tuple-element.48), channel_id=1, source_target_pairs={{0,2},{2,0},{1,3},{3,1},{4,6},{6,4},{5,7},{7,5},{8,10},{10,8},{9,1... | collective-permute-start | bytes 552968 | tf_op jit(solution)/shard_map/ppermute | solution.py:244
  30.1 0.0 collective-permute-done.11.refs_0_
  30.1 0.0 collective-permute-done.12.refs_1_
  30.1 3.4 %shard_map.75 = (f32[64,1440]{1,0:T(8,128)S(1)}, bf16[64,1440]{1,0:T(8,128)(2,1)S(1)}) custom-call(s32[3]{0:T(128)S(1)} %pad_add_fusion.place_ref, bf16[64,1456]{1,0:T(8,128)(2,1)S(1)} %get-tuple-element.61.refs_0_, bf16[64,1456]{1,0:T(8,128)(2,1)S(1)} %get-tuple-element.62.refs_1_, bf16[1440,720]{1,0:T(8,128)(2,1)S(1)} %get-tuple-element.41.refs_2_.refs_4_, ...), custom_call_target="tpu_custom_call" | custom-call | flops 1592524800 | bytes 745472 | tf_op jit(solution)/shard_map/pallas_call | solution.py:110
  33.5 0.6 %collective-permute-start.13 = (bf16[64,1440]{1,0:T(8,128)(2,1)S(1)}, bf16[64,1440]{1,0:T(8,128)(2,1)S(1)}, u32[]{:S(2)}, u32[]{:S(2)}) collective-permute-start(bf16[64,1440]{1,0:T(8,128)(2,1)S(1)} %convert_element_type.31), channel_id=1, source_target_pairs={{0,4},{4,0},{8,12},{12,8},{1,5},{5,1},{9,13},{13,9},{2,6},{6,2},{1... | collective-permute-start | bytes 552968 | tf_op jit(solution)/shard_map/ppermute | solution.py:237
  34.1 1.4 %collective-permute-start.14 = (bf16[64,1440]{1,0:T(8,128)(2,1)S(1)}, bf16[64,1440]{1,0:T(8,128)(2,1)S(1)}, u32[]{:S(2)}, u32[]{:S(2)}) collective-permute-start(bf16[64,1440]{1,0:T(8,128)(2,1)S(1)} %get-tuple-element.64), channel_id=1, source_target_pairs={{0,6},{2,4},{4,2},{6,0},{8,14},{10,12},{12,10},{14,8},{1,7},{3,5},... | collective-permute-start | bytes 552968 | tf_op jit(solution)/shard_map/ppermute | solution.py:241
  35.6 0.0 collective-permute-done.7.refs_0_
  35.6 0.0 collective-permute-done.8.refs_1_
  35.6 4.6 %shard_map.72 = (f32[64,1440]{1,0:T(8,128)S(1)}, bf16[64,1440]{1,0:T(8,128)(2,1)S(1)}, f32[64,1440]{1,0:T(8,128)S(1)}, bf16[64,1440]{1,0:T(8,128)(2,1)S(1)}) custom-call(s32[3]{0:T(128)S(1)} %pad_add_fusion.place_ref, bf16[64,1456]{1,0:T(8,128)(2,1)S(1)} %get-tuple-element.50.refs_0_, bf16[64,1456]{1,0:T(8,128)(2,1)S(1)} %get-tuple-element.49.refs_1_, ...), custom_call_target="tpu_custom_call" | custom-call | flops 3185049600 | bytes 1490944 | tf_op jit(solution)/shard_map/pallas_call | solution.py:110
  40.2 1.6 %collective-permute-start.9 = (bf16[64,1440]{1,0:T(8,128)(2,1)S(1)}, bf16[64,1440]{1,0:T(8,128)(2,1)S(1)}, u32[]{:S(2)}, u32[]{:S(2)}) collective-permute-start(bf16[64,1440]{1,0:T(8,128)(2,1)S(1)} %get-tuple-element.54), channel_id=1, source_target_pairs={{0,2},{2,0},{1,3},{3,1},{4,6},{6,4},{5,7},{7,5},{8,10},{10,8},{9,1... | collective-permute-start | bytes 552968 | tf_op jit(solution)/shard_map/ppermute | solution.py:244
  41.8 2.0 %collective-permute-done.14 = bf16[64,1440]{1,0:T(8,128)(2,1)S(1)} collective-permute-done((bf16[64,1440]{1,0:T(8,128)(2,1)S(1)}, bf16[64,1440]{1,0:T(8,128)(2,1)S(1)}, u32[]{:S(2)}, u32[]{:S(2)}) %collective-permute-start.14) | collective-permute-done | bytes 184352 | tf_op jit(solution)/shard_map/ppermute | solution.py:241
  43.8 0.1 add_convert_fusion
  43.9 1.8 %collective-permute-start.15 = (bf16[64,1440]{1,0:T(8,128)(2,1)S(1)}, bf16[64,1440]{1,0:T(8,128)(2,1)S(1)}, u32[]{:S(2)}, u32[]{:S(2)}) collective-permute-start(bf16[64,1440]{1,0:T(8,128)(2,1)S(1)} %add_convert_fusion), channel_id=1, source_target_pairs={{0,12},{4,8},{8,4},{12,0},{1,13},{5,9},{9,5},{13,1},{2,14},{6,10},... | collective-permute-start | bytes 552968 | tf_op jit(solution)/shard_map/ppermute | solution.py:237
  45.7 2.2 %collective-permute-done.9.refs_0_ = bf16[64,1440]{1,0:T(8,128)(2,1)S(1)} collective-permute-done((bf16[64,1440]{1,0:T(8,128)(2,1)S(1)}, bf16[64,1440]{1,0:T(8,128)(2,1)S(1)}, u32[]{:S(2)}, u32[]{:S(2)}) %collective-permute-start.9) | collective-permute-done | bytes 184352 | tf_op jit(solution)/shard_map/ppermute | solution.py:244
  47.9 1.4 %collective-permute-start.10 = (bf16[64,1440]{1,0:T(8,128)(2,1)S(1)}, bf16[64,1440]{1,0:T(8,128)(2,1)S(1)}, u32[]{:S(2)}, u32[]{:S(2)}) collective-permute-start(bf16[64,1440]{1,0:T(8,128)(2,1)S(1)} %get-tuple-element.56), channel_id=1, source_target_pairs={{0,2},{2,0},{1,3},{3,1},{4,6},{6,4},{5,7},{7,5},{8,10},{10,8},{9,1... | collective-permute-start | bytes 552968 | tf_op jit(solution)/shard_map/ppermute | solution.py:244
  49.4 0.7 %shard_map.77 = (bf16[64,720]{1,0:T(8,128)(2,1)S(1)}, bf16[64,720]{1,0:T(8,128)(2,1)S(1)}) custom-call(s32[3]{0:T(128)S(1)} %pad_add_fusion.place_ref, f32[64,1440]{1,0:T(8,128)S(1)} %get-tuple-element.66.refs_0_, bf16[64,1440]{1,0:T(8,128)(2,1)S(1)} %get-tuple-element.67.refs_1_), custom_call_target="tpu_custom_call" | custom-call | tf_op jit(solution)/shard_map/pallas_call | solution.py:202
  50.1 0.8 %collective-permute-start.16 = (bf16[64,720]{1,0:T(8,128)(2,1)S(1)}, bf16[64,720]{1,0:T(8,128)(2,1)S(1)}, u32[]{:S(2)}, u32[]{:S(2)}) collective-permute-start(bf16[64,720]{1,0:T(8,128)(2,1)S(1)} %get-tuple-element.68), channel_id=1, source_target_pairs={{0,4},{4,0},{8,12},{12,8},{1,5},{5,1},{9,13},{13,9},{2,6},{6,2},{1... | collective-permute-start | bytes 276488 | tf_op jit(solution)/shard_map/ppermute | solution.py:237
  51.0 0.2 collective-permute-start.18
  51.2 0.4 collective-permute-done.15.refs_2_
  51.6 3.2 %collective-permute-done.10.refs_1_ = bf16[64,1440]{1,0:T(8,128)(2,1)S(1)} collective-permute-done((bf16[64,1440]{1,0:T(8,128)(2,1)S(1)}, bf16[64,1440]{1,0:T(8,128)(2,1)S(1)}, u32[]{:S(2)}, u32[]{:S(2)}) %collective-permute-start.10) | collective-permute-done | bytes 184352 | tf_op jit(solution)/shard_map/ppermute | solution.py:244
  54.7 0.8 %shard_map.76 = (f32[64,720]{1,0:T(8,128)S(1)}, bf16[64,720]{1,0:T(8,128)(2,1)S(1)}) custom-call(s32[3]{0:T(128)S(1)} %pad_add_fusion.place_ref, f32[64,1440]{1,0:T(8,128)S(1)} %get-tuple-element.53.refs_0_, bf16[64,1440]{1,0:T(8,128)(2,1)S(1)} %collective-permute-done.10.refs_1_, bf16[64,1440]{1,0:T(8,128)(2,1)S(1)} %collective-permute-done.15.refs_2_), custom_call_target="tpu_custom_call" | custom-call | tf_op jit(solution)/shard_map/pallas_call | solution.py:202
  55.5 0.1 collective-permute-start.17
  55.6 0.1 collective-permute-done.16
  55.7 0.4 collective-permute-done.18
  56.1 0.8 %collective-permute-done.17 = bf16[64,720]{1,0:T(8,128)(2,1)S(1)} collective-permute-done((bf16[64,720]{1,0:T(8,128)(2,1)S(1)}, bf16[64,720]{1,0:T(8,128)(2,1)S(1)}, u32[]{:S(2)}, u32[]{:S(2)}) %collective-permute-start.17) | collective-permute-done | bytes 92192 | tf_op jit(solution)/shard_map/ppermute | solution.py:244
  57.0 0.8 %copy.26 = bf16[128,720]{0,1:T(8,128)(2,1)} copy(bf16[128,720]{1,0:T(8,128)(2,1)S(1)} %maximum_select_fusion) | data formatting | bytes 368640 | tf_op jit(solution)/shard_map/jit(_where)/select_n | solution.py:283
  (12 shorter events, 0.1 us)
Async XLA Ops:
  1.9 11.1 %collective-permute-start = (bf16[64,1456]{1,0:T(8,128)(2,1)S(1)}, bf16[64,1456]{1,0:T(8,128)(2,1)S(1)}, u32[]{:S(2)}, u32[]{:S(2)}) collective-permute-start(bf16[64,1456]{1,0:T(8,128)(2,1)S(1)} %shard_map.64.refs_1_.refs_2_), channel_id=1, source_target_pairs={{0,12},{4,8},{8,4},{12,0},{1,13},{5,9},{9,5},{13,1},{2,14},{6,10},... | collective-permute-start | bytes 559112 | tf_op jit(solution)/shard_map/ppermute | solution.py:237
  7.0 9.2 %collective-permute-start.1 = (bf16[64,1456]{1,0:T(8,128)(2,1)S(1)}, bf16[64,1456]{1,0:T(8,128)(2,1)S(1)}, u32[]{:S(2)}, u32[]{:S(2)}) collective-permute-start(bf16[64,1456]{1,0:T(8,128)(2,1)S(1)} %shard_map.64.refs_1_.refs_2_), channel_id=1, source_target_pairs={{0,4},{4,0},{8,12},{12,8},{1,5},{5,1},{9,13},{13,9},{2,6},{6,2},{1... | collective-permute-start | bytes 559112 | tf_op jit(solution)/shard_map/ppermute | solution.py:237
  7.0 9.2 %collective-permute-start.2 = (bf16[64,1456]{1,0:T(8,128)(2,1)S(1)}, bf16[64,1456]{1,0:T(8,128)(2,1)S(1)}, u32[]{:S(2)}, u32[]{:S(2)}) collective-permute-start(bf16[64,1456]{1,0:T(8,128)(2,1)S(1)} %shard_map.64.refs_1_.refs_2_), channel_id=1, source_target_pairs={{0,2},{2,0},{1,3},{3,1},{4,6},{6,4},{5,7},{7,5},{8,10},{10,8},{9,1... | collective-permute-start | bytes 559112 | tf_op jit(solution)/shard_map/ppermute | solution.py:244
  8.5 11.1 %collective-permute-start.4 = (bf16[1440,720]{1,0:T(8,128)(2,1)}, bf16[1440,720]{1,0:T(8,128)(2,1)S(1)}, u32[]{:S(2)}, u32[]{:S(2)}) collective-permute-start(bf16[1440,720]{1,0:T(8,128)(2,1)} %bitcast.10), channel_id=1, source_target_pairs={{0,1},{1,0},{2,3},{3,2},{4,5},{5,4},{6,7},{7,6},{8,9},{9,8},{10,11... | collective-permute-start | bytes 6220808 | tf_op jit(solution)/shard_map/ppermute | solution.py:244
  8.5 11.1 %collective-permute-start.5 = (bf16[1440,720]{1,0:T(8,128)(2,1)}, bf16[1440,720]{1,0:T(8,128)(2,1)S(1)}, u32[]{:S(2)}, u32[]{:S(2)}) collective-permute-start(bf16[1440,720]{1,0:T(8,128)(2,1)} %bitcast.12), channel_id=1, source_target_pairs={{0,1},{1,0},{2,3},{3,2},{4,5},{5,4},{6,7},{7,6},{8,9},{9,8},{10,11... | collective-permute-start | bytes 6220808 | tf_op jit(solution)/shard_map/ppermute | solution.py:244
  16.2 7.3 %collective-permute-start.6 = (bf16[1440,720]{1,0:T(8,128)(2,1)S(1)}, bf16[1440,720]{1,0:T(8,128)(2,1)S(1)}, u32[]{:S(2)}, u32[]{:S(2)}) collective-permute-start(bf16[1440,720]{1,0:T(8,128)(2,1)S(1)} %get-tuple-element.43.refs_4_.refs_6_), channel_id=1, source_target_pairs={{0,1},{1,0},{2,3},{3,2},{4,5},{5,4},{6,7},{7,6},{8,9},{9,8},{10,11... | collective-permute-start | bytes 6220808 | tf_op jit(solution)/shard_map/ppermute | solution.py:244
  16.2 7.3 %collective-permute-start.3 = (bf16[64,1456]{1,0:T(8,128)(2,1)S(1)}, bf16[64,1456]{1,0:T(8,128)(2,1)S(1)}, u32[]{:S(2)}, u32[]{:S(2)}) collective-permute-start(bf16[64,1456]{1,0:T(8,128)(2,1)S(1)} %get-tuple-element.40.refs_0_), channel_id=1, source_target_pairs={{0,2},{2,0},{1,3},{3,1},{4,6},{6,4},{5,7},{7,5},{8,10},{10,8},{9,1... | collective-permute-start | bytes 559112 | tf_op jit(solution)/shard_map/ppermute | solution.py:244
  17.8 12.4 %collective-permute-start.11 = (bf16[64,1456]{1,0:T(8,128)(2,1)S(1)}, bf16[64,1456]{1,0:T(8,128)(2,1)S(1)}, u32[]{:S(2)}, u32[]{:S(2)}) collective-permute-start(bf16[64,1456]{1,0:T(8,128)(2,1)S(1)} %get-tuple-element.40.refs_0_), channel_id=1, source_target_pairs={{0,4},{4,0},{8,12},{12,8},{1,5},{5,1},{9,13},{13,9},{2,6},{6,2},{1... | collective-permute-start | bytes 559112 | tf_op jit(solution)/shard_map/ppermute | solution.py:237
  19.5 10.6 %collective-permute-start.12 = (bf16[64,1456]{1,0:T(8,128)(2,1)S(1)}, bf16[64,1456]{1,0:T(8,128)(2,1)S(1)}, u32[]{:S(2)}, u32[]{:S(2)}) collective-permute-start(bf16[64,1456]{1,0:T(8,128)(2,1)S(1)} %get-tuple-element.57), channel_id=1, source_target_pairs={{0,6},{2,4},{4,2},{6,0},{8,14},{10,12},{12,10},{14,8},{1,7},{3,5},... | collective-permute-start | bytes 559112 | tf_op jit(solution)/shard_map/ppermute | solution.py:241
  26.9 8.7 %collective-permute-start.8 = (bf16[64,1456]{1,0:T(8,128)(2,1)S(1)}, bf16[64,1456]{1,0:T(8,128)(2,1)S(1)}, u32[]{:S(2)}, u32[]{:S(2)}) collective-permute-start(bf16[64,1456]{1,0:T(8,128)(2,1)S(1)} %get-tuple-element.49.refs_1_), channel_id=1, source_target_pairs={{0,4},{4,0},{8,12},{12,8},{1,5},{5,1},{9,13},{13,9},{2,6},{6,2},{1... | collective-permute-start | bytes 559112 | tf_op jit(solution)/shard_map/ppermute | solution.py:237
  28.6 7.0 %collective-permute-start.7 = (bf16[64,1440]{1,0:T(8,128)(2,1)S(1)}, bf16[64,1440]{1,0:T(8,128)(2,1)S(1)}, u32[]{:S(2)}, u32[]{:S(2)}) collective-permute-start(bf16[64,1440]{1,0:T(8,128)(2,1)S(1)} %get-tuple-element.48), channel_id=1, source_target_pairs={{0,2},{2,0},{1,3},{3,1},{4,6},{6,4},{5,7},{7,5},{8,10},{10,8},{9,1... | collective-permute-start | bytes 552968 | tf_op jit(solution)/shard_map/ppermute | solution.py:244
  33.5 8.3 %collective-permute-start.13 = (bf16[64,1440]{1,0:T(8,128)(2,1)S(1)}, bf16[64,1440]{1,0:T(8,128)(2,1)S(1)}, u32[]{:S(2)}, u32[]{:S(2)}) collective-permute-start(bf16[64,1440]{1,0:T(8,128)(2,1)S(1)} %convert_element_type.31), channel_id=1, source_target_pairs={{0,4},{4,0},{8,12},{12,8},{1,5},{5,1},{9,13},{13,9},{2,6},{6,2},{1... | collective-permute-start | bytes 552968 | tf_op jit(solution)/shard_map/ppermute | solution.py:237
  34.1 9.7 %collective-permute-start.14 = (bf16[64,1440]{1,0:T(8,128)(2,1)S(1)}, bf16[64,1440]{1,0:T(8,128)(2,1)S(1)}, u32[]{:S(2)}, u32[]{:S(2)}) collective-permute-start(bf16[64,1440]{1,0:T(8,128)(2,1)S(1)} %get-tuple-element.64), channel_id=1, source_target_pairs={{0,6},{2,4},{4,2},{6,0},{8,14},{10,12},{12,10},{14,8},{1,7},{3,5},... | collective-permute-start | bytes 552968 | tf_op jit(solution)/shard_map/ppermute | solution.py:241
  40.2 7.7 %collective-permute-start.9 = (bf16[64,1440]{1,0:T(8,128)(2,1)S(1)}, bf16[64,1440]{1,0:T(8,128)(2,1)S(1)}, u32[]{:S(2)}, u32[]{:S(2)}) collective-permute-start(bf16[64,1440]{1,0:T(8,128)(2,1)S(1)} %get-tuple-element.54), channel_id=1, source_target_pairs={{0,2},{2,0},{1,3},{3,1},{4,6},{6,4},{5,7},{7,5},{8,10},{10,8},{9,1... | collective-permute-start | bytes 552968 | tf_op jit(solution)/shard_map/ppermute | solution.py:244
  43.9 7.6 %collective-permute-start.15 = (bf16[64,1440]{1,0:T(8,128)(2,1)S(1)}, bf16[64,1440]{1,0:T(8,128)(2,1)S(1)}, u32[]{:S(2)}, u32[]{:S(2)}) collective-permute-start(bf16[64,1440]{1,0:T(8,128)(2,1)S(1)} %add_convert_fusion), channel_id=1, source_target_pairs={{0,12},{4,8},{8,4},{12,0},{1,13},{5,9},{9,5},{13,1},{2,14},{6,10},... | collective-permute-start | bytes 552968 | tf_op jit(solution)/shard_map/ppermute | solution.py:237
  47.9 6.8 %collective-permute-start.10 = (bf16[64,1440]{1,0:T(8,128)(2,1)S(1)}, bf16[64,1440]{1,0:T(8,128)(2,1)S(1)}, u32[]{:S(2)}, u32[]{:S(2)}) collective-permute-start(bf16[64,1440]{1,0:T(8,128)(2,1)S(1)} %get-tuple-element.56), channel_id=1, source_target_pairs={{0,2},{2,0},{1,3},{3,1},{4,6},{6,4},{5,7},{7,5},{8,10},{10,8},{9,1... | collective-permute-start | bytes 552968 | tf_op jit(solution)/shard_map/ppermute | solution.py:244
  50.1 5.5 %collective-permute-start.16 = (bf16[64,720]{1,0:T(8,128)(2,1)S(1)}, bf16[64,720]{1,0:T(8,128)(2,1)S(1)}, u32[]{:S(2)}, u32[]{:S(2)}) collective-permute-start(bf16[64,720]{1,0:T(8,128)(2,1)S(1)} %get-tuple-element.68), channel_id=1, source_target_pairs={{0,4},{4,0},{8,12},{12,8},{1,5},{5,1},{9,13},{13,9},{2,6},{6,2},{1... | collective-permute-start | bytes 276488 | tf_op jit(solution)/shard_map/ppermute | solution.py:237
  51.0 5.1 %collective-permute-start.18 = (bf16[64,720]{1,0:T(8,128)(2,1)S(1)}, bf16[64,720]{1,0:T(8,128)(2,1)S(1)}, u32[]{:S(2)}, u32[]{:S(2)}) collective-permute-start(bf16[64,720]{1,0:T(8,128)(2,1)S(1)} %get-tuple-element.70), channel_id=1, source_target_pairs={{0,5},{1,4},{4,1},{5,0},{8,13},{9,12},{12,9},{13,8},{2,7},{3,6},{6... | collective-permute-start | bytes 276488 | tf_op jit(solution)/shard_map/ppermute | solution.py:278
  55.5 1.4 %collective-permute-start.17 = (bf16[64,720]{1,0:T(8,128)(2,1)S(1)}, bf16[64,720]{1,0:T(8,128)(2,1)S(1)}, u32[]{:S(2)}, u32[]{:S(2)}) collective-permute-start(bf16[64,720]{1,0:T(8,128)(2,1)S(1)} %get-tuple-element.69), channel_id=1, source_target_pairs={{0,1},{1,0},{2,3},{3,2},{4,5},{5,4},{6,7},{7,6},{8,9},{9,8},{10,11... | collective-permute-start | bytes 276488 | tf_op jit(solution)/shard_map/ppermute | solution.py:244

commit v5 on v4

--- a/solution.py
+++ b/solution.py
@@ -214,7 +214,7 @@
     del refs
 
 
-def hold(*arrays):
+def hold(*arrays, weight=0):
     return pl.pallas_call(
         hold_kernel,
         out_shape=tuple(jax.ShapeDtypeStruct(x.shape, x.dtype) for x in arrays),
@@ -222,6 +222,7 @@
         out_specs=tuple([pl.BlockSpec(memory_space=pl.ANY)] * len(arrays)),
         input_output_aliases={i: i for i in range(len(arrays))},
         compiler_params=pltpu.CompilerParams(vmem_limit_bytes=1024 * 1024),
+        cost_estimate=pl.CostEstimate(flops=0, bytes_accessed=weight, transcendentals=0),
     )(*arrays)
 
 
@@ -271,13 +272,14 @@
         return x.astype(jnp.bfloat16)
 
     merged = near_sum3 + f32(back3) + f32(z(bf16(near_sum2), 1)) + f32(diagonal(far_sum2))
-    back1, far_sum0 = hold(swap(far_sum1, "ep"), far_sum0)
+    back1 = swap(far_sum1, "ep")
     here1, there1 = halves(place, jnp.bfloat16, near_sum1, back1)
     seq = [(i, i ^ 1) for i in range(lax.axis_size("seq"))]
     across = [(2 * i + c, 2 * j + 1 - c) for i, j in seq for c in range(2)]
     last_there = lax.ppermute(there1, ("seq", "tp"), across)
     last_here = z(here1, 1)
     here0, there0 = halves(place, jnp.float32, near_sum0, swap(far_sum0, "ep"), z(bf16(merged), 3))
+    last_here, last_there = hold(last_here, last_there, weight=1 << 24)
     keep = bf16(here0 + f32(last_here))
     get = bf16(f32(swap(there0, "tp")) + f32(last_there))
     return jnp.where(tp == 0, jnp.concatenate([keep, get]), jnp.concatenate([get, keep]))

time: 57.9 us -> 56.7 us (0.979)
  waiting for transfers between devices: 16 us -> 15 us
    ppermute x9, waiting for transfers between devices: 9.88 us -> 6.06 us  [swap(): return lax.ppermute(x, axis, [(0, 1), (1, 0)])]
    ppermute x1, waiting for transfers between devices: 0.39 us -> 1.83 us  [gathered(): last_there = lax.ppermute(there1, ('seq', 'tp'), across)]
    ppermute x7, waiting for transfers between devices: 3.69 us -> 5.11 us  [z(): lax.ppermute(x, 'seq', [(i, i ^ k) for i in range(lax.axis_size('seq'))])]
    ppermute x9, starting transfers between devices: 8.14 us -> 7.23 us  [swap(): return lax.ppermute(x, axis, [(0, 1), (1, 0)])]
    ppermute x7, starting transfers between devices: 11.8 us -> 12.7 us  [z(): lax.ppermute(x, 'seq', [(i, i ^ k) for i in range(lax.axis_size('seq'))])]
  transfers between devices with their start and end apart: 19 -> 19, of which waited for: 9 -> 8; matrix products, arithmetic and copies ran while one was open for 0% -> 0% of each run, Pallas kernels for 29% -> 30%
where the time goes in v5:
time: 56.7 us; the launch traced here: 56.6 us
  starting transfers between devices  21.7 us (38%)
  Pallas kernels  18.6 us (33%)
  waiting for transfers between devices  15 us (26%)
  local copies, waits for them, and re-layouts  0.82 us (1%)
    ppermute x7, starting transfers between devices, z(): lax.ppermute(x, 'seq', [(i, i ^ k) for i in range(lax.axis_size('seq'))])  12.7 us
    pallas_call x3, Pallas kernels, experts(): pl.pallas_call(functools.partial(expert_kernel, expert_count, count), out...  11.3 us
    ppermute x9, starting transfers between devices, swap(): return lax.ppermute(x, axis, [(0, 1), (1, 0)])  7.23 us
    ppermute x9, waiting for transfers between devices, swap(): return lax.ppermute(x, axis, [(0, 1), (1, 0)])  6.06 us
    ppermute x7, waiting for transfers between devices, z(): lax.ppermute(x, 'seq', [(i, i ^ k) for i in range(lax.axis_size('seq'))])  5.11 us
    pallas_call x2, Pallas kernels, stage(): pl.pallas_call(functools.partial(stage_kernel, len(arrays)), out_shape=tu...  3.94 us
    ppermute x2, waiting for transfers between devices, diagonal(): return lax.ppermute(x, ('seq', 'ep'), flat)  2.04 us
    ppermute x1, waiting for transfers between devices, gathered(): last_there = lax.ppermute(there1, ('seq', 'tp'), across)  1.83 us
  transfers between devices with their start and end apart: 19, of which 8 were waited for; matrix products, arithmetic and copies ran while one was open for 0% of the time, Pallas kernels for 30%

profile of v5, /device:TPU:0, one launch (start us, length us, event | category | flops | bytes accessed | tf_op | source)
XLA Modules:
  0.0 56.6 jit_solution(3678018598220214707)
XLA Ops:
  0.0 0.1 pad_add_fusion.place_ref
  0.1 1.8 %shard_map.64.refs_1_.refs_2_ = bf16[64,1456]{1,0:T(8,128)(2,1)S(1)} custom-call(s32[3]{0:T(128)S(1)} %pad_add_fusion.place_ref, bf16[1440,128]{1,0:T(8,128)(2,1)} %bitcast.14, s32[4,128]{1,0:T(4,128)} %bitcast.15, s32[4,128]{1,0:T(4,128)} %bitcast.16), custom_call_target="tpu_custom_call" | custom-call | tf_op jit(solution)/shard_map/pallas_call | solution.py:153
  1.9 5.1 %collective-permute-start = (bf16[64,1456]{1,0:T(8,128)(2,1)S(1)}, bf16[64,1456]{1,0:T(8,128)(2,1)S(1)}, u32[]{:S(2)}, u32[]{:S(2)}) collective-permute-start(bf16[64,1456]{1,0:T(8,128)(2,1)S(1)} %shard_map.64.refs_1_.refs_2_), channel_id=1, source_target_pairs={{0,12},{4,8},{8,4},{12,0},{1,13},{5,9},{9,5},{13,1},{2,14},{6,10},... | collective-permute-start | bytes 559112 | tf_op jit(solution)/shard_map/ppermute | solution.py:238
  7.0 0.0 collective-permute-start.1
  7.0 1.5 %collective-permute-start.2 = (bf16[64,1456]{1,0:T(8,128)(2,1)S(1)}, bf16[64,1456]{1,0:T(8,128)(2,1)S(1)}, u32[]{:S(2)}, u32[]{:S(2)}) collective-permute-start(bf16[64,1456]{1,0:T(8,128)(2,1)S(1)} %shard_map.64.refs_1_.refs_2_), channel_id=1, source_target_pairs={{0,2},{2,0},{1,3},{3,1},{4,6},{6,4},{5,7},{7,5},{8,10},{10,8},{9,1... | collective-permute-start | bytes 559112 | tf_op jit(solution)/shard_map/ppermute | solution.py:245
  8.5 0.0 collective-permute-start.4
  8.5 0.5 collective-permute-start.5
  9.0 2.3 %shard_map.66 = (bf16[1440,720]{1,0:T(8,128)(2,1)S(1)}, bf16[1440,720]{1,0:T(8,128)(2,1)S(1)}) custom-call(bf16[1440,720]{1,0:T(8,128)(2,1)} %bitcast.11, bf16[1440,720]{1,0:T(8,128)(2,1)} %bitcast.13, bf16[64,1456]{1,0:T(8,128)(2,1)S(1)} %shard_map.64.refs_1_.refs_2_), custom_call_target="tpu_custom_call" | custom-call | bytes 4147200 | tf_op jit(solution)/shard_map/pallas_call | solution.py:174
  11.3 1.6 %shard_map.65.refs_3_ = bf16[1440,720]{1,0:T(8,128)(2,1)S(1)} custom-call(bf16[1440,720]{1,0:T(8,128)(2,1)} %bitcast.9, bf16[64,1456]{1,0:T(8,128)(2,1)S(1)} %shard_map.64.refs_1_.refs_2_), custom_call_target="tpu_custom_call" | custom-call | bytes 2073600 | tf_op jit(solution)/shard_map/pallas_call | solution.py:174
  12.9 0.0 collective-permute-done.refs_0_
  12.9 3.2 %collective-permute-done.1.refs_1_ = bf16[64,1456]{1,0:T(8,128)(2,1)S(1)} collective-permute-done((bf16[64,1456]{1,0:T(8,128)(2,1)S(1)}, bf16[64,1456]{1,0:T(8,128)(2,1)S(1)}, u32[]{:S(2)}, u32[]{:S(2)}) %collective-permute-start.1) | collective-permute-done | bytes 186400 | tf_op jit(solution)/shard_map/ppermute | solution.py:238
  16.2 0.0 collective-permute-done.2.refs_2_
  16.2 0.0 collective-permute-start.6
  16.2 1.5 %collective-permute-start.3 = (bf16[64,1456]{1,0:T(8,128)(2,1)S(1)}, bf16[64,1456]{1,0:T(8,128)(2,1)S(1)}, u32[]{:S(2)}, u32[]{:S(2)}) collective-permute-start(bf16[64,1456]{1,0:T(8,128)(2,1)S(1)} %get-tuple-element.40.refs_0_), channel_id=1, source_target_pairs={{0,2},{2,0},{1,3},{3,1},{4,6},{6,4},{5,7},{7,5},{8,10},{10,8},{9,1... | collective-permute-start | bytes 559112 | tf_op jit(solution)/shard_map/ppermute | solution.py:245
  17.8 1.8 %collective-permute-start.10 = (bf16[64,1456]{1,0:T(8,128)(2,1)S(1)}, bf16[64,1456]{1,0:T(8,128)(2,1)S(1)}, u32[]{:S(2)}, u32[]{:S(2)}) collective-permute-start(bf16[64,1456]{1,0:T(8,128)(2,1)S(1)} %get-tuple-element.40.refs_0_), channel_id=1, source_target_pairs={{0,4},{4,0},{8,12},{12,8},{1,5},{5,1},{9,13},{13,9},{2,6},{6,2},{1... | collective-permute-start | bytes 559112 | tf_op jit(solution)/shard_map/ppermute | solution.py:238
  19.5 0.0 collective-permute-done.4.refs_1_
  19.5 0.0 collective-permute-done.5.refs_2_
  19.5 0.3 collective-permute-start.11
  19.8 3.7 %collective-permute-done.3.refs_1_ = bf16[64,1456]{1,0:T(8,128)(2,1)S(1)} collective-permute-done((bf16[64,1456]{1,0:T(8,128)(2,1)S(1)}, bf16[64,1456]{1,0:T(8,128)(2,1)S(1)}, u32[]{:S(2)}, u32[]{:S(2)}) %collective-permute-start.3) | collective-permute-done | bytes 186400 | tf_op jit(solution)/shard_map/ppermute | solution.py:245
  23.5 0.0 collective-permute-done.6.refs_7_.refs_9_
  23.5 3.3 %shard_map.69 = (f32[64,1440]{1,0:T(8,128)S(1)}, bf16[64,1440]{1,0:T(8,128)(2,1)S(1)}) custom-call(s32[3]{0:T(128)S(1)} %pad_add_fusion.place_ref, bf16[64,1456]{1,0:T(8,128)(2,1)S(1)} %get-tuple-element.40.refs_0_, bf16[64,1456]{1,0:T(8,128)(2,1)S(1)} %collective-permute-done.3.refs_1_, bf16[1440,720]{1,0:T(8,128)(2,1)S(1)} %get-tuple-element.41.refs_2_.refs_4_, ...), custom_call_target="tpu_custom_call" | custom-call | flops 1592524800 | bytes 745472 | tf_op jit(solution)/shard_map/pallas_call | solution.py:110
  26.9 1.8 %collective-permute-start.8 = (bf16[64,1456]{1,0:T(8,128)(2,1)S(1)}, bf16[64,1456]{1,0:T(8,128)(2,1)S(1)}, u32[]{:S(2)}, u32[]{:S(2)}) collective-permute-start(bf16[64,1456]{1,0:T(8,128)(2,1)S(1)} %get-tuple-element.49.refs_1_), channel_id=1, source_target_pairs={{0,4},{4,0},{8,12},{12,8},{1,5},{5,1},{9,13},{13,9},{2,6},{6,2},{1... | collective-permute-start | bytes 559112 | tf_op jit(solution)/shard_map/ppermute | solution.py:238
  28.6 1.5 %collective-permute-start.7 = (bf16[64,1440]{1,0:T(8,128)(2,1)S(1)}, bf16[64,1440]{1,0:T(8,128)(2,1)S(1)}, u32[]{:S(2)}, u32[]{:S(2)}) collective-permute-start(bf16[64,1440]{1,0:T(8,128)(2,1)S(1)} %get-tuple-element.48), channel_id=1, source_target_pairs={{0,2},{2,0},{1,3},{3,1},{4,6},{6,4},{5,7},{7,5},{8,10},{10,8},{9,1... | collective-permute-start | bytes 552968 | tf_op jit(solution)/shard_map/ppermute | solution.py:245
  30.1 0.0 collective-permute-done.10.refs_0_
  30.1 0.0 collective-permute-done.11.refs_1_
  30.1 3.4 %shard_map.74 = (f32[64,1440]{1,0:T(8,128)S(1)}, bf16[64,1440]{1,0:T(8,128)(2,1)S(1)}) custom-call(s32[3]{0:T(128)S(1)} %pad_add_fusion.place_ref, bf16[64,1456]{1,0:T(8,128)(2,1)S(1)} %get-tuple-element.59.refs_0_, bf16[64,1456]{1,0:T(8,128)(2,1)S(1)} %get-tuple-element.60.refs_1_, bf16[1440,720]{1,0:T(8,128)(2,1)S(1)} %get-tuple-element.41.refs_2_.refs_4_, ...), custom_call_target="tpu_custom_call" | custom-call | flops 1592524800 | bytes 745472 | tf_op jit(solution)/shard_map/pallas_call | solution.py:110
  33.5 0.6 %collective-permute-start.12 = (bf16[64,1440]{1,0:T(8,128)(2,1)S(1)}, bf16[64,1440]{1,0:T(8,128)(2,1)S(1)}, u32[]{:S(2)}, u32[]{:S(2)}) collective-permute-start(bf16[64,1440]{1,0:T(8,128)(2,1)S(1)} %convert_element_type.31), channel_id=1, source_target_pairs={{0,4},{4,0},{8,12},{12,8},{1,5},{5,1},{9,13},{13,9},{2,6},{6,2},{1... | collective-permute-start | bytes 552968 | tf_op jit(solution)/shard_map/ppermute | solution.py:238
  34.1 1.4 %collective-permute-start.13 = (bf16[64,1440]{1,0:T(8,128)(2,1)S(1)}, bf16[64,1440]{1,0:T(8,128)(2,1)S(1)}, u32[]{:S(2)}, u32[]{:S(2)}) collective-permute-start(bf16[64,1440]{1,0:T(8,128)(2,1)S(1)} %get-tuple-element.62), channel_id=1, source_target_pairs={{0,6},{2,4},{4,2},{6,0},{8,14},{10,12},{12,10},{14,8},{1,7},{3,5},... | collective-permute-start | bytes 552968 | tf_op jit(solution)/shard_map/ppermute | solution.py:242
  35.6 0.0 collective-permute-done.7.refs_0_
  35.6 0.0 collective-permute-done.8.refs_1_
  35.6 4.6 %shard_map.72 = (f32[64,1440]{1,0:T(8,128)S(1)}, bf16[64,1440]{1,0:T(8,128)(2,1)S(1)}, f32[64,1440]{1,0:T(8,128)S(1)}, bf16[64,1440]{1,0:T(8,128)(2,1)S(1)}) custom-call(s32[3]{0:T(128)S(1)} %pad_add_fusion.place_ref, bf16[64,1456]{1,0:T(8,128)(2,1)S(1)} %get-tuple-element.50.refs_0_, bf16[64,1456]{1,0:T(8,128)(2,1)S(1)} %get-tuple-element.49.refs_1_, ...), custom_call_target="tpu_custom_call" | custom-call | flops 3185049600 | bytes 1490944 | tf_op jit(solution)/shard_map/pallas_call | solution.py:110
  40.2 1.6 %collective-permute-start.15 = (bf16[64,1440]{1,0:T(8,128)(2,1)S(1)}, bf16[64,1440]{1,0:T(8,128)(2,1)S(1)}, u32[]{:S(2)}, u32[]{:S(2)}) collective-permute-start(bf16[64,1440]{1,0:T(8,128)(2,1)S(1)} %get-tuple-element.65), channel_id=1, source_target_pairs={{0,2},{2,0},{1,3},{3,1},{4,6},{6,4},{5,7},{7,5},{8,10},{10,8},{9,1... | collective-permute-start | bytes 552968 | tf_op jit(solution)/shard_map/ppermute | solution.py:245
  41.8 0.0 collective-permute-done.12
  41.8 2.0 %collective-permute-done.13 = bf16[64,1440]{1,0:T(8,128)(2,1)S(1)} collective-permute-done((bf16[64,1440]{1,0:T(8,128)(2,1)S(1)}, bf16[64,1440]{1,0:T(8,128)(2,1)S(1)}, u32[]{:S(2)}, u32[]{:S(2)}) %collective-permute-start.13) | collective-permute-done | bytes 184352 | tf_op jit(solution)/shard_map/ppermute | solution.py:242
  43.8 0.1 add_convert_fusion
  43.9 1.8 %collective-permute-start.14 = (bf16[64,1440]{1,0:T(8,128)(2,1)S(1)}, bf16[64,1440]{1,0:T(8,128)(2,1)S(1)}, u32[]{:S(2)}, u32[]{:S(2)}) collective-permute-start(bf16[64,1440]{1,0:T(8,128)(2,1)S(1)} %add_convert_fusion), channel_id=1, source_target_pairs={{0,12},{4,8},{8,4},{12,0},{1,13},{5,9},{9,5},{13,1},{2,14},{6,10},... | collective-permute-start | bytes 552968 | tf_op jit(solution)/shard_map/ppermute | solution.py:238
  45.7 0.5 collective-permute-start.9
  46.3 1.8 %collective-permute-done.15.refs_1_ = bf16[64,1440]{1,0:T(8,128)(2,1)S(1)} collective-permute-done((bf16[64,1440]{1,0:T(8,128)(2,1)S(1)}, bf16[64,1440]{1,0:T(8,128)(2,1)S(1)}, u32[]{:S(2)}, u32[]{:S(2)}) %collective-permute-start.15) | collective-permute-done | bytes 184352 | tf_op jit(solution)/shard_map/ppermute | solution.py:245
  48.1 0.7 %shard_map.76 = (bf16[64,720]{1,0:T(8,128)(2,1)S(1)}, bf16[64,720]{1,0:T(8,128)(2,1)S(1)}) custom-call(s32[3]{0:T(128)S(1)} %pad_add_fusion.place_ref, f32[64,1440]{1,0:T(8,128)S(1)} %get-tuple-element.64.refs_0_, bf16[64,1440]{1,0:T(8,128)(2,1)S(1)} %collective-permute-done.15.refs_1_), custom_call_target="tpu_custom_call" | custom-call | tf_op jit(solution)/shard_map/pallas_call | solution.py:202
  48.8 1.7 %collective-permute-start.16 = (bf16[64,720]{1,0:T(8,128)(2,1)S(1)}, bf16[64,720]{1,0:T(8,128)(2,1)S(1)}, u32[]{:S(2)}, u32[]{:S(2)}) collective-permute-start(bf16[64,720]{1,0:T(8,128)(2,1)S(1)} %get-tuple-element.66), channel_id=1, source_target_pairs={{0,4},{4,0},{8,12},{12,8},{1,5},{5,1},{9,13},{13,9},{2,6},{6,2},{1... | collective-permute-start | bytes 276488 | tf_op jit(solution)/shard_map/ppermute | solution.py:238
  50.5 1.1 %collective-permute-done.14.refs_2_ = bf16[64,1440]{1,0:T(8,128)(2,1)S(1)} collective-permute-done((bf16[64,1440]{1,0:T(8,128)(2,1)S(1)}, bf16[64,1440]{1,0:T(8,128)(2,1)S(1)}, u32[]{:S(2)}, u32[]{:S(2)}) %collective-permute-start.14) | collective-permute-done | bytes 184352 | tf_op jit(solution)/shard_map/ppermute | solution.py:238
  51.6 0.6 %collective-permute-done.9.refs_1_ = bf16[64,1440]{1,0:T(8,128)(2,1)S(1)} collective-permute-done((bf16[64,1440]{1,0:T(8,128)(2,1)S(1)}, bf16[64,1440]{1,0:T(8,128)(2,1)S(1)}, u32[]{:S(2)}, u32[]{:S(2)}) %collective-permute-start.9) | collective-permute-done | bytes 184352 | tf_op jit(solution)/shard_map/ppermute | solution.py:245
  52.2 0.8 %shard_map.75 = (f32[64,720]{1,0:T(8,128)S(1)}, bf16[64,720]{1,0:T(8,128)(2,1)S(1)}) custom-call(s32[3]{0:T(128)S(1)} %pad_add_fusion.place_ref, f32[64,1440]{1,0:T(8,128)S(1)} %get-tuple-element.53.refs_0_, bf16[64,1440]{1,0:T(8,128)(2,1)S(1)} %collective-permute-done.9.refs_1_, bf16[64,1440]{1,0:T(8,128)(2,1)S(1)} %collective-permute-done.14.refs_2_), custom_call_target="tpu_custom_call" | custom-call | tf_op jit(solution)/shard_map/pallas_call | solution.py:202
  52.9 0.1 collective-permute-start.18
  53.0 0.8 %collective-permute-done.16.refs_0_ = bf16[64,720]{1,0:T(8,128)(2,1)S(1)} collective-permute-done((bf16[64,720]{1,0:T(8,128)(2,1)S(1)}, bf16[64,720]{1,0:T(8,128)(2,1)S(1)}, u32[]{:S(2)}, u32[]{:S(2)}) %collective-permute-start.16) | collective-permute-done | bytes 92192 | tf_op jit(solution)/shard_map/ppermute | solution.py:238
  53.8 1.8 %collective-permute-done.17.refs_1_ = bf16[64,720]{1,0:T(8,128)(2,1)S(1)} collective-permute-done((bf16[64,720]{1,0:T(8,128)(2,1)S(1)}, bf16[64,720]{1,0:T(8,128)(2,1)S(1)}, u32[]{:S(2)}, u32[]{:S(2)}) %collective-permute-start.17) | collective-permute-done | bytes 92192 | tf_op jit(solution)/shard_map/ppermute | solution.py:279
  55.7 0.0 collective-permute-done.18
  55.8 0.8 %copy.26 = bf16[128,720]{0,1:T(8,128)(2,1)} copy(bf16[128,720]{1,0:T(8,128)(2,1)S(1)} %maximum_select_fusion) | data formatting | bytes 368640 | tf_op jit(solution)/shard_map/jit(_where)/select_n | solution.py:285
  (12 shorter events, 0.1 us)
Async XLA Ops:
  1.9 11.1 %collective-permute-start = (bf16[64,1456]{1,0:T(8,128)(2,1)S(1)}, bf16[64,1456]{1,0:T(8,128)(2,1)S(1)}, u32[]{:S(2)}, u32[]{:S(2)}) collective-permute-start(bf16[64,1456]{1,0:T(8,128)(2,1)S(1)} %shard_map.64.refs_1_.refs_2_), channel_id=1, source_target_pairs={{0,12},{4,8},{8,4},{12,0},{1,13},{5,9},{9,5},{13,1},{2,14},{6,10},... | collective-permute-start | bytes 559112 | tf_op jit(solution)/shard_map/ppermute | solution.py:238
  7.0 9.2 %collective-permute-start.1 = (bf16[64,1456]{1,0:T(8,128)(2,1)S(1)}, bf16[64,1456]{1,0:T(8,128)(2,1)S(1)}, u32[]{:S(2)}, u32[]{:S(2)}) collective-permute-start(bf16[64,1456]{1,0:T(8,128)(2,1)S(1)} %shard_map.64.refs_1_.refs_2_), channel_id=1, source_target_pairs={{0,4},{4,0},{8,12},{12,8},{1,5},{5,1},{9,13},{13,9},{2,6},{6,2},{1... | collective-permute-start | bytes 559112 | tf_op jit(solution)/shard_map/ppermute | solution.py:238
  7.0 9.2 %collective-permute-start.2 = (bf16[64,1456]{1,0:T(8,128)(2,1)S(1)}, bf16[64,1456]{1,0:T(8,128)(2,1)S(1)}, u32[]{:S(2)}, u32[]{:S(2)}) collective-permute-start(bf16[64,1456]{1,0:T(8,128)(2,1)S(1)} %shard_map.64.refs_1_.refs_2_), channel_id=1, source_target_pairs={{0,2},{2,0},{1,3},{3,1},{4,6},{6,4},{5,7},{7,5},{8,10},{10,8},{9,1... | collective-permute-start | bytes 559112 | tf_op jit(solution)/shard_map/ppermute | solution.py:245
  8.5 11.1 %collective-permute-start.4 = (bf16[1440,720]{1,0:T(8,128)(2,1)}, bf16[1440,720]{1,0:T(8,128)(2,1)S(1)}, u32[]{:S(2)}, u32[]{:S(2)}) collective-permute-start(bf16[1440,720]{1,0:T(8,128)(2,1)} %bitcast.10), channel_id=1, source_target_pairs={{0,1},{1,0},{2,3},{3,2},{4,5},{5,4},{6,7},{7,6},{8,9},{9,8},{10,11... | collective-permute-start | bytes 6220808 | tf_op jit(solution)/shard_map/ppermute | solution.py:245
  8.5 11.1 %collective-permute-start.5 = (bf16[1440,720]{1,0:T(8,128)(2,1)}, bf16[1440,720]{1,0:T(8,128)(2,1)S(1)}, u32[]{:S(2)}, u32[]{:S(2)}) collective-permute-start(bf16[1440,720]{1,0:T(8,128)(2,1)} %bitcast.12), channel_id=1, source_target_pairs={{0,1},{1,0},{2,3},{3,2},{4,5},{5,4},{6,7},{7,6},{8,9},{9,8},{10,11... | collective-permute-start | bytes 6220808 | tf_op jit(solution)/shard_map/ppermute | solution.py:245
  16.2 7.3 %collective-permute-start.6 = (bf16[1440,720]{1,0:T(8,128)(2,1)S(1)}, bf16[1440,720]{1,0:T(8,128)(2,1)S(1)}, u32[]{:S(2)}, u32[]{:S(2)}) collective-permute-start(bf16[1440,720]{1,0:T(8,128)(2,1)S(1)} %get-tuple-element.43.refs_4_.refs_6_), channel_id=1, source_target_pairs={{0,1},{1,0},{2,3},{3,2},{4,5},{5,4},{6,7},{7,6},{8,9},{9,8},{10,11... | collective-permute-start | bytes 6220808 | tf_op jit(solution)/shard_map/ppermute | solution.py:245
  16.2 7.3 %collective-permute-start.3 = (bf16[64,1456]{1,0:T(8,128)(2,1)S(1)}, bf16[64,1456]{1,0:T(8,128)(2,1)S(1)}, u32[]{:S(2)}, u32[]{:S(2)}) collective-permute-start(bf16[64,1456]{1,0:T(8,128)(2,1)S(1)} %get-tuple-element.40.refs_0_), channel_id=1, source_target_pairs={{0,2},{2,0},{1,3},{3,1},{4,6},{6,4},{5,7},{7,5},{8,10},{10,8},{9,1... | collective-permute-start | bytes 559112 | tf_op jit(solution)/shard_map/ppermute | solution.py:245
  17.8 12.4 %collective-permute-start.10 = (bf16[64,1456]{1,0:T(8,128)(2,1)S(1)}, bf16[64,1456]{1,0:T(8,128)(2,1)S(1)}, u32[]{:S(2)}, u32[]{:S(2)}) collective-permute-start(bf16[64,1456]{1,0:T(8,128)(2,1)S(1)} %get-tuple-element.40.refs_0_), channel_id=1, source_target_pairs={{0,4},{4,0},{8,12},{12,8},{1,5},{5,1},{9,13},{13,9},{2,6},{6,2},{1... | collective-permute-start | bytes 559112 | tf_op jit(solution)/shard_map/ppermute | solution.py:238
  19.5 10.6 %collective-permute-start.11 = (bf16[64,1456]{1,0:T(8,128)(2,1)S(1)}, bf16[64,1456]{1,0:T(8,128)(2,1)S(1)}, u32[]{:S(2)}, u32[]{:S(2)}) collective-permute-start(bf16[64,1456]{1,0:T(8,128)(2,1)S(1)} %get-tuple-element.55), channel_id=1, source_target_pairs={{0,6},{2,4},{4,2},{6,0},{8,14},{10,12},{12,10},{14,8},{1,7},{3,5},... | collective-permute-start | bytes 559112 | tf_op jit(solution)/shard_map/ppermute | solution.py:242
  26.9 8.7 %collective-permute-start.8 = (bf16[64,1456]{1,0:T(8,128)(2,1)S(1)}, bf16[64,1456]{1,0:T(8,128)(2,1)S(1)}, u32[]{:S(2)}, u32[]{:S(2)}) collective-permute-start(bf16[64,1456]{1,0:T(8,128)(2,1)S(1)} %get-tuple-element.49.refs_1_), channel_id=1, source_target_pairs={{0,4},{4,0},{8,12},{12,8},{1,5},{5,1},{9,13},{13,9},{2,6},{6,2},{1... | collective-permute-start | bytes 559112 | tf_op jit(solution)/shard_map/ppermute | solution.py:238
  28.6 7.0 %collective-permute-start.7 = (bf16[64,1440]{1,0:T(8,128)(2,1)S(1)}, bf16[64,1440]{1,0:T(8,128)(2,1)S(1)}, u32[]{:S(2)}, u32[]{:S(2)}) collective-permute-start(bf16[64,1440]{1,0:T(8,128)(2,1)S(1)} %get-tuple-element.48), channel_id=1, source_target_pairs={{0,2},{2,0},{1,3},{3,1},{4,6},{6,4},{5,7},{7,5},{8,10},{10,8},{9,1... | collective-permute-start | bytes 552968 | tf_op jit(solution)/shard_map/ppermute | solution.py:245
  33.5 8.3 %collective-permute-start.12 = (bf16[64,1440]{1,0:T(8,128)(2,1)S(1)}, bf16[64,1440]{1,0:T(8,128)(2,1)S(1)}, u32[]{:S(2)}, u32[]{:S(2)}) collective-permute-start(bf16[64,1440]{1,0:T(8,128)(2,1)S(1)} %convert_element_type.31), channel_id=1, source_target_pairs={{0,4},{4,0},{8,12},{12,8},{1,5},{5,1},{9,13},{13,9},{2,6},{6,2},{1... | collective-permute-start | bytes 552968 | tf_op jit(solution)/shard_map/ppermute | solution.py:238
  34.1 9.7 %collective-permute-start.13 = (bf16[64,1440]{1,0:T(8,128)(2,1)S(1)}, bf16[64,1440]{1,0:T(8,128)(2,1)S(1)}, u32[]{:S(2)}, u32[]{:S(2)}) collective-permute-start(bf16[64,1440]{1,0:T(8,128)(2,1)S(1)} %get-tuple-element.62), channel_id=1, source_target_pairs={{0,6},{2,4},{4,2},{6,0},{8,14},{10,12},{12,10},{14,8},{1,7},{3,5},... | collective-permute-start | bytes 552968 | tf_op jit(solution)/shard_map/ppermute | solution.py:242
  40.2 7.8 %collective-permute-start.15 = (bf16[64,1440]{1,0:T(8,128)(2,1)S(1)}, bf16[64,1440]{1,0:T(8,128)(2,1)S(1)}, u32[]{:S(2)}, u32[]{:S(2)}) collective-permute-start(bf16[64,1440]{1,0:T(8,128)(2,1)S(1)} %get-tuple-element.65), channel_id=1, source_target_pairs={{0,2},{2,0},{1,3},{3,1},{4,6},{6,4},{5,7},{7,5},{8,10},{10,8},{9,1... | collective-permute-start | bytes 552968 | tf_op jit(solution)/shard_map/ppermute | solution.py:245
  43.9 7.7 %collective-permute-start.14 = (bf16[64,1440]{1,0:T(8,128)(2,1)S(1)}, bf16[64,1440]{1,0:T(8,128)(2,1)S(1)}, u32[]{:S(2)}, u32[]{:S(2)}) collective-permute-start(bf16[64,1440]{1,0:T(8,128)(2,1)S(1)} %add_convert_fusion), channel_id=1, source_target_pairs={{0,12},{4,8},{8,4},{12,0},{1,13},{5,9},{9,5},{13,1},{2,14},{6,10},... | collective-permute-start | bytes 552968 | tf_op jit(solution)/shard_map/ppermute | solution.py:238
  45.7 6.4 %collective-permute-start.9 = (bf16[64,1440]{1,0:T(8,128)(2,1)S(1)}, bf16[64,1440]{1,0:T(8,128)(2,1)S(1)}, u32[]{:S(2)}, u32[]{:S(2)}) collective-permute-start(bf16[64,1440]{1,0:T(8,128)(2,1)S(1)} %get-tuple-element.54), channel_id=1, source_target_pairs={{0,2},{2,0},{1,3},{3,1},{4,6},{6,4},{5,7},{7,5},{8,10},{10,8},{9,1... | collective-permute-start | bytes 552968 | tf_op jit(solution)/shard_map/ppermute | solution.py:245
  48.8 5.0 %collective-permute-start.16 = (bf16[64,720]{1,0:T(8,128)(2,1)S(1)}, bf16[64,720]{1,0:T(8,128)(2,1)S(1)}, u32[]{:S(2)}, u32[]{:S(2)}) collective-permute-start(bf16[64,720]{1,0:T(8,128)(2,1)S(1)} %get-tuple-element.66), channel_id=1, source_target_pairs={{0,4},{4,0},{8,12},{12,8},{1,5},{5,1},{9,13},{13,9},{2,6},{6,2},{1... | collective-permute-start | bytes 276488 | tf_op jit(solution)/shard_map/ppermute | solution.py:238
  50.5 5.1 %collective-permute-start.17 = (bf16[64,720]{1,0:T(8,128)(2,1)S(1)}, bf16[64,720]{1,0:T(8,128)(2,1)S(1)}, u32[]{:S(2)}, u32[]{:S(2)}) collective-permute-start(bf16[64,720]{1,0:T(8,128)(2,1)S(1)} %get-tuple-element.67), channel_id=1, source_target_pairs={{0,5},{1,4},{4,1},{5,0},{8,13},{9,12},{12,9},{13,8},{2,7},{3,6},{6... | collective-permute-start | bytes 276488 | tf_op jit(solution)/shard_map/ppermute | solution.py:279
  52.9 2.7 %collective-permute-start.18 = (bf16[64,720]{1,0:T(8,128)(2,1)S(1)}, bf16[64,720]{1,0:T(8,128)(2,1)S(1)}, u32[]{:S(2)}, u32[]{:S(2)}) collective-permute-start(bf16[64,720]{1,0:T(8,128)(2,1)S(1)} %get-tuple-element.69), channel_id=1, source_target_pairs={{0,1},{1,0},{2,3},{3,2},{4,5},{5,4},{6,7},{7,6},{8,9},{9,8},{10,11... | collective-permute-start | bytes 276488 | tf_op jit(solution)/shard_map/ppermute | solution.py:245

commit v6 on v5

--- a/solution.py
+++ b/solution.py
@@ -92,9 +92,7 @@
         gate_pre = jnp.dot(x, wg[...], preferred_element_type=jnp.float32)
         up_pre = jnp.dot(x, wu[...], preferred_element_type=jnp.float32)
         act = ((up_pre + 1.0) * gate_pre * jax.nn.sigmoid(1.702 * gate_pre)).astype(jnp.bfloat16)
-        out = lax.dot_general(
-            act, wd[...], (((1,), (1,)), ((), ())), preferred_element_type=jnp.float32
-        )
+        out = jnp.dot(act, wd[...], preferred_element_type=jnp.float32)
         total = out * weight if total is None else total + out * weight
     half_rows = outs[0].shape[0]
     for i, ref in enumerate(outs):
@@ -210,6 +208,26 @@
     )(place, *arrays)
 
 
+def turn_kernel(w, after_ref, out, held, sem):
+    del after_ref
+    copy = pltpu.make_async_copy(w, held, sem)
+    copy.start()
+    copy.wait()
+    out[...] = held[...].T
+
+
+def turned(after, w):
+    return pl.pallas_call(
+        turn_kernel,
+        out_shape=jax.ShapeDtypeStruct(w.shape[::-1], w.dtype),
+        in_specs=[pl.BlockSpec(memory_space=pl.ANY)] * 2,
+        out_specs=pl.BlockSpec(memory_space=pltpu.VMEM),
+        scratch_shapes=[pltpu.VMEM(w.shape, w.dtype), pltpu.SemaphoreType.DMA],
+        compiler_params=pltpu.CompilerParams(vmem_limit_bytes=8 * 1024 * 1024),
+        cost_estimate=pl.CostEstimate(flops=0, bytes_accessed=2 * w.size, transcendentals=0),
+    )(pltpu.with_memory_space_constraint(w, pltpu.HBM), after)
+
+
 def hold_kernel(*refs):
     del refs
 
@@ -251,7 +269,7 @@
         z(own, 3),
         z(own, 1),
         swap(own, "ep"),
-        *stage(own, w_down[0]),
+        turned(own, w_down[0]),
         *stage(own, w_gate[0], w_up[0]),
     )
     held3, gate2, up2 = hold(near3, gate2, up2)

time: 56.7 us -> 56.3 us (level)
    pallas_call x0 -> x1, Pallas kernels: none -> 2.3 us  [turned(): pl.pallas_call(turn_kernel, out_shape=jax.ShapeDtypeStruct(w.shape[::-1],...]
    pallas_call x2 -> x1, Pallas kernels: 3.94 us -> 2.3 us  [stage(): pl.pallas_call(functools.partial(stage_kernel, len(arrays)), out_shape=tu...]
    pallas_call x3, Pallas kernels: 11.3 us -> 10.2 us  [experts(): pl.pallas_call(functools.partial(expert_kernel, expert_count, count), out...]
    ppermute x7, waiting for transfers between devices: 5.11 us -> 4.25 us  [z(): lax.ppermute(x, 'seq', [(i, i ^ k) for i in range(lax.axis_size('seq'))])]
    ppermute x9, starting transfers between devices: 7.23 us -> 6.52 us  [swap(): return lax.ppermute(x, axis, [(0, 1), (1, 0)])]
    ppermute x7, starting transfers between devices: 12.7 us -> 13.4 us  [z(): lax.ppermute(x, 'seq', [(i, i ^ k) for i in range(lax.axis_size('seq'))])]
    ppermute x2, waiting for transfers between devices: 2.04 us -> 2.64 us  [diagonal(): return lax.ppermute(x, ('seq', 'ep'), flat)]
  transfers between devices with their start and end apart: 19 -> 19, of which waited for: 8 -> 8; matrix products, arithmetic and copies ran while one was open for 0% -> 0% of each run, Pallas kernels for 30% -> 29%
where the time goes in v6:
time: 56.3 us; the launch traced here: 56.1 us
  starting transfers between devices  21.7 us (39%)
  Pallas kernels  18.1 us (32%)
  waiting for transfers between devices  15.1 us (27%)
  local copies, waits for them, and re-layouts  0.82 us (1%)
    ppermute x7, starting transfers between devices, z(): lax.ppermute(x, 'seq', [(i, i ^ k) for i in range(lax.axis_size('seq'))])  13.4 us
    pallas_call x3, Pallas kernels, experts(): pl.pallas_call(functools.partial(expert_kernel, expert_count, count), out...  10.2 us
    ppermute x9, starting transfers between devices, swap(): return lax.ppermute(x, axis, [(0, 1), (1, 0)])  6.52 us
    ppermute x9, waiting for transfers between devices, swap(): return lax.ppermute(x, axis, [(0, 1), (1, 0)])  6.08 us
    ppermute x7, waiting for transfers between devices, z(): lax.ppermute(x, 'seq', [(i, i ^ k) for i in range(lax.axis_size('seq'))])  4.25 us
    ppermute x2, waiting for transfers between devices, diagonal(): return lax.ppermute(x, ('seq', 'ep'), flat)  2.64 us
    pallas_call x1, Pallas kernels, stage(): pl.pallas_call(functools.partial(stage_kernel, len(arrays)), out_shape=tu...  2.3 us
    pallas_call x1, Pallas kernels, turned(): pl.pallas_call(turn_kernel, out_shape=jax.ShapeDtypeStruct(w.shape[::-1],...  2.3 us
  transfers between devices with their start and end apart: 19, of which 8 were waited for; matrix products, arithmetic and copies ran while one was open for 0% of the time, Pallas kernels for 29%

profile of v6, /device:TPU:0, one launch (start us, length us, event | category | flops | bytes accessed | tf_op | source)
XLA Modules:
  0.0 56.1 jit_solution(15656622380411515577)
XLA Ops:
  0.0 0.1 pad_add_fusion.place_ref
  0.1 1.8 %shard_map.64.after_ref.refs_2_ = bf16[64,1456]{1,0:T(8,128)(2,1)S(1)} custom-call(s32[3]{0:T(128)S(1)} %pad_add_fusion.place_ref, bf16[1440,128]{1,0:T(8,128)(2,1)} %bitcast.14, s32[4,128]{1,0:T(4,128)} %bitcast.15, s32[4,128]{1,0:T(4,128)} %bitcast.16), custom_call_target="tpu_custom_call" | custom-call | tf_op jit(solution)/shard_map/pallas_call | solution.py:151
  1.9 5.1 %collective-permute-start = (bf16[64,1456]{1,0:T(8,128)(2,1)S(1)}, bf16[64,1456]{1,0:T(8,128)(2,1)S(1)}, u32[]{:S(2)}, u32[]{:S(2)}) collective-permute-start(bf16[64,1456]{1,0:T(8,128)(2,1)S(1)} %shard_map.64.after_ref.refs_2_), channel_id=1, source_target_pairs={{0,12},{4,8},{8,4},{12,0},{1,13},{5,9},{9,5},{13,1},{2,14},{6,10},... | collective-permute-start | bytes 559112 | tf_op jit(solution)/shard_map/ppermute | solution.py:256
  7.0 0.0 collective-permute-start.1
  7.0 1.5 %collective-permute-start.2 = (bf16[64,1456]{1,0:T(8,128)(2,1)S(1)}, bf16[64,1456]{1,0:T(8,128)(2,1)S(1)}, u32[]{:S(2)}, u32[]{:S(2)}) collective-permute-start(bf16[64,1456]{1,0:T(8,128)(2,1)S(1)} %shard_map.64.after_ref.refs_2_), channel_id=1, source_target_pairs={{0,2},{2,0},{1,3},{3,1},{4,6},{6,4},{5,7},{7,5},{8,10},{10,8},{9,1... | collective-permute-start | bytes 559112 | tf_op jit(solution)/shard_map/ppermute | solution.py:263
  8.5 0.0 collective-permute-start.4
  8.5 0.5 collective-permute-start.5
  9.0 2.3 %shard_map.66 = (bf16[1440,720]{1,0:T(8,128)(2,1)S(1)}, bf16[1440,720]{1,0:T(8,128)(2,1)S(1)}) custom-call(bf16[1440,720]{1,0:T(8,128)(2,1)} %bitcast.11, bf16[1440,720]{1,0:T(8,128)(2,1)} %bitcast.13, bf16[64,1456]{1,0:T(8,128)(2,1)S(1)} %shard_map.64.after_ref.refs_2_), custom_call_target="tpu_custom_call" | custom-call | bytes 4147200 | tf_op jit(solution)/shard_map/pallas_call | solution.py:172
  11.3 2.3 %shard_map.65.refs_3_ = bf16[720,1440]{1,0:T(8,128)(2,1)S(1)} custom-call(bf16[1440,720]{1,0:T(8,128)(2,1)} %bitcast.9, bf16[64,1456]{1,0:T(8,128)(2,1)S(1)} %shard_map.64.after_ref.refs_2_), custom_call_target="tpu_custom_call" | custom-call | bytes 2073600 | tf_op jit(solution)/shard_map/pallas_call | solution.py:220
  13.6 0.0 collective-permute-done.refs_0_
  13.6 2.6 %collective-permute-done.1.refs_1_ = bf16[64,1456]{1,0:T(8,128)(2,1)S(1)} collective-permute-done((bf16[64,1456]{1,0:T(8,128)(2,1)S(1)}, bf16[64,1456]{1,0:T(8,128)(2,1)S(1)}, u32[]{:S(2)}, u32[]{:S(2)}) %collective-permute-start.1) | collective-permute-done | bytes 186400 | tf_op jit(solution)/shard_map/ppermute | solution.py:256
  16.2 0.0 collective-permute-done.2.refs_2_
  16.2 0.0 collective-permute-start.6
  16.2 1.5 %collective-permute-start.3 = (bf16[64,1456]{1,0:T(8,128)(2,1)S(1)}, bf16[64,1456]{1,0:T(8,128)(2,1)S(1)}, u32[]{:S(2)}, u32[]{:S(2)}) collective-permute-start(bf16[64,1456]{1,0:T(8,128)(2,1)S(1)} %get-tuple-element.40.refs_0_), channel_id=1, source_target_pairs={{0,2},{2,0},{1,3},{3,1},{4,6},{6,4},{5,7},{7,5},{8,10},{10,8},{9,1... | collective-permute-start | bytes 559112 | tf_op jit(solution)/shard_map/ppermute | solution.py:263
  17.8 1.8 %collective-permute-start.10 = (bf16[64,1456]{1,0:T(8,128)(2,1)S(1)}, bf16[64,1456]{1,0:T(8,128)(2,1)S(1)}, u32[]{:S(2)}, u32[]{:S(2)}) collective-permute-start(bf16[64,1456]{1,0:T(8,128)(2,1)S(1)} %get-tuple-element.40.refs_0_), channel_id=1, source_target_pairs={{0,4},{4,0},{8,12},{12,8},{1,5},{5,1},{9,13},{13,9},{2,6},{6,2},{1... | collective-permute-start | bytes 559112 | tf_op jit(solution)/shard_map/ppermute | solution.py:256
  19.5 0.0 collective-permute-done.4.refs_1_
  19.5 0.0 collective-permute-done.5.refs_2_
  19.5 0.3 collective-permute-start.11
  19.8 3.7 %collective-permute-done.3.refs_1_ = bf16[64,1456]{1,0:T(8,128)(2,1)S(1)} collective-permute-done((bf16[64,1456]{1,0:T(8,128)(2,1)S(1)}, bf16[64,1456]{1,0:T(8,128)(2,1)S(1)}, u32[]{:S(2)}, u32[]{:S(2)}) %collective-permute-start.3) | collective-permute-done | bytes 186400 | tf_op jit(solution)/shard_map/ppermute | solution.py:263
  23.5 0.0 collective-permute-done.6.refs_7_.refs_9_
  23.5 2.8 %shard_map.69 = (f32[64,1440]{1,0:T(8,128)S(1)}, bf16[64,1440]{1,0:T(8,128)(2,1)S(1)}) custom-call(s32[3]{0:T(128)S(1)} %pad_add_fusion.place_ref, bf16[64,1456]{1,0:T(8,128)(2,1)S(1)} %get-tuple-element.40.refs_0_, bf16[64,1456]{1,0:T(8,128)(2,1)S(1)} %collective-permute-done.3.refs_1_, bf16[1440,720]{1,0:T(8,128)(2,1)S(1)} %get-tuple-element.41.refs_2_.refs_4_, ...), custom_call_target="tpu_custom_call" | custom-call | flops 1592524800 | bytes 745472 | tf_op jit(solution)/shard_map/pallas_call | solution.py:108
  26.3 1.8 %collective-permute-start.8 = (bf16[64,1456]{1,0:T(8,128)(2,1)S(1)}, bf16[64,1456]{1,0:T(8,128)(2,1)S(1)}, u32[]{:S(2)}, u32[]{:S(2)}) collective-permute-start(bf16[64,1456]{1,0:T(8,128)(2,1)S(1)} %get-tuple-element.49.refs_1_), channel_id=1, source_target_pairs={{0,4},{4,0},{8,12},{12,8},{1,5},{5,1},{9,13},{13,9},{2,6},{6,2},{1... | collective-permute-start | bytes 559112 | tf_op jit(solution)/shard_map/ppermute | solution.py:256
  28.1 1.5 %collective-permute-start.7 = (bf16[64,1440]{1,0:T(8,128)(2,1)S(1)}, bf16[64,1440]{1,0:T(8,128)(2,1)S(1)}, u32[]{:S(2)}, u32[]{:S(2)}) collective-permute-start(bf16[64,1440]{1,0:T(8,128)(2,1)S(1)} %get-tuple-element.48), channel_id=1, source_target_pairs={{0,2},{2,0},{1,3},{3,1},{4,6},{6,4},{5,7},{7,5},{8,10},{10,8},{9,1... | collective-permute-start | bytes 552968 | tf_op jit(solution)/shard_map/ppermute | solution.py:263
  29.6 0.0 collective-permute-done.10.refs_0_
  29.6 0.0 collective-permute-done.11.refs_1_
  29.6 2.8 %shard_map.74 = (f32[64,1440]{1,0:T(8,128)S(1)}, bf16[64,1440]{1,0:T(8,128)(2,1)S(1)}) custom-call(s32[3]{0:T(128)S(1)} %pad_add_fusion.place_ref, bf16[64,1456]{1,0:T(8,128)(2,1)S(1)} %get-tuple-element.59.refs_0_, bf16[64,1456]{1,0:T(8,128)(2,1)S(1)} %get-tuple-element.60.refs_1_, bf16[1440,720]{1,0:T(8,128)(2,1)S(1)} %get-tuple-element.41.refs_2_.refs_4_, ...), custom_call_target="tpu_custom_call" | custom-call | flops 1592524800 | bytes 745472 | tf_op jit(solution)/shard_map/pallas_call | solution.py:108
  32.4 1.2 %collective-permute-start.12 = (bf16[64,1440]{1,0:T(8,128)(2,1)S(1)}, bf16[64,1440]{1,0:T(8,128)(2,1)S(1)}, u32[]{:S(2)}, u32[]{:S(2)}) collective-permute-start(bf16[64,1440]{1,0:T(8,128)(2,1)S(1)} %convert_element_type.31), channel_id=1, source_target_pairs={{0,4},{4,0},{8,12},{12,8},{1,5},{5,1},{9,13},{13,9},{2,6},{6,2},{1... | collective-permute-start | bytes 552968 | tf_op jit(solution)/shard_map/ppermute | solution.py:256
  33.6 1.6 %collective-permute-start.13 = (bf16[64,1440]{1,0:T(8,128)(2,1)S(1)}, bf16[64,1440]{1,0:T(8,128)(2,1)S(1)}, u32[]{:S(2)}, u32[]{:S(2)}) collective-permute-start(bf16[64,1440]{1,0:T(8,128)(2,1)S(1)} %get-tuple-element.62), channel_id=1, source_target_pairs={{0,6},{2,4},{4,2},{6,0},{8,14},{10,12},{12,10},{14,8},{1,7},{3,5},... | collective-permute-start | bytes 552968 | tf_op jit(solution)/shard_map/ppermute | solution.py:260
  35.1 0.0 collective-permute-done.7.refs_0_
  35.1 0.0 collective-permute-done.8.refs_1_
  35.1 4.6 %shard_map.72 = (f32[64,1440]{1,0:T(8,128)S(1)}, bf16[64,1440]{1,0:T(8,128)(2,1)S(1)}, f32[64,1440]{1,0:T(8,128)S(1)}, bf16[64,1440]{1,0:T(8,128)(2,1)S(1)}) custom-call(s32[3]{0:T(128)S(1)} %pad_add_fusion.place_ref, bf16[64,1456]{1,0:T(8,128)(2,1)S(1)} %get-tuple-element.50.refs_0_, bf16[64,1456]{1,0:T(8,128)(2,1)S(1)} %get-tuple-element.49.refs_1_, ...), custom_call_target="tpu_custom_call" | custom-call | flops 3185049600 | bytes 1490944 | tf_op jit(solution)/shard_map/pallas_call | solution.py:108
  39.8 0.9 %collective-permute-start.15 = (bf16[64,1440]{1,0:T(8,128)(2,1)S(1)}, bf16[64,1440]{1,0:T(8,128)(2,1)S(1)}, u32[]{:S(2)}, u32[]{:S(2)}) collective-permute-start(bf16[64,1440]{1,0:T(8,128)(2,1)S(1)} %get-tuple-element.65), channel_id=1, source_target_pairs={{0,2},{2,0},{1,3},{3,1},{4,6},{6,4},{5,7},{7,5},{8,10},{10,8},{9,1... | collective-permute-start | bytes 552968 | tf_op jit(solution)/shard_map/ppermute | solution.py:263
  40.6 2.6 %collective-permute-done.13 = bf16[64,1440]{1,0:T(8,128)(2,1)S(1)} collective-permute-done((bf16[64,1440]{1,0:T(8,128)(2,1)S(1)}, bf16[64,1440]{1,0:T(8,128)(2,1)S(1)}, u32[]{:S(2)}, u32[]{:S(2)}) %collective-permute-start.13) | collective-permute-done | bytes 184352 | tf_op jit(solution)/shard_map/ppermute | solution.py:260
  43.3 0.1 add_convert_fusion
  43.4 1.8 %collective-permute-start.14 = (bf16[64,1440]{1,0:T(8,128)(2,1)S(1)}, bf16[64,1440]{1,0:T(8,128)(2,1)S(1)}, u32[]{:S(2)}, u32[]{:S(2)}) collective-permute-start(bf16[64,1440]{1,0:T(8,128)(2,1)S(1)} %add_convert_fusion), channel_id=1, source_target_pairs={{0,12},{4,8},{8,4},{12,0},{1,13},{5,9},{9,5},{13,1},{2,14},{6,10},... | collective-permute-start | bytes 552968 | tf_op jit(solution)/shard_map/ppermute | solution.py:256
  45.1 0.5 collective-permute-start.9
  45.7 1.9 %collective-permute-done.15.refs_1_ = bf16[64,1440]{1,0:T(8,128)(2,1)S(1)} collective-permute-done((bf16[64,1440]{1,0:T(8,128)(2,1)S(1)}, bf16[64,1440]{1,0:T(8,128)(2,1)S(1)}, u32[]{:S(2)}, u32[]{:S(2)}) %collective-permute-start.15) | collective-permute-done | bytes 184352 | tf_op jit(solution)/shard_map/ppermute | solution.py:263
  47.6 0.7 %shard_map.76 = (bf16[64,720]{1,0:T(8,128)(2,1)S(1)}, bf16[64,720]{1,0:T(8,128)(2,1)S(1)}) custom-call(s32[3]{0:T(128)S(1)} %pad_add_fusion.place_ref, f32[64,1440]{1,0:T(8,128)S(1)} %get-tuple-element.64.refs_0_, bf16[64,1440]{1,0:T(8,128)(2,1)S(1)} %collective-permute-done.15.refs_1_), custom_call_target="tpu_custom_call" | custom-call | tf_op jit(solution)/shard_map/pallas_call | solution.py:200
  48.4 1.8 %collective-permute-start.16 = (bf16[64,720]{1,0:T(8,128)(2,1)S(1)}, bf16[64,720]{1,0:T(8,128)(2,1)S(1)}, u32[]{:S(2)}, u32[]{:S(2)}) collective-permute-start(bf16[64,720]{1,0:T(8,128)(2,1)S(1)} %get-tuple-element.66), channel_id=1, source_target_pairs={{0,4},{4,0},{8,12},{12,8},{1,5},{5,1},{9,13},{13,9},{2,6},{6,2},{1... | collective-permute-start | bytes 276488 | tf_op jit(solution)/shard_map/ppermute | solution.py:256
  50.1 0.0 collective-permute-start.17
  50.1 1.0 %collective-permute-done.14.refs_2_ = bf16[64,1440]{1,0:T(8,128)(2,1)S(1)} collective-permute-done((bf16[64,1440]{1,0:T(8,128)(2,1)S(1)}, bf16[64,1440]{1,0:T(8,128)(2,1)S(1)}, u32[]{:S(2)}, u32[]{:S(2)}) %collective-permute-start.14) | collective-permute-done | bytes 184352 | tf_op jit(solution)/shard_map/ppermute | solution.py:256
  51.1 0.5 collective-permute-done.9.refs_1_
  51.6 0.8 %shard_map.75 = (f32[64,720]{1,0:T(8,128)S(1)}, bf16[64,720]{1,0:T(8,128)(2,1)S(1)}) custom-call(s32[3]{0:T(128)S(1)} %pad_add_fusion.place_ref, f32[64,1440]{1,0:T(8,128)S(1)} %get-tuple-element.53.refs_0_, bf16[64,1440]{1,0:T(8,128)(2,1)S(1)} %collective-permute-done.9.refs_1_, bf16[64,1440]{1,0:T(8,128)(2,1)S(1)} %collective-permute-done.14.refs_2_), custom_call_target="tpu_custom_call" | custom-call | tf_op jit(solution)/shard_map/pallas_call | solution.py:200
  52.3 0.1 collective-permute-start.18
  52.4 0.7 %collective-permute-done.16.refs_0_ = bf16[64,720]{1,0:T(8,128)(2,1)S(1)} collective-permute-done((bf16[64,720]{1,0:T(8,128)(2,1)S(1)}, bf16[64,720]{1,0:T(8,128)(2,1)S(1)}, u32[]{:S(2)}, u32[]{:S(2)}) %collective-permute-start.16) | collective-permute-done | bytes 92192 | tf_op jit(solution)/shard_map/ppermute | solution.py:256
  53.1 2.1 %collective-permute-done.17.refs_1_ = bf16[64,720]{1,0:T(8,128)(2,1)S(1)} collective-permute-done((bf16[64,720]{1,0:T(8,128)(2,1)S(1)}, bf16[64,720]{1,0:T(8,128)(2,1)S(1)}, u32[]{:S(2)}, u32[]{:S(2)}) %collective-permute-start.17) | collective-permute-done | bytes 92192 | tf_op jit(solution)/shard_map/ppermute | solution.py:297
  55.2 0.0 collective-permute-done.18
  55.3 0.8 %copy.26 = bf16[128,720]{0,1:T(8,128)(2,1)} copy(bf16[128,720]{1,0:T(8,128)(2,1)S(1)} %maximum_select_fusion) | data formatting | bytes 368640 | tf_op jit(solution)/shard_map/jit(_where)/select_n | solution.py:303
  (12 shorter events, 0.1 us)
Async XLA Ops:
  1.9 11.7 %collective-permute-start = (bf16[64,1456]{1,0:T(8,128)(2,1)S(1)}, bf16[64,1456]{1,0:T(8,128)(2,1)S(1)}, u32[]{:S(2)}, u32[]{:S(2)}) collective-permute-start(bf16[64,1456]{1,0:T(8,128)(2,1)S(1)} %shard_map.64.after_ref.refs_2_), channel_id=1, source_target_pairs={{0,12},{4,8},{8,4},{12,0},{1,13},{5,9},{9,5},{13,1},{2,14},{6,10},... | collective-permute-start | bytes 559112 | tf_op jit(solution)/shard_map/ppermute | solution.py:256
  7.0 9.2 %collective-permute-start.1 = (bf16[64,1456]{1,0:T(8,128)(2,1)S(1)}, bf16[64,1456]{1,0:T(8,128)(2,1)S(1)}, u32[]{:S(2)}, u32[]{:S(2)}) collective-permute-start(bf16[64,1456]{1,0:T(8,128)(2,1)S(1)} %shard_map.64.after_ref.refs_2_), channel_id=1, source_target_pairs={{0,4},{4,0},{8,12},{12,8},{1,5},{5,1},{9,13},{13,9},{2,6},{6,2},{1... | collective-permute-start | bytes 559112 | tf_op jit(solution)/shard_map/ppermute | solution.py:256
  7.0 9.2 %collective-permute-start.2 = (bf16[64,1456]{1,0:T(8,128)(2,1)S(1)}, bf16[64,1456]{1,0:T(8,128)(2,1)S(1)}, u32[]{:S(2)}, u32[]{:S(2)}) collective-permute-start(bf16[64,1456]{1,0:T(8,128)(2,1)S(1)} %shard_map.64.after_ref.refs_2_), channel_id=1, source_target_pairs={{0,2},{2,0},{1,3},{3,1},{4,6},{6,4},{5,7},{7,5},{8,10},{10,8},{9,1... | collective-permute-start | bytes 559112 | tf_op jit(solution)/shard_map/ppermute | solution.py:263
  8.5 11.1 %collective-permute-start.4 = (bf16[1440,720]{1,0:T(8,128)(2,1)}, bf16[1440,720]{1,0:T(8,128)(2,1)S(1)}, u32[]{:S(2)}, u32[]{:S(2)}) collective-permute-start(bf16[1440,720]{1,0:T(8,128)(2,1)} %bitcast.10), channel_id=1, source_target_pairs={{0,1},{1,0},{2,3},{3,2},{4,5},{5,4},{6,7},{7,6},{8,9},{9,8},{10,11... | collective-permute-start | bytes 6220808 | tf_op jit(solution)/shard_map/ppermute | solution.py:263
  8.5 11.1 %collective-permute-start.5 = (bf16[1440,720]{1,0:T(8,128)(2,1)}, bf16[1440,720]{1,0:T(8,128)(2,1)S(1)}, u32[]{:S(2)}, u32[]{:S(2)}) collective-permute-start(bf16[1440,720]{1,0:T(8,128)(2,1)} %bitcast.12), channel_id=1, source_target_pairs={{0,1},{1,0},{2,3},{3,2},{4,5},{5,4},{6,7},{7,6},{8,9},{9,8},{10,11... | collective-permute-start | bytes 6220808 | tf_op jit(solution)/shard_map/ppermute | solution.py:263
  16.2 7.3 %collective-permute-start.6 = (bf16[720,1440]{1,0:T(8,128)(2,1)S(1)}, bf16[720,1440]{1,0:T(8,128)(2,1)S(1)}, u32[]{:S(2)}, u32[]{:S(2)}) collective-permute-start(bf16[720,1440]{1,0:T(8,128)(2,1)S(1)} %get-tuple-element.43.refs_4_.refs_6_), channel_id=1, source_target_pairs={{0,1},{1,0},{2,3},{3,2},{4,5},{5,4},{6,7},{7,6},{8,9},{9,8},{10,11... | collective-permute-start | bytes 6220808 | tf_op jit(solution)/shard_map/ppermute | solution.py:263
  16.2 7.3 %collective-permute-start.3 = (bf16[64,1456]{1,0:T(8,128)(2,1)S(1)}, bf16[64,1456]{1,0:T(8,128)(2,1)S(1)}, u32[]{:S(2)}, u32[]{:S(2)}) collective-permute-start(bf16[64,1456]{1,0:T(8,128)(2,1)S(1)} %get-tuple-element.40.refs_0_), channel_id=1, source_target_pairs={{0,2},{2,0},{1,3},{3,1},{4,6},{6,4},{5,7},{7,5},{8,10},{10,8},{9,1... | collective-permute-start | bytes 559112 | tf_op jit(solution)/shard_map/ppermute | solution.py:263
  17.8 11.8 %collective-permute-start.10 = (bf16[64,1456]{1,0:T(8,128)(2,1)S(1)}, bf16[64,1456]{1,0:T(8,128)(2,1)S(1)}, u32[]{:S(2)}, u32[]{:S(2)}) collective-permute-start(bf16[64,1456]{1,0:T(8,128)(2,1)S(1)} %get-tuple-element.40.refs_0_), channel_id=1, source_target_pairs={{0,4},{4,0},{8,12},{12,8},{1,5},{5,1},{9,13},{13,9},{2,6},{6,2},{1... | collective-permute-start | bytes 559112 | tf_op jit(solution)/shard_map/ppermute | solution.py:256
  19.5 10.0 %collective-permute-start.11 = (bf16[64,1456]{1,0:T(8,128)(2,1)S(1)}, bf16[64,1456]{1,0:T(8,128)(2,1)S(1)}, u32[]{:S(2)}, u32[]{:S(2)}) collective-permute-start(bf16[64,1456]{1,0:T(8,128)(2,1)S(1)} %get-tuple-element.55), channel_id=1, source_target_pairs={{0,6},{2,4},{4,2},{6,0},{8,14},{10,12},{12,10},{14,8},{1,7},{3,5},... | collective-permute-start | bytes 559112 | tf_op jit(solution)/shard_map/ppermute | solution.py:260
  26.3 8.8 %collective-permute-start.8 = (bf16[64,1456]{1,0:T(8,128)(2,1)S(1)}, bf16[64,1456]{1,0:T(8,128)(2,1)S(1)}, u32[]{:S(2)}, u32[]{:S(2)}) collective-permute-start(bf16[64,1456]{1,0:T(8,128)(2,1)S(1)} %get-tuple-element.49.refs_1_), channel_id=1, source_target_pairs={{0,4},{4,0},{8,12},{12,8},{1,5},{5,1},{9,13},{13,9},{2,6},{6,2},{1... | collective-permute-start | bytes 559112 | tf_op jit(solution)/shard_map/ppermute | solution.py:256
  28.1 7.1 %collective-permute-start.7 = (bf16[64,1440]{1,0:T(8,128)(2,1)S(1)}, bf16[64,1440]{1,0:T(8,128)(2,1)S(1)}, u32[]{:S(2)}, u32[]{:S(2)}) collective-permute-start(bf16[64,1440]{1,0:T(8,128)(2,1)S(1)} %get-tuple-element.48), channel_id=1, source_target_pairs={{0,2},{2,0},{1,3},{3,1},{4,6},{6,4},{5,7},{7,5},{8,10},{10,8},{9,1... | collective-permute-start | bytes 552968 | tf_op jit(solution)/shard_map/ppermute | solution.py:263
  32.4 8.2 %collective-permute-start.12 = (bf16[64,1440]{1,0:T(8,128)(2,1)S(1)}, bf16[64,1440]{1,0:T(8,128)(2,1)S(1)}, u32[]{:S(2)}, u32[]{:S(2)}) collective-permute-start(bf16[64,1440]{1,0:T(8,128)(2,1)S(1)} %convert_element_type.31), channel_id=1, source_target_pairs={{0,4},{4,0},{8,12},{12,8},{1,5},{5,1},{9,13},{13,9},{2,6},{6,2},{1... | collective-permute-start | bytes 552968 | tf_op jit(solution)/shard_map/ppermute | solution.py:256
  33.6 9.7 %collective-permute-start.13 = (bf16[64,1440]{1,0:T(8,128)(2,1)S(1)}, bf16[64,1440]{1,0:T(8,128)(2,1)S(1)}, u32[]{:S(2)}, u32[]{:S(2)}) collective-permute-start(bf16[64,1440]{1,0:T(8,128)(2,1)S(1)} %get-tuple-element.62), channel_id=1, source_target_pairs={{0,6},{2,4},{4,2},{6,0},{8,14},{10,12},{12,10},{14,8},{1,7},{3,5},... | collective-permute-start | bytes 552968 | tf_op jit(solution)/shard_map/ppermute | solution.py:260
  39.8 7.8 %collective-permute-start.15 = (bf16[64,1440]{1,0:T(8,128)(2,1)S(1)}, bf16[64,1440]{1,0:T(8,128)(2,1)S(1)}, u32[]{:S(2)}, u32[]{:S(2)}) collective-permute-start(bf16[64,1440]{1,0:T(8,128)(2,1)S(1)} %get-tuple-element.65), channel_id=1, source_target_pairs={{0,2},{2,0},{1,3},{3,1},{4,6},{6,4},{5,7},{7,5},{8,10},{10,8},{9,1... | collective-permute-start | bytes 552968 | tf_op jit(solution)/shard_map/ppermute | solution.py:263
  43.4 7.7 %collective-permute-start.14 = (bf16[64,1440]{1,0:T(8,128)(2,1)S(1)}, bf16[64,1440]{1,0:T(8,128)(2,1)S(1)}, u32[]{:S(2)}, u32[]{:S(2)}) collective-permute-start(bf16[64,1440]{1,0:T(8,128)(2,1)S(1)} %add_convert_fusion), channel_id=1, source_target_pairs={{0,12},{4,8},{8,4},{12,0},{1,13},{5,9},{9,5},{13,1},{2,14},{6,10},... | collective-permute-start | bytes 552968 | tf_op jit(solution)/shard_map/ppermute | solution.py:256
  45.1 6.4 %collective-permute-start.9 = (bf16[64,1440]{1,0:T(8,128)(2,1)S(1)}, bf16[64,1440]{1,0:T(8,128)(2,1)S(1)}, u32[]{:S(2)}, u32[]{:S(2)}) collective-permute-start(bf16[64,1440]{1,0:T(8,128)(2,1)S(1)} %get-tuple-element.54), channel_id=1, source_target_pairs={{0,2},{2,0},{1,3},{3,1},{4,6},{6,4},{5,7},{7,5},{8,10},{10,8},{9,1... | collective-permute-start | bytes 552968 | tf_op jit(solution)/shard_map/ppermute | solution.py:263
  48.4 4.8 %collective-permute-start.16 = (bf16[64,720]{1,0:T(8,128)(2,1)S(1)}, bf16[64,720]{1,0:T(8,128)(2,1)S(1)}, u32[]{:S(2)}, u32[]{:S(2)}) collective-permute-start(bf16[64,720]{1,0:T(8,128)(2,1)S(1)} %get-tuple-element.66), channel_id=1, source_target_pairs={{0,4},{4,0},{8,12},{12,8},{1,5},{5,1},{9,13},{13,9},{2,6},{6,2},{1... | collective-permute-start | bytes 276488 | tf_op jit(solution)/shard_map/ppermute | solution.py:256
  50.1 5.1 %collective-permute-start.17 = (bf16[64,720]{1,0:T(8,128)(2,1)S(1)}, bf16[64,720]{1,0:T(8,128)(2,1)S(1)}, u32[]{:S(2)}, u32[]{:S(2)}) collective-permute-start(bf16[64,720]{1,0:T(8,128)(2,1)S(1)} %get-tuple-element.67), channel_id=1, source_target_pairs={{0,5},{1,4},{4,1},{5,0},{8,13},{9,12},{12,9},{13,8},{2,7},{3,6},{6... | collective-permute-start | bytes 276488 | tf_op jit(solution)/shard_map/ppermute | solution.py:297
  52.3 2.9 %collective-permute-start.18 = (bf16[64,720]{1,0:T(8,128)(2,1)S(1)}, bf16[64,720]{1,0:T(8,128)(2,1)S(1)}, u32[]{:S(2)}, u32[]{:S(2)}) collective-permute-start(bf16[64,720]{1,0:T(8,128)(2,1)S(1)} %get-tuple-element.69), channel_id=1, source_target_pairs={{0,1},{1,0},{2,3},{3,2},{4,5},{5,4},{6,7},{7,6},{8,9},{9,8},{10,11... | collective-permute-start | bytes 276488 | tf_op jit(solution)/shard_map/ppermute | solution.py:263
